TPU v7x, 32 devices: a whole 2x2x4 slice. The times are simulated.
32 devices in a mesh: query: 16 (over z, y, x), entity: 2 (over core).
Axes of the slice: x: 2, y: 2, z: 4, core: 2. Of those that a mesh axis runs over, the one named last changes fastest.
Arguments:
- anchor_ids: int32 [8192], P('query'), may hold values from 0 to 4095
- relation_ids: int32 [8192], P('query'), may hold values from 0 to 4130
- side_flags: int32 [8192], P('query'), may hold values from 0 to 1
- teacher_entities: bfloat16 [4096, 1000], P(('entity', 'query')), may hold values from -1.2 to 1.2, as said below
- student_entities: bfloat16 [4096, 128], P(('entity', 'query')), may hold values from -2.1 to 2.1, as said below
- teacher_relations: bfloat16 [4131, 1000], replicated, may hold values from -9 to 33, as said below
- student_relations: bfloat16 [4131, 128], replicated, may hold values from -9 to 63.6875, as said below
Outputs:
- divergence: float32 [8192], P('query')
- entity_grad: float32 [4096, 128], P(('entity', 'query'))
- query_grad: float32 [8192, 128], P('query')
Inputs may be any that keep to these rules, and one draw needn't show every extreme that they name: `teacher_entities`: Real-valued embeddings. `student_entities`: Real-valued embeddings. `teacher_relations`: Real-valued embeddings. `student_relations`: Real-valued embeddings.
All inputs are finite; a program needn't handle non-finite values.
Results may differ from a plain program's by a relative error of at most 0.013.
Values may be sent and summed in bfloat16 or wider, within the bound.
No kernel may reach another device: no remote copies, remote signals or barrier semaphores. Data moves between devices by JAX's collectives and lax.ppermute only.
A program may use at most 128 MiB of HBM per device.

v0:
```python
import functools

import jax
import jax.numpy as jnp
import numpy as np
from jax import lax
from jax.experimental import pallas as pl
from jax.experimental.pallas import tpu as pltpu
from jax.sharding import PartitionSpec as P

F32 = jnp.float32
BF16 = jnp.bfloat16
VMEM = pl.BlockSpec(memory_space=pltpu.VMEM)
SMEM = pl.BlockSpec(memory_space=pltpu.SMEM)
ANY = pl.BlockSpec(memory_space=pl.ANY)
MIB = 1 << 20


def places(n):
    sides = 2 if n % 2 == 0 else 1
    m = n // sides
    order = list(range(m))
    if m % 2 == 0:
        order = [2 * z for z in range(m // 2)] + [2 * z + 1 for z in reversed(range(m // 2))]
    return [[order[p] * sides + x for x in range(sides)] for p in range(m)]


def spread_steps(m, across):
    held = [(0, 0)]
    steps = []
    while len(held) < m * (2 if across else 1):
        taken = []
        for shift in (1, -1, 0):
            if shift == 0 and not across:
                continue
            if shift:
                found = [((k, o), (k, (o + shift) % m)) for k, o in held]
            else:
                found = [((k, o), (1 - k, o)) for k, o in held]
            names = [t[2] for t in taken]
            found = [f for f in found if f[1] not in held and f[1] not in names]
            if found:
                best = min(found, key=lambda f: (f[1][0], -min(f[1][1], m - f[1][1]), f[1][1]))
                taken.append((shift,) + best)
        held += [t[2] for t in taken]
        steps.append(taken)
    return steps, held


def move(x, place, shift):
    m = len(place)
    pairs = []
    for p in range(m):
        for side in range(len(place[0])):
            source = place[(p + shift) % m][side] if shift else place[p][1 - side]
            pairs.append((source, place[p][side]))
    return lax.ppermute(x, "query", sorted(pairs))


def owners(place, held, n):
    owner = np.zeros((n, n), np.int32)
    for p in range(len(place)):
        for side in range(len(place[0])):
            for slot, (k, o) in enumerate(held):
                owner[place[p][side], slot] = place[(p + o) % len(place)][side ^ k]
    return owner


def partner(x, size, far):
    return lax.ppermute(x, "entity", [(i, i ^ far) for i in range(size)])


class Shape:
    def __init__(self, tw, sw):
        self.tw, self.sw = tw, sw
        self.half = tw // 2
        self.wide = -(-self.half // 128) * 128
        self.re, self.im = sw, sw + self.wide
        self.total = sw + 2 * self.wide


def put_row(out, student, teacher, shape):
    out[:, : shape.sw] = student.astype(BF16)
    pad = jnp.zeros((teacher.shape[0], shape.wide - shape.half), F32)
    for start, at in ((0, shape.re), (shape.half, shape.im)):
        piece = teacher[:, start : start + shape.half]
        out[:, at : at + shape.wide] = jnp.concatenate([piece, pad], axis=1).astype(BF16)


def pack_kernel(shape, teacher_t, student, out):
    put_row(out, student[...].astype(F32), teacher_t[...].astype(F32).T, shape)


def pack(teacher, student, shape):
    return pl.pallas_call(
        functools.partial(pack_kernel, shape),
        out_shape=jax.ShapeDtypeStruct((teacher.shape[0], shape.total), BF16),
        in_specs=[VMEM, VMEM],
        out_specs=VMEM,
        compiler_params=pltpu.CompilerParams(vmem_limit_bytes=8 * MIB),
        name="pack_rows",
    )(teacher.T, student)


def relation_kernel(shape, rel, block, base, cols, table_t, student, out, acc, acc_s):
    step = pl.program_id(0)
    start = (base[0] + step) * block
    ids = cols[:, 1:2] - start
    hot = (ids == lax.broadcasted_iota(jnp.int32, (cols.shape[0], block), 1)).astype(F32).astype(BF16)
    lanes = lax.broadcasted_iota(jnp.int32, table_t.shape, 1)
    rows = lax.broadcasted_iota(jnp.int32, student.shape, 0)
    table = jnp.where(lanes < rel - start, table_t[...], jnp.zeros_like(table_t))
    small = jnp.where(rows < rel - start, student[...], jnp.zeros_like(student))
    part = lax.dot_general(hot, table, (((1,), (1,)), ((), ())), preferred_element_type=F32)
    part_s = jnp.dot(hot, small, preferred_element_type=F32)

    @pl.when(step == 0)
    def _():
        acc[...] = part
        acc_s[...] = part_s

    @pl.when(step > 0)
    def _():
        acc[...] += part
        acc_s[...] += part_s

    @pl.when(step == pl.num_programs(0) - 1)
    def _():
        put_row(out, acc_s[...], acc[...], shape)


def relation_rows(base, cols, table, student, count, block, shape):
    rel, tw = table.shape
    q = cols.shape[0]
    final = -(-rel // block) - 1
    whole = lambda i, base: (0, 0)
    return pl.pallas_call(
        functools.partial(relation_kernel, shape, rel, block),
        out_shape=jax.ShapeDtypeStruct((q, shape.total), BF16),
        grid_spec=pltpu.PrefetchScalarGridSpec(
            num_scalar_prefetch=1,
            grid=(count,),
            in_specs=[
                pl.BlockSpec((q, cols.shape[1]), whole),
                pl.BlockSpec((tw, block), lambda i, base: (0, jnp.minimum(base[0] + i, final))),
                pl.BlockSpec((block, shape.sw), lambda i, base: (jnp.minimum(base[0] + i, final), 0)),
            ],
            out_specs=pl.BlockSpec((q, shape.total), whole),
            scratch_shapes=[pltpu.VMEM((q, tw), F32), pltpu.VMEM((q, shape.sw), F32)],
        ),
        compiler_params=pltpu.CompilerParams(vmem_limit_bytes=56 * MIB),
        cost_estimate=pl.CostEstimate(
            flops=2 * q * tw * block * count, bytes_accessed=2 * tw * block * count, transcendentals=0
        ),
        name="relation_rows",
    )(base, cols, table.T, student)


def load_shards(shards, table, sems, own):
    copies = [
        pltpu.make_async_copy(shard, table.at[pl.ds(j * own, own)], sems.at[j]) for j, shard in enumerate(shards)
    ]
    for copy in copies:
        copy.start()
    return copies


def anchor_kernel(count, own, has_acc, bases, cols, *rest):
    acc_in, rest = (rest[0], rest[1:]) if has_acc else (None, rest)
    shards, (out, table, hot, sems) = rest[:count], rest[count:]
    copies = load_shards(shards, table, sems, own)
    q = cols.shape[0]
    ids = cols[:, 0:1]
    lane = lax.broadcasted_iota(jnp.int32, (q, own), 1)
    for j in range(count):
        hot[:, j * own : (j + 1) * own] = (ids - bases[j] == lane).astype(F32).astype(BF16)
    for copy in copies:
        copy.wait()
    found = jnp.dot(hot[...], table[...], preferred_element_type=F32).astype(BF16)
    out[...] = found + acc_in[...] if has_acc else found


def anchor_rows(bases, ids, shards, acc, shape):
    own = shards[0].shape[0]
    q, count = ids.shape[0], len(shards)
    operands = [bases, ids] + ([] if acc is None else [acc]) + list(shards)
    return pl.pallas_call(
        functools.partial(anchor_kernel, count, own, acc is not None),
        out_shape=jax.ShapeDtypeStruct((q, shape.total), BF16),
        in_specs=[SMEM, VMEM] + ([] if acc is None else [VMEM]) + [ANY] * count,
        out_specs=VMEM,
        scratch_shapes=[
            pltpu.VMEM((count * own, shape.total), BF16),
            pltpu.VMEM((q, count * own), BF16),
            pltpu.SemaphoreType.DMA((count,)),
        ],
        compiler_params=pltpu.CompilerParams(vmem_limit_bytes=2 * count * own * (shape.total + q) + 12 * MIB),
        cost_estimate=pl.CostEstimate(
            flops=2 * q * count * own * shape.total,
            bytes_accessed=2 * (count * own + 2 * q) * shape.total,
            transcendentals=0,
        ),
        name="anchor_rows",
    )(*operands)


def score_kernel(shape, own, n, chunk, mine, other, relation, relation_b, cols, *rest):
    shards, (t_out, s_out, stats, q_student, table, q_teacher, sems) = rest[:n], rest[n:]
    copies = load_shards(shards, table, sems, own)
    q = mine.shape[0]
    sw, wide = shape.sw, shape.wide
    rows = 128

    def build(i, _):
        at = pl.ds(pl.multiple_of(i * rows, rows), rows)
        g = (2 * cols[at, 2:3] - 1).astype(F32)
        a = mine[at, :].astype(F32) + other[at, :].astype(F32)
        r = relation[at, :].astype(F32) + relation_b[at, :].astype(F32)
        a_re, a_im = a[:, shape.re : shape.re + wide], a[:, shape.im : shape.im + wide]
        r_re, r_im = r[:, shape.re : shape.re + wide], r[:, shape.im : shape.im + wide]
        q_teacher[at, :wide] = (a_re * r_re - g * a_im * r_im).astype(BF16)
        q_teacher[at, wide:] = (a_im * r_re + g * a_re * r_im).astype(BF16)
        a_s, r_s = a[:, :sw], r[:, :sw]
        a_x, r_x = pltpu.roll(a_s, sw // 2, 1), pltpu.roll(r_s, sw // 2, 1)
        low = lax.broadcasted_iota(jnp.int32, (rows, sw), 1) < sw // 2
        re2, im2 = jnp.where(low, r_s, r_x), jnp.where(low, r_x, r_s)
        q_student[at, :] = (a_s * re2 + jnp.where(low, -g, g) * a_x * im2).astype(BF16)
        return 0

    lax.fori_loop(0, q // rows, build, 0)
    for copy in copies:
        copy.wait()

    dims = (((1,), (1,)), ((), ()))

    def score(c, carry):
        top_t, total_t, weighted, top_s, total_s = carry
        at = pl.ds(pl.multiple_of(c * chunk, chunk), chunk)
        t = lax.dot_general(table[at, sw:], q_teacher[...], dims, preferred_element_type=F32)
        s = lax.dot_general(table[at, :sw], q_student[...], dims, preferred_element_type=F32)
        t_out[at, :] = t
        s_out[at, :] = s
        new_t = jnp.maximum(top_t, jnp.max(t, axis=0, keepdims=True))
        new_s = jnp.maximum(top_s, jnp.max(s, axis=0, keepdims=True))
        scale_t, scale_s = jnp.exp(top_t - new_t), jnp.exp(top_s - new_s)
        e = jnp.exp(t - new_t)
        total_t = total_t * scale_t + jnp.sum(e, axis=0, keepdims=True)
        weighted = weighted * scale_t + jnp.sum(e * (t - s), axis=0, keepdims=True)
        total_s = total_s * scale_s + jnp.sum(jnp.exp(s - new_s), axis=0, keepdims=True)
        return new_t, total_t, weighted, new_s, total_s

    lowest = jnp.full((1, q), -jnp.inf, F32)
    nothing = jnp.zeros((1, q), F32)
    found = lax.fori_loop(0, n * own // chunk, score, (lowest, nothing, nothing, lowest, nothing), unroll=True)
    stats[...] = jnp.concatenate(list(found) + [nothing] * 3, axis=0)


def scores(mine, other, relation, relation_b, cols, shards, shape):
    n, own = len(shards), shards[0].shape[0]
    q = mine.shape[0]
    slab = n * own
    chunk = 512 if slab % 512 == 0 else own
    return pl.pallas_call(
        functools.partial(score_kernel, shape, own, n, chunk),
        out_shape=(
            jax.ShapeDtypeStruct((slab, q), F32),
            jax.ShapeDtypeStruct((slab, q), F32),
            jax.ShapeDtypeStruct((8, q), F32),
            jax.ShapeDtypeStruct((q, shape.sw), BF16),
        ),
        in_specs=[VMEM] * 5 + [ANY] * n,
        out_specs=(VMEM,) * 4,
        scratch_shapes=[
            pltpu.VMEM((slab, shape.total), BF16),
            pltpu.VMEM((q, 2 * shape.wide), BF16),
            pltpu.SemaphoreType.DMA((n,)),
        ],
        compiler_params=pltpu.CompilerParams(vmem_limit_bytes=8 * slab * q + 2 * slab * shape.total + 10 * MIB),
        cost_estimate=pl.CostEstimate(
            flops=2 * q * slab * shape.total, bytes_accessed=2 * slab * shape.total + 8 * slab * q, transcendentals=2 * slab * q
        ),
        name="scores",
    )(mine, other, relation, relation_b, cols, *shards)


def combine(a, b):
    top_t, top_s = jnp.maximum(a[0:1], b[0:1]), jnp.maximum(a[3:4], b[3:4])
    at, bt = jnp.exp(a[0:1] - top_t), jnp.exp(b[0:1] - top_t)
    as_, bs = jnp.exp(a[3:4] - top_s), jnp.exp(b[3:4] - top_s)
    total_t = a[1:2] * at + b[1:2] * bt
    weighted = a[2:3] * at + b[2:3] * bt
    total_s = a[4:5] * as_ + b[4:5] * bs
    return top_t, total_t, weighted, top_s, total_s


def grad_kernel(n, own, chunk, sw, order, t_in, s_in, mine, other, q_student, *rest):
    shards, (divergence, q_grad), outs = rest[:n], rest[n : n + 2], rest[n + 2 : -3]
    table, e_grad, sems = rest[-3:]
    copies = [
        pltpu.make_async_copy(shard.at[:, pl.ds(0, sw)], table.at[pl.ds(j * own, own)], sems.at[j])
        for j, shard in enumerate(shards)
    ]
    for copy in copies:
        copy.start()
    top_t, total_t, weighted, top_s, total_s = combine(mine[...], other[...])
    divergence[...] = weighted / total_t - top_t - jnp.log(total_t) + top_s + jnp.log(total_s)
    over_t, over_s = 1.0 / total_t, 1.0 / total_s
    for copy in copies:
        copy.wait()
    per = chunk // own

    def step(c, total):
        at = pl.ds(pl.multiple_of(c * chunk, chunk), chunk)
        prob_t = jnp.exp(t_in[at, :] - top_t) * over_t
        prob_s = jnp.exp(s_in[at, :] - top_s) * over_s
        weights = (prob_s - prob_t).astype(BF16)
        grad = jnp.dot(weights, q_student[...], preferred_element_type=F32).astype(BF16)
        for k in range(per):
            e_grad[order[c * per + k]] = grad[k * own : (k + 1) * own, :]
        return total + lax.dot_general(
            table[at, :], weights, (((0,), (0,)), ((), ())), preferred_element_type=F32
        )

    q = q_student.shape[0]
    total = lax.fori_loop(0, n * own // chunk, step, jnp.zeros((sw, q), F32), unroll=True)
    q_grad[...] = total.T
    count = n // len(outs)
    for d, out in enumerate(outs):
        out[...] = e_grad[d * count : (d + 1) * count]


def gradients(order, near, t, s, mine, other, q_student, shards):
    n, own = len(shards), shards[0].shape[0]
    q, sw = q_student.shape
    slab = n * own
    chunk = 512 if slab % 512 == 0 else own
    return pl.pallas_call(
        functools.partial(grad_kernel, n, own, chunk, sw),
        out_shape=(
            jax.ShapeDtypeStruct((1, q), F32),
            jax.ShapeDtypeStruct((q, sw), F32),
        )
        + (jax.ShapeDtypeStruct((n // near, own, sw), BF16),) * near,
        in_specs=[SMEM] + [VMEM] * 5 + [ANY] * n,
        out_specs=(VMEM,) * (2 + near),
        scratch_shapes=[
            pltpu.VMEM((slab, sw), BF16),
            pltpu.VMEM((n, own, sw), BF16),
            pltpu.SemaphoreType.DMA((n,)),
        ],
        compiler_params=pltpu.CompilerParams(vmem_limit_bytes=8 * slab * q + 10 * MIB),
        cost_estimate=pl.CostEstimate(
            flops=4 * q * slab * sw, bytes_accessed=8 * slab * q, transcendentals=2 * slab * q
        ),
        name="gradients",
    )(order, t, s, mine, other, q_student, *shards)


def add_kernel(count, *refs):
    terms, outs = refs[:count], refs[count:]
    for e, out in enumerate(outs):
        total = terms[0][e].astype(F32)
        for term in terms[1:]:
            total += term[e].astype(F32)
        out[...] = total.astype(out.dtype)


def add_blocks(terms):
    far, own, sw = terms[0].shape
    return pl.pallas_call(
        functools.partial(add_kernel, len(terms)),
        out_shape=(jax.ShapeDtypeStruct((own, sw), F32),)
        + (jax.ShapeDtypeStruct((own, sw), BF16),) * (far - 1),
        in_specs=[VMEM] * len(terms),
        out_specs=(VMEM,) * far,
        compiler_params=pltpu.CompilerParams(vmem_limit_bytes=8 * MIB),
        name="add_blocks",
    )(*terms)


def reduce_blocks(blocks, beside, n):
    near, far = len(blocks), n // len(blocks)
    terms = [blocks[0]]
    for d in range(1, near):
        terms.append(lax.ppermute(blocks[d], "query", [(i, i ^ d) for i in range(n)]))
    terms[-1], beside = lax.optimization_barrier((terms[-1], beside))
    sums = add_blocks(terms)
    total = sums[0]
    for e in range(1, far):
        pairs = [(h * near + r, (h ^ e if far & (far - 1) == 0 else (h + e) % far) * near + r) for h in range(far) for r in range(near)]
        total = total + lax.ppermute(sums[e], "query", pairs).astype(F32)
    return total, beside


def make(n, groups):
    place = places(n)
    steps, held = spread_steps(len(place), len(place[0]) == 2)
    table = owners(place, held, n)
    near = next(k for k in (4, 2, 1) if n % k == 0)
    me = np.arange(n)[:, None]
    far_move = (table // near) ^ (me // near) if n // near & (n // near - 1) == 0 else (table // near - me // near) % (n // near)
    position = ((table % near) ^ (me % near)) * (n // near) + far_move

    def per_device(
        anchor_ids,
        relation_ids,
        side_flags,
        teacher_entities,
        student_entities,
        teacher_relations,
        student_relations,
    ):
        own, tw = teacher_entities.shape
        shape = Shape(tw, student_entities.shape[1])
        owner, order = jnp.asarray(np.stack([table, position], axis=1))[lax.axis_index("query")]
        bases = (owner + lax.axis_index("entity") * n) * own
        cols = jnp.stack([anchor_ids, relation_ids, side_flags], axis=1)

        have = {(0, 0): pack(teacher_entities, student_entities, shape)}
        block = 768
        per_core = -(-teacher_relations.shape[0] // (2 * block))
        base = (lax.axis_index("entity") % 2 * per_core).astype(jnp.int32)[None]
        own_key = (0, 0)
        have[own_key], base = lax.optimization_barrier((have[own_key], base))
        anchors, counted = None, 0
        for number, step in enumerate(steps):
            got = {new: move(have[old], place, shift) for shift, old, new in step}
            beside = None
            if number == 0:
                relation = relation_rows(base, cols, teacher_relations, student_relations, per_core, block, shape)
                beside = relation
            elif number >= len(steps) // 2:
                names = held[counted : len(have)]
                anchors = anchor_rows(bases[counted:], cols, [have[h] for h in names], anchors, shape)
                counted = len(have)
                beside = anchors
            sent = [old for _, old, _ in steps[number + 1] if old in got] if number + 1 < len(steps) else []
            if sent and beside is not None:
                gate = sent[len(sent) // 2]
                got[gate], beside = lax.optimization_barrier((got[gate], beside))
                if number == 0:
                    relation = beside
                else:
                    anchors = beside
            if number == 0:
                relation_b = partner(relation, groups, 1)
            have.update(got)
        shards = [have[h] for h in held]
        mine = anchor_rows(bases[counted:], cols, shards[counted:], anchors, shape)
        far = 1
        while far < groups // 2:
            mine = mine + partner(mine, groups, far)
            far *= 2
        other = partner(mine, groups, far)
        t, s, stats, q_student = scores(mine, other, relation, relation_b, cols, shards, shape)
        far = 1
        while far < groups // 2:
            found = combine(stats, partner(stats, groups, far))
            stats = jnp.concatenate(list(found) + [jnp.zeros_like(found[0])] * 3, axis=0)
            far *= 2
        divergence, q_grad, *blocks = gradients(
            order, near, t, s, stats, partner(stats, groups, far), q_student, shards
        )
        far = 1
        while far < groups:
            q_grad = q_grad + partner(q_grad, groups, far)
            far *= 2
        entity_grad, q_grad = reduce_blocks(blocks, q_grad, n)
        return (divergence[0], entity_grad, q_grad)

    return per_device


def solution(mesh):
    in_specs = (
        P("query"),
        P("query"),
        P("query"),
        P(("entity", "query"), None),
        P(("entity", "query"), None),
        P(),
        P(),
    )
    out_specs = (P("query"), P(("entity", "query"), None), P("query", None))
    return jax.shard_map(
        make(mesh.shape["query"], mesh.shape["entity"]),
        mesh=mesh, in_specs=in_specs, out_specs=out_specs, check_vma=False,
    )
```

profile of v0, /device:TPU:0, one launch (start us, length us, event | category | flops | bytes accessed | tf_op | source)
XLA Modules:
  0.0 88.7 jit_solution(13588785889978364659)
XLA Ops:
  0.7 0.9 %copy-done.2 = bf16[128,1000]{0,1:T(8,128)(2,1)S(1)} copy-done((bf16[128,1000]{0,1:T(8,128)(2,1)S(1)}, bf16[128,1000]{0,1:T(8,128)(2,1)}, u32[]{:S(2)}) %copy-start.2) | copy-done | bytes 256024
  2.6 3.0 %collective-permute-start.2 = (bf16[128,1152]{1,0:T(8,128)(2,1)S(1)}, bf16[128,1152]{1,0:T(8,128)(2,1)S(1)}, u32[]{:S(2)}, u32[]{:S(2)}) collective-permute-start(bf16[128,1152]{1,0:T(8,128)(2,1)S(1)} %pack_rows.1.rest_0_), channel_id=1, source_target_pairs={{0,4},{2,6},{4,12},{6,14},{8,0},{10,2},{12,20},{14,22},{16,8},{18,... | collective-permute-start | bytes 884744 | tf_op jit(solution)/shard_map/ppermute | solution.py:57
  5.8 1.9 %collective-permute-start = (bf16[128,1152]{1,0:T(8,128)(2,1)S(1)}, bf16[128,1152]{1,0:T(8,128)(2,1)S(1)}, u32[]{:S(2)}, u32[]{:S(2)}) collective-permute-start(bf16[128,1152]{1,0:T(8,128)(2,1)S(1)} %pack_rows.1.rest_0_), channel_id=1, source_target_pairs={{0,2},{2,0},{4,6},{6,4},{8,10},{10,8},{12,14},{14,12},{16,18},{18,... | collective-permute-start | bytes 884744 | tf_op jit(solution)/shard_map/ppermute | solution.py:57
  9.2 3.5 %collective-permute-done.2.rest_1_ = bf16[128,1152]{1,0:T(8,128)(2,1)S(1)} collective-permute-done((bf16[128,1152]{1,0:T(8,128)(2,1)S(1)}, bf16[128,1152]{1,0:T(8,128)(2,1)S(1)}, u32[]{:S(2)}, u32[]{:S(2)}) %collective-permute-start.2) | collective-permute-done | bytes 294944 | tf_op jit(solution)/shard_map/ppermute | solution.py:57
  12.7 1.7 %collective-permute-start.3 = (bf16[128,1152]{1,0:T(8,128)(2,1)S(1)}, bf16[128,1152]{1,0:T(8,128)(2,1)S(1)}, u32[]{:S(2)}, u32[]{:S(2)}) collective-permute-start(bf16[128,1152]{1,0:T(8,128)(2,1)S(1)} %collective-permute-done.2.rest_1_), channel_id=1, source_target_pairs={{0,4},{2,6},{4,12},{6,14},{8,0},{10,2},{12,20},{14,22},{16,8},{18,... | collective-permute-start | bytes 884744 | tf_op jit(solution)/shard_map/ppermute | solution.py:57
  14.4 7.6 %relation_rows.1.relation = bf16[512,1152]{1,0:T(8,128)(2,1)} custom-call(s32[1]{0:T(128)} %bitcast.7.base, s32[512,3]{1,0:T(8,128)} %copy.18.cols, bf16[1000,4131]{1,0:T(8,128)(2,1)} %bitcast.18, bf16[4131,128]{1,0:T(8,128)(2,1)} %student.3), custom_call_target="tpu_custom_call" | custom-call | flops 2359296000 | bytes 4608000 | tf_op jit(solution)/shard_map/relation_rows/pallas_call | solution.py:137
  22.3 1.7 %collective-permute-start.7 = (bf16[128,1152]{1,0:T(8,128)(2,1)S(1)}, bf16[128,1152]{1,0:T(8,128)(2,1)S(1)}, u32[]{:S(2)}, u32[]{:S(2)}) collective-permute-start(bf16[128,1152]{1,0:T(8,128)(2,1)S(1)} %collective-permute-done.2.rest_1_), channel_id=1, source_target_pairs={{0,2},{2,0},{4,6},{6,4},{8,10},{10,8},{12,14},{14,12},{16,18},{18,... | collective-permute-start | bytes 884744 | tf_op jit(solution)/shard_map/ppermute | solution.py:57
  24.7 1.5 %collective-permute-start.4 = (bf16[128,1152]{1,0:T(8,128)(2,1)S(1)}, bf16[128,1152]{1,0:T(8,128)(2,1)S(1)}, u32[]{:S(2)}, u32[]{:S(2)}) collective-permute-start(bf16[128,1152]{1,0:T(8,128)(2,1)S(1)} %collective-permute-done.3.rest_4_), channel_id=1, source_target_pairs={{0,4},{2,6},{4,12},{6,14},{8,0},{10,2},{12,20},{14,22},{16,8},{18,... | collective-permute-start | bytes 884744 | tf_op jit(solution)/shard_map/ppermute | solution.py:57
  27.1 4.8 %collective-permute-done.6.rest_5_ = bf16[128,1152]{1,0:T(8,128)(2,1)S(1)} collective-permute-done((bf16[128,1152]{1,0:T(8,128)(2,1)S(1)}, bf16[128,1152]{1,0:T(8,128)(2,1)S(1)}, u32[]{:S(2)}, u32[]{:S(2)}) %collective-permute-start.6) | collective-permute-done | bytes 294944 | tf_op jit(solution)/shard_map/ppermute | solution.py:57
  32.3 3.1 %anchor_rows.4.rest_0_ = bf16[512,1152]{1,0:T(8,128)(2,1)S(1)} custom-call(s32[16]{0:T(128)S(1)} %bitcast.17, s32[512,3]{1,0:T(8,128)S(1)} %copy-done, bf16[128,1152]{1,0:T(8,128)(2,1)S(1)} %pack_rows.1.rest_0_, bf16[128,1152]{1,0:T(8,128)(2,1)S(1)} %collective-permute-done.2.rest_1_, bf16[128,1152]{1,0:T(8,128)(2,1)S(1)} %collective-permute-done.5.rest_2_, ...), custom_call_target="tpu_custom_call" | custom-call | flops 1056964608 | bytes 4423680 | tf_op jit(solution)/shard_map/anchor_rows/pallas_call | solution.py:187
  35.4 1.7 %collective-permute-start.11 = (bf16[128,1152]{1,0:T(8,128)(2,1)S(1)}, bf16[128,1152]{1,0:T(8,128)(2,1)S(1)}, u32[]{:S(2)}, u32[]{:S(2)}) collective-permute-start(bf16[128,1152]{1,0:T(8,128)(2,1)S(1)} %collective-permute-done.4.rest_1_.rest_7_), channel_id=1, source_target_pairs={{0,2},{2,0},{4,6},{6,4},{8,10},{10,8},{12,14},{14,12},{16,18},{18,... | collective-permute-start | bytes 884744 | tf_op jit(solution)/shard_map/ppermute | solution.py:57
  37.2 1.5 %collective-permute-start.10 = (bf16[128,1152]{1,0:T(8,128)(2,1)S(1)}, bf16[128,1152]{1,0:T(8,128)(2,1)S(1)}, u32[]{:S(2)}, u32[]{:S(2)}) collective-permute-start(bf16[128,1152]{1,0:T(8,128)(2,1)S(1)} %collective-permute-done.4.rest_1_.rest_7_), channel_id=1, source_target_pairs={{0,4},{2,6},{4,12},{6,14},{8,0},{10,2},{12,20},{14,22},{16,8},{18,... | collective-permute-start | bytes 884744 | tf_op jit(solution)/shard_map/ppermute | solution.py:57
  38.7 3.6 %collective-permute-done.8.rest_2_.rest_8_ = bf16[128,1152]{1,0:T(8,128)(2,1)S(1)} collective-permute-done((bf16[128,1152]{1,0:T(8,128)(2,1)S(1)}, bf16[128,1152]{1,0:T(8,128)(2,1)S(1)}, u32[]{:S(2)}, u32[]{:S(2)}) %collective-permute-start.8) | collective-permute-done | bytes 294944 | tf_op jit(solution)/shard_map/ppermute | solution.py:57
  42.3 1.8 %anchor_rows.5.rest_0_ = bf16[512,1152]{1,0:T(8,128)(2,1)S(1)} custom-call(s32[9]{0:T(128)S(1)} %slice_bitcast_fusion.bases, s32[512,3]{1,0:T(8,128)S(1)} %copy-done, bf16[512,1152]{1,0:T(8,128)(2,1)S(1)} %anchor_rows.4.rest_0_, bf16[128,1152]{1,0:T(8,128)(2,1)S(1)} %collective-permute-done.4.rest_1_.rest_7_, ...), custom_call_target="tpu_custom_call" | custom-call | flops 452984832 | bytes 3244032 | tf_op jit(solution)/shard_map/anchor_rows/pallas_call | solution.py:187
  44.9 1.3 %collective-permute-start.14 = (bf16[128,1152]{1,0:T(8,128)(2,1)S(1)}, bf16[128,1152]{1,0:T(8,128)(2,1)S(1)}, u32[]{:S(2)}, u32[]{:S(2)}) collective-permute-start(bf16[128,1152]{1,0:T(8,128)(2,1)S(1)} %collective-permute-done.8.rest_2_.rest_8_), channel_id=1, source_target_pairs={{0,2},{2,0},{4,6},{6,4},{8,10},{10,8},{12,14},{14,12},{16,18},{18,... | collective-permute-start | bytes 884744 | tf_op jit(solution)/shard_map/ppermute | solution.py:57
  46.2 1.5 %collective-permute-start.12 = (bf16[128,1152]{1,0:T(8,128)(2,1)S(1)}, bf16[128,1152]{1,0:T(8,128)(2,1)S(1)}, u32[]{:S(2)}, u32[]{:S(2)}) collective-permute-start(bf16[128,1152]{1,0:T(8,128)(2,1)S(1)} %collective-permute-done.11.rest_3_.rest_12_), channel_id=1, source_target_pairs={{0,4},{2,6},{4,12},{6,14},{8,0},{10,2},{12,20},{14,22},{16,8},{18,... | collective-permute-start | bytes 884744 | tf_op jit(solution)/shard_map/ppermute | solution.py:57
  47.9 1.8 %anchor_rows.6.rest_0_ = bf16[512,1152]{1,0:T(8,128)(2,1)S(1)} custom-call(s32[6]{0:T(128)S(1)} %slice_bitcast_fusion.1.bases, s32[512,3]{1,0:T(8,128)S(1)} %copy-done, bf16[512,1152]{1,0:T(8,128)(2,1)S(1)} %anchor_rows.5.rest_0_, bf16[128,1152]{1,0:T(8,128)(2,1)S(1)} %collective-permute-done.10.rest_1_.rest_10_, ...), custom_call_target="tpu_custom_call" | custom-call | flops 452984832 | bytes 3244032 | tf_op jit(solution)/shard_map/anchor_rows/pallas_call | solution.py:187
  49.7 1.9 %collective-permute-done.14.rest_3_.rest_15_ = bf16[128,1152]{1,0:T(8,128)(2,1)S(1)} collective-permute-done((bf16[128,1152]{1,0:T(8,128)(2,1)S(1)}, bf16[128,1152]{1,0:T(8,128)(2,1)S(1)}, u32[]{:S(2)}, u32[]{:S(2)}) %collective-permute-start.14) | collective-permute-done | bytes 294944 | tf_op jit(solution)/shard_map/ppermute | solution.py:57
  51.7 1.3 %collective-permute-done.12.rest_1_.rest_13_ = bf16[128,1152]{1,0:T(8,128)(2,1)S(1)} collective-permute-done((bf16[128,1152]{1,0:T(8,128)(2,1)S(1)}, bf16[128,1152]{1,0:T(8,128)(2,1)S(1)}, u32[]{:S(2)}, u32[]{:S(2)}) %collective-permute-start.12) | collective-permute-done | bytes 294944 | tf_op jit(solution)/shard_map/ppermute | solution.py:57
  52.9 1.8 %anchor_rows.7.mine = bf16[512,1152]{1,0:T(8,128)(2,1)S(1)} custom-call(s32[3]{0:T(128)S(1)} %slice_bitcast_fusion.2.bases, s32[512,3]{1,0:T(8,128)S(1)} %copy-done, bf16[512,1152]{1,0:T(8,128)(2,1)S(1)} %anchor_rows.6.rest_0_, bf16[128,1152]{1,0:T(8,128)(2,1)S(1)} %collective-permute-done.12.rest_1_.rest_13_, ...), custom_call_target="tpu_custom_call" | custom-call | flops 452984832 | bytes 3244032 | tf_op jit(solution)/shard_map/anchor_rows/pallas_call | solution.py:187
  54.9 2.8 %collective-permute-done.15.other = bf16[512,1152]{1,0:T(8,128)(2,1)S(1)} collective-permute-done((bf16[512,1152]{1,0:T(8,128)(2,1)S(1)}, bf16[512,1152]{1,0:T(8,128)(2,1)S(1)}, u32[]{:S(2)}, u32[]{:S(2)}) %collective-permute-start.15) | collective-permute-done | bytes 1179680 | tf_op jit(solution)/shard_map/ppermute | solution.py:70
  57.7 6.4 %scores.1 = (f32[2048,512]{1,0:T(8,128)S(1)}, f32[2048,512]{1,0:T(8,128)S(1)}, f32[8,512]{1,0:T(8,128)S(1)}, bf16[512,128]{1,0:T(8,128)(2,1)S(1)}) custom-call(bf16[512,1152]{1,0:T(8,128)(2,1)S(1)} %anchor_rows.7.mine, bf16[512,1152]{1,0:T(8,128)(2,1)S(1)} %collective-permute-done.15.other, bf16[512,1152]{1,0:T(8,128)(2,1)S(1)} %copy-done.1, ...), custom_call_target="tpu_custom_call" | custom-call | flops 2415919104 | bytes 13107200 | tf_op jit(solution)/shard_map/scores/pallas_call | solution.py:263
  64.3 1.0 %collective-permute-done.17.other = f32[8,512]{1,0:T(8,128)S(1)} collective-permute-done((f32[8,512]{1,0:T(8,128)S(1)}, f32[8,512]{1,0:T(8,128)S(1)}, u32[]{:S(2)}, u32[]{:S(2)}) %collective-permute-start.17) | collective-permute-done | bytes 16416 | tf_op jit(solution)/shard_map/ppermute | solution.py:70
  65.3 3.0 %gradients.1 = (f32[1,512]{1,0:T(1,128)}, f32[512,128]{1,0:T(8,128)S(1)}, bf16[4,128,128]{2,1,0:T(8,128)(2,1)S(1)}, bf16[4,128,128]{2,1,0:T(8,128)(2,1)S(1)}, bf...) custom-call(s32[16]{0:T(128)S(1)} %get-tuple-element.52.order, f32[2048,512]{1,0:T(8,128)S(1)} %get-tuple-element.35.t_in, ...), custom_call_target="tpu_custom_call" | custom-call | flops 536870912 | bytes 8388608 | tf_op jit(solution)/shard_map/gradients/pallas_call | solution.py:337
  68.5 1.5 %collective-permute-start.20 = (bf16[4,128,128]{2,1,0:T(8,128)(2,1)S(1)}, bf16[4,128,128]{2,1,0:T(8,128)(2,1)S(1)}, u32[]{:S(2)}, u32[]{:S(2)}) collective-permute-start(bf16[4,128,128]{2,1,0:T(8,128)(2,1)S(1)} %get-tuple-element.43), channel_id=1, source_target_pairs={{0,6},{2,4},{4,2},{6,0},{8,14},{10,12},{12,10},{14,8},{16,22},{18,... | collective-permute-start | bytes 393224 | tf_op jit(solution)/shard_map/ppermute | solution.py:385
  70.0 1.5 %collective-permute-start.18 = (bf16[4,128,128]{2,1,0:T(8,128)(2,1)S(1)}, bf16[4,128,128]{2,1,0:T(8,128)(2,1)S(1)}, u32[]{:S(2)}, u32[]{:S(2)}) collective-permute-start(bf16[4,128,128]{2,1,0:T(8,128)(2,1)S(1)} %get-tuple-element.41), channel_id=1, source_target_pairs={{0,2},{2,0},{4,6},{6,4},{8,10},{10,8},{12,14},{14,12},{16,18},{18,... | collective-permute-start | bytes 393224 | tf_op jit(solution)/shard_map/ppermute | solution.py:385
  72.8 3.0 %collective-permute-done.20.refs_3_ = bf16[4,128,128]{2,1,0:T(8,128)(2,1)S(1)} collective-permute-done((bf16[4,128,128]{2,1,0:T(8,128)(2,1)S(1)}, bf16[4,128,128]{2,1,0:T(8,128)(2,1)S(1)}, u32[]{:S(2)}, u32[]{:S(2)}) %collective-permute-start.20) | collective-permute-done | bytes 131104 | tf_op jit(solution)/shard_map/ppermute | solution.py:385
  75.7 2.3 %collective-permute-done.18.refs_1_ = bf16[4,128,128]{2,1,0:T(8,128)(2,1)S(1)} collective-permute-done((bf16[4,128,128]{2,1,0:T(8,128)(2,1)S(1)}, bf16[4,128,128]{2,1,0:T(8,128)(2,1)S(1)}, u32[]{:S(2)}, u32[]{:S(2)}) %collective-permute-start.18) | collective-permute-done | bytes 131104 | tf_op jit(solution)/shard_map/ppermute | solution.py:385
  78.2 1.6 %collective-permute-start.22 = (bf16[128,128]{1,0:T(8,128)(2,1)S(1)}, bf16[128,128]{1,0:T(8,128)(2,1)S(1)}, u32[]{:S(2)}, u32[]{:S(2)}) collective-permute-start(bf16[128,128]{1,0:T(8,128)(2,1)S(1)} %get-tuple-element.47), channel_id=1, source_target_pairs={{0,8},{2,10},{4,12},{6,14},{8,0},{10,2},{12,4},{14,6},{16,24},{18,... | collective-permute-start | bytes 98312 | tf_op jit(solution)/shard_map/ppermute | solution.py:391
  79.8 2.6 %collective-permute-start.23 = (bf16[128,128]{1,0:T(8,128)(2,1)S(1)}, bf16[128,128]{1,0:T(8,128)(2,1)S(1)}, u32[]{:S(2)}, u32[]{:S(2)}) collective-permute-start(bf16[128,128]{1,0:T(8,128)(2,1)S(1)} %get-tuple-element.48), channel_id=1, source_target_pairs={{0,16},{2,18},{4,20},{6,22},{8,24},{10,26},{12,28},{14,30},{16,0},... | collective-permute-start | bytes 98312 | tf_op jit(solution)/shard_map/ppermute | solution.py:391
  82.6 2.5 %collective-permute-done.23 = bf16[128,128]{1,0:T(8,128)(2,1)S(1)} collective-permute-done((bf16[128,128]{1,0:T(8,128)(2,1)S(1)}, bf16[128,128]{1,0:T(8,128)(2,1)S(1)}, u32[]{:S(2)}, u32[]{:S(2)}) %collective-permute-start.23) | collective-permute-done | bytes 32800 | tf_op jit(solution)/shard_map/ppermute | solution.py:391
  85.1 2.9 %collective-permute-done.24 = bf16[128,128]{1,0:T(8,128)(2,1)S(1)} collective-permute-done((bf16[128,128]{1,0:T(8,128)(2,1)S(1)}, bf16[128,128]{1,0:T(8,128)(2,1)S(1)}, u32[]{:S(2)}, u32[]{:S(2)}) %collective-permute-start.24) | collective-permute-done | bytes 32800 | tf_op jit(solution)/shard_map/ppermute | solution.py:391
  (44 shorter events, 8.7 us)
Async XLA Ops:
  0.6 0.9 %copy-start.2 = (bf16[128,1000]{0,1:T(8,128)(2,1)S(1)}, bf16[128,1000]{0,1:T(8,128)(2,1)}, u32[]{:S(2)}) copy-start(bf16[128,1000]{0,1:T(8,128)(2,1)} %param.11) | copy-start | bytes 768004
  1.6 0.8 copy-start.3
  2.6 10.1 %collective-permute-start.2 = (bf16[128,1152]{1,0:T(8,128)(2,1)S(1)}, bf16[128,1152]{1,0:T(8,128)(2,1)S(1)}, u32[]{:S(2)}, u32[]{:S(2)}) collective-permute-start(bf16[128,1152]{1,0:T(8,128)(2,1)S(1)} %pack_rows.1.rest_0_), channel_id=1, source_target_pairs={{0,4},{2,6},{4,12},{6,14},{8,0},{10,2},{12,20},{14,22},{16,8},{18,... | collective-permute-start | bytes 884744 | tf_op jit(solution)/shard_map/ppermute | solution.py:57
  5.6 16.4 %collective-permute-start.5 = (bf16[128,1152]{1,0:T(8,128)(2,1)S(1)}, bf16[128,1152]{1,0:T(8,128)(2,1)S(1)}, u32[]{:S(2)}, u32[]{:S(2)}) collective-permute-start(bf16[128,1152]{1,0:T(8,128)(2,1)S(1)} %pack_rows.1.rest_0_), channel_id=1, source_target_pairs={{0,8},{2,10},{4,0},{6,2},{8,16},{10,18},{12,4},{14,6},{16,24},{18,... | collective-permute-start | bytes 884744 | tf_op jit(solution)/shard_map/ppermute | solution.py:57
  5.8 20.5 %collective-permute-start = (bf16[128,1152]{1,0:T(8,128)(2,1)S(1)}, bf16[128,1152]{1,0:T(8,128)(2,1)S(1)}, u32[]{:S(2)}, u32[]{:S(2)}) collective-permute-start(bf16[128,1152]{1,0:T(8,128)(2,1)S(1)} %pack_rows.1.rest_0_), channel_id=1, source_target_pairs={{0,2},{2,0},{4,6},{6,4},{8,10},{10,8},{12,14},{14,12},{16,18},{18,... | collective-permute-start | bytes 884744 | tf_op jit(solution)/shard_map/ppermute | solution.py:57
  12.7 12.0 %collective-permute-start.3 = (bf16[128,1152]{1,0:T(8,128)(2,1)S(1)}, bf16[128,1152]{1,0:T(8,128)(2,1)S(1)}, u32[]{:S(2)}, u32[]{:S(2)}) collective-permute-start(bf16[128,1152]{1,0:T(8,128)(2,1)S(1)} %collective-permute-done.2.rest_1_), channel_id=1, source_target_pairs={{0,4},{2,6},{4,12},{6,14},{8,0},{10,2},{12,20},{14,22},{16,8},{18,... | collective-permute-start | bytes 884744 | tf_op jit(solution)/shard_map/ppermute | solution.py:57
  14.4 17.9 %copy-start = (s32[512,3]{1,0:T(8,128)S(1)}, s32[512,3]{1,0:T(8,128)}, u32[]{:S(2)}) copy-start(s32[512,3]{1,0:T(8,128)} %copy.18.cols) | copy-start | bytes 18436
  22.0 9.9 %collective-permute-start.6 = (bf16[128,1152]{1,0:T(8,128)(2,1)S(1)}, bf16[128,1152]{1,0:T(8,128)(2,1)S(1)}, u32[]{:S(2)}, u32[]{:S(2)}) collective-permute-start(bf16[128,1152]{1,0:T(8,128)(2,1)S(1)} %collective-permute-done.5.rest_2_), channel_id=1, source_target_pairs={{0,8},{2,10},{4,0},{6,2},{8,16},{10,18},{12,4},{14,6},{16,24},{18,... | collective-permute-start | bytes 884744 | tf_op jit(solution)/shard_map/ppermute | solution.py:57
  22.3 10.0 %collective-permute-start.7 = (bf16[128,1152]{1,0:T(8,128)(2,1)S(1)}, bf16[128,1152]{1,0:T(8,128)(2,1)S(1)}, u32[]{:S(2)}, u32[]{:S(2)}) collective-permute-start(bf16[128,1152]{1,0:T(8,128)(2,1)S(1)} %collective-permute-done.2.rest_1_), channel_id=1, source_target_pairs={{0,2},{2,0},{4,6},{6,4},{8,10},{10,8},{12,14},{14,12},{16,18},{18,... | collective-permute-start | bytes 884744 | tf_op jit(solution)/shard_map/ppermute | solution.py:57
  24.7 10.7 %collective-permute-start.4 = (bf16[128,1152]{1,0:T(8,128)(2,1)S(1)}, bf16[128,1152]{1,0:T(8,128)(2,1)S(1)}, u32[]{:S(2)}, u32[]{:S(2)}) collective-permute-start(bf16[128,1152]{1,0:T(8,128)(2,1)S(1)} %collective-permute-done.3.rest_4_), channel_id=1, source_target_pairs={{0,4},{2,6},{4,12},{6,14},{8,0},{10,2},{12,20},{14,22},{16,8},{18,... | collective-permute-start | bytes 884744 | tf_op jit(solution)/shard_map/ppermute | solution.py:57
  26.2 17.9 %collective-permute-start.1 = (bf16[128,1152]{1,0:T(8,128)(2,1)S(1)}, bf16[128,1152]{1,0:T(8,128)(2,1)S(1)}, u32[]{:S(2)}, u32[]{:S(2)}) collective-permute-start(bf16[128,1152]{1,0:T(8,128)(2,1)S(1)} %collective-permute-done.rest_3_), channel_id=1, source_target_pairs={{0,8},{2,10},{4,0},{6,2},{8,16},{10,18},{12,4},{14,6},{16,24},{18,... | collective-permute-start | bytes 884744 | tf_op jit(solution)/shard_map/ppermute | solution.py:57
  26.8 11.9 %collective-permute-start.9 = (bf16[128,1152]{1,0:T(8,128)(2,1)S(1)}, bf16[128,1152]{1,0:T(8,128)(2,1)S(1)}, u32[]{:S(2)}, u32[]{:S(2)}) collective-permute-start(bf16[128,1152]{1,0:T(8,128)(2,1)S(1)} %collective-permute-done.3.rest_4_), channel_id=1, source_target_pairs={{0,2},{2,0},{4,6},{6,4},{8,10},{10,8},{12,14},{14,12},{16,18},{18,... | collective-permute-start | bytes 884744 | tf_op jit(solution)/shard_map/ppermute | solution.py:57
  32.0 10.4 %collective-permute-start.8 = (bf16[128,1152]{1,0:T(8,128)(2,1)S(1)}, bf16[128,1152]{1,0:T(8,128)(2,1)S(1)}, u32[]{:S(2)}, u32[]{:S(2)}) collective-permute-start(bf16[128,1152]{1,0:T(8,128)(2,1)S(1)} %collective-permute-done.6.rest_5_), channel_id=1, source_target_pairs={{0,8},{2,10},{4,0},{6,2},{8,16},{10,18},{12,4},{14,6},{16,24},{18,... | collective-permute-start | bytes 884744 | tf_op jit(solution)/shard_map/ppermute | solution.py:57
  35.4 10.8 %collective-permute-start.11 = (bf16[128,1152]{1,0:T(8,128)(2,1)S(1)}, bf16[128,1152]{1,0:T(8,128)(2,1)S(1)}, u32[]{:S(2)}, u32[]{:S(2)}) collective-permute-start(bf16[128,1152]{1,0:T(8,128)(2,1)S(1)} %collective-permute-done.4.rest_1_.rest_7_), channel_id=1, source_target_pairs={{0,2},{2,0},{4,6},{6,4},{8,10},{10,8},{12,14},{14,12},{16,18},{18,... | collective-permute-start | bytes 884744 | tf_op jit(solution)/shard_map/ppermute | solution.py:57
  37.2 10.7 %copy-start.1 = (bf16[512,1152]{1,0:T(8,128)(2,1)S(1)}, bf16[512,1152]{1,0:T(8,128)(2,1)}, u32[]{:S(2)}) copy-start(bf16[512,1152]{1,0:T(8,128)(2,1)} %relation_rows.1.relation) | copy-start | bytes 3538948
  37.2 10.7 %collective-permute-start.10 = (bf16[128,1152]{1,0:T(8,128)(2,1)S(1)}, bf16[128,1152]{1,0:T(8,128)(2,1)S(1)}, u32[]{:S(2)}, u32[]{:S(2)}) collective-permute-start(bf16[128,1152]{1,0:T(8,128)(2,1)S(1)} %collective-permute-done.4.rest_1_.rest_7_), channel_id=1, source_target_pairs={{0,4},{2,6},{4,12},{6,14},{8,0},{10,2},{12,20},{14,22},{16,8},{18,... | collective-permute-start | bytes 884744 | tf_op jit(solution)/shard_map/ppermute | solution.py:57
  44.2 7.5 %collective-permute-start.13 = (bf16[128,1152]{1,0:T(8,128)(2,1)S(1)}, bf16[128,1152]{1,0:T(8,128)(2,1)S(1)}, u32[]{:S(2)}, u32[]{:S(2)}) collective-permute-start(bf16[128,1152]{1,0:T(8,128)(2,1)S(1)} %collective-permute-done.1.rest_2_.rest_11_), channel_id=1, source_target_pairs={{0,8},{2,10},{4,0},{6,2},{8,16},{10,18},{12,4},{14,6},{16,24},{18,... | collective-permute-start | bytes 884744 | tf_op jit(solution)/shard_map/ppermute | solution.py:57
  44.9 6.8 %collective-permute-start.14 = (bf16[128,1152]{1,0:T(8,128)(2,1)S(1)}, bf16[128,1152]{1,0:T(8,128)(2,1)S(1)}, u32[]{:S(2)}, u32[]{:S(2)}) collective-permute-start(bf16[128,1152]{1,0:T(8,128)(2,1)S(1)} %collective-permute-done.8.rest_2_.rest_8_), channel_id=1, source_target_pairs={{0,2},{2,0},{4,6},{6,4},{8,10},{10,8},{12,14},{14,12},{16,18},{18,... | collective-permute-start | bytes 884744 | tf_op jit(solution)/shard_map/ppermute | solution.py:57
  46.2 6.7 %collective-permute-start.12 = (bf16[128,1152]{1,0:T(8,128)(2,1)S(1)}, bf16[128,1152]{1,0:T(8,128)(2,1)S(1)}, u32[]{:S(2)}, u32[]{:S(2)}) collective-permute-start(bf16[128,1152]{1,0:T(8,128)(2,1)S(1)} %collective-permute-done.11.rest_3_.rest_12_), channel_id=1, source_target_pairs={{0,4},{2,6},{4,12},{6,14},{8,0},{10,2},{12,20},{14,22},{16,8},{18,... | collective-permute-start | bytes 884744 | tf_op jit(solution)/shard_map/ppermute | solution.py:57
  47.9 7.0 %collective-permute-start.16 = (bf16[512,1152]{1,0:T(8,128)(2,1)S(1)}, bf16[512,1152]{1,0:T(8,128)(2,1)S(1)}, u32[]{:S(2)}, u32[]{:S(2)}) collective-permute-start(bf16[512,1152]{1,0:T(8,128)(2,1)S(1)} %copy-done.1), channel_id=1, source_target_pairs={{0,1},{1,0},{2,3},{3,2},{4,5},{5,4},{6,7},{7,6},{8,9},{9,8},{10,11... | collective-permute-start | bytes 3538952 | tf_op jit(solution)/shard_map/ppermute | solution.py:70
  54.8 2.9 %collective-permute-start.15 = (bf16[512,1152]{1,0:T(8,128)(2,1)S(1)}, bf16[512,1152]{1,0:T(8,128)(2,1)S(1)}, u32[]{:S(2)}, u32[]{:S(2)}) collective-permute-start(bf16[512,1152]{1,0:T(8,128)(2,1)S(1)} %anchor_rows.7.mine), channel_id=1, source_target_pairs={{0,1},{1,0},{2,3},{3,2},{4,5},{5,4},{6,7},{7,6},{8,9},{9,8},{10,11... | collective-permute-start | bytes 3538952 | tf_op jit(solution)/shard_map/ppermute | solution.py:70
  64.1 1.2 %collective-permute-start.17 = (f32[8,512]{1,0:T(8,128)S(1)}, f32[8,512]{1,0:T(8,128)S(1)}, u32[]{:S(2)}, u32[]{:S(2)}) collective-permute-start(f32[8,512]{1,0:T(8,128)S(1)} %get-tuple-element.37.mine), channel_id=1, source_target_pairs={{0,1},{1,0},{2,3},{3,2},{4,5},{5,4},{6,7},{7,6},{8,9},{9,8},{10,11... | collective-permute-start | bytes 49160 | tf_op jit(solution)/shard_map/ppermute | solution.py:70
  68.3 3.7 %collective-permute-start.21 = (f32[512,128]{1,0:T(8,128)S(1)}, f32[512,128]{1,0:T(8,128)S(1)}, u32[]{:S(2)}, u32[]{:S(2)}) collective-permute-start(f32[512,128]{1,0:T(8,128)S(1)} %get-tuple-element.44), channel_id=1, source_target_pairs={{0,1},{1,0},{2,3},{3,2},{4,5},{5,4},{6,7},{7,6},{8,9},{9,8},{10,11... | collective-permute-start | bytes 786440 | tf_op jit(solution)/shard_map/ppermute | solution.py:70
  68.5 7.2 %collective-permute-start.20 = (bf16[4,128,128]{2,1,0:T(8,128)(2,1)S(1)}, bf16[4,128,128]{2,1,0:T(8,128)(2,1)S(1)}, u32[]{:S(2)}, u32[]{:S(2)}) collective-permute-start(bf16[4,128,128]{2,1,0:T(8,128)(2,1)S(1)} %get-tuple-element.43), channel_id=1, source_target_pairs={{0,6},{2,4},{4,2},{6,0},{8,14},{10,12},{12,10},{14,8},{16,22},{18,... | collective-permute-start | bytes 393224 | tf_op jit(solution)/shard_map/ppermute | solution.py:385
  70.0 8.1 %collective-permute-start.18 = (bf16[4,128,128]{2,1,0:T(8,128)(2,1)S(1)}, bf16[4,128,128]{2,1,0:T(8,128)(2,1)S(1)}, u32[]{:S(2)}, u32[]{:S(2)}) collective-permute-start(bf16[4,128,128]{2,1,0:T(8,128)(2,1)S(1)} %get-tuple-element.41), channel_id=1, source_target_pairs={{0,2},{2,0},{4,6},{6,4},{8,10},{10,8},{12,14},{14,12},{16,18},{18,... | collective-permute-start | bytes 393224 | tf_op jit(solution)/shard_map/ppermute | solution.py:385
  71.5 6.6 %collective-permute-start.19 = (bf16[4,128,128]{2,1,0:T(8,128)(2,1)S(1)}, bf16[4,128,128]{2,1,0:T(8,128)(2,1)S(1)}, u32[]{:S(2)}, u32[]{:S(2)}) collective-permute-start(bf16[4,128,128]{2,1,0:T(8,128)(2,1)S(1)} %get-tuple-element.42), channel_id=1, source_target_pairs={{0,4},{2,6},{4,0},{6,2},{8,12},{10,14},{12,8},{14,10},{16,20},{18,... | collective-permute-start | bytes 393224 | tf_op jit(solution)/shard_map/ppermute | solution.py:385
  78.2 4.5 %collective-permute-start.22 = (bf16[128,128]{1,0:T(8,128)(2,1)S(1)}, bf16[128,128]{1,0:T(8,128)(2,1)S(1)}, u32[]{:S(2)}, u32[]{:S(2)}) collective-permute-start(bf16[128,128]{1,0:T(8,128)(2,1)S(1)} %get-tuple-element.47), channel_id=1, source_target_pairs={{0,8},{2,10},{4,12},{6,14},{8,0},{10,2},{12,4},{14,6},{16,24},{18,... | collective-permute-start | bytes 98312 | tf_op jit(solution)/shard_map/ppermute | solution.py:391
  79.8 5.4 %collective-permute-start.23 = (bf16[128,128]{1,0:T(8,128)(2,1)S(1)}, bf16[128,128]{1,0:T(8,128)(2,1)S(1)}, u32[]{:S(2)}, u32[]{:S(2)}) collective-permute-start(bf16[128,128]{1,0:T(8,128)(2,1)S(1)} %get-tuple-element.48), channel_id=1, source_target_pairs={{0,16},{2,18},{4,20},{6,22},{8,24},{10,26},{12,28},{14,30},{16,0},... | collective-permute-start | bytes 98312 | tf_op jit(solution)/shard_map/ppermute | solution.py:391
  82.4 5.7 %collective-permute-start.24 = (bf16[128,128]{1,0:T(8,128)(2,1)S(1)}, bf16[128,128]{1,0:T(8,128)(2,1)S(1)}, u32[]{:S(2)}, u32[]{:S(2)}) collective-permute-start(bf16[128,128]{1,0:T(8,128)(2,1)S(1)} %get-tuple-element.49), channel_id=1, source_target_pairs={{0,24},{2,26},{4,28},{6,30},{8,16},{10,18},{12,20},{14,22},{16,8},... | collective-permute-start | bytes 98312 | tf_op jit(solution)/shard_map/ppermute | solution.py:391
where the time goes:
time: 89 us; the launch traced here: 88.7 us
  waiting for transfers between devices  29.8 us (33%)
  starting transfers between devices  26.7 us (30%)
  Pallas kernels  25.8 us (29%)
  local copies, waits for them, and re-layouts  3.46 us (4%)
  other arithmetic  2.11 us (2%)
    ppermute x15, starting transfers between devices, move(): return lax.ppermute(x, 'query', sorted(pairs))  18.3 us
    ppermute x15, waiting for transfers between devices, move(): return lax.ppermute(x, 'query', sorted(pairs))  15.1 us
    pallas_call x4, Pallas kernels, anchor_rows(): pl.pallas_call(functools.partial(anchor_kernel, count, own, acc is not No...  8.57 us
    pallas_call x1, Pallas kernels, relation_rows(): pl.pallas_call(functools.partial(relation_kernel, shape, rel, block), out...  7.61 us
    pallas_call x1, Pallas kernels, scores(): pl.pallas_call(functools.partial(score_kernel, shape, own, n, chunk), out...  6.37 us
    ppermute x3, waiting for transfers between devices, reduce_blocks(): total = total + lax.ppermute(sums[e], 'query', pairs).astype(F32)  5.48 us
    ppermute x3, waiting for transfers between devices, reduce_blocks(): lax.ppermute(blocks[d], 'query', [(i, i ^ d) for i in range(n)])  5.32 us
    ppermute x3, starting transfers between devices, reduce_blocks(): total = total + lax.ppermute(sums[e], 'query', pairs).astype(F32)  4.45 us
  transfers between devices with their start and end apart: 25, of which 11 were waited for; matrix products, arithmetic and copies ran while one was open for 4% of the time, Pallas kernels for 18%

commit v1 on v0

--- a/solution.py
+++ b/solution.py
@@ -87,19 +87,25 @@
         out[:, at : at + shape.wide] = jnp.concatenate([piece, pad], axis=1).astype(BF16)
 
 
-def pack_kernel(shape, teacher_t, student, out):
+def pack_kernel(shape, teacher_t, student, anchor_ids, relation_ids, side_flags, out, cols):
+    rows = jnp.concatenate([anchor_ids[...], relation_ids[...], side_flags[...]], axis=0).astype(F32)
+    rows = jnp.concatenate([rows, jnp.zeros((5, rows.shape[1]), F32)], axis=0)
+    cols[...] = rows.T.astype(jnp.int32)
     put_row(out, student[...].astype(F32), teacher_t[...].astype(F32).T, shape)
 
 
-def pack(teacher, student, shape):
+def pack(teacher, student, ids, shape):
     return pl.pallas_call(
         functools.partial(pack_kernel, shape),
-        out_shape=jax.ShapeDtypeStruct((teacher.shape[0], shape.total), BF16),
-        in_specs=[VMEM, VMEM],
-        out_specs=VMEM,
-        compiler_params=pltpu.CompilerParams(vmem_limit_bytes=8 * MIB),
+        out_shape=(
+            jax.ShapeDtypeStruct((teacher.shape[0], shape.total), BF16),
+            jax.ShapeDtypeStruct((ids[0].shape[0], 8), jnp.int32),
+        ),
+        in_specs=[VMEM] * 5,
+        out_specs=(VMEM, VMEM),
+        compiler_params=pltpu.CompilerParams(vmem_limit_bytes=60 * MIB),
         name="pack_rows",
-    )(teacher.T, student)
+    )(teacher.T, student, *[x[None] for x in ids])
 
 
 def relation_kernel(shape, rel, block, base, cols, table_t, student, out, acc, acc_s):
@@ -107,22 +113,33 @@
     start = (base[0] + step) * block
     ids = cols[:, 1:2] - start
     hot = (ids == lax.broadcasted_iota(jnp.int32, (cols.shape[0], block), 1)).astype(F32).astype(BF16)
-    lanes = lax.broadcasted_iota(jnp.int32, table_t.shape, 1)
-    rows = lax.broadcasted_iota(jnp.int32, student.shape, 0)
-    table = jnp.where(lanes < rel - start, table_t[...], jnp.zeros_like(table_t))
-    small = jnp.where(rows < rel - start, student[...], jnp.zeros_like(student))
-    part = lax.dot_general(hot, table, (((1,), (1,)), ((), ())), preferred_element_type=F32)
-    part_s = jnp.dot(hot, small, preferred_element_type=F32)
-
-    @pl.when(step == 0)
+
+    def add(table, small):
+        part = lax.dot_general(hot, table, (((1,), (1,)), ((), ())), preferred_element_type=F32)
+        part_s = jnp.dot(hot, small, preferred_element_type=F32)
+
+        @pl.when(step == 0)
+        def _():
+            acc[...] = part
+            acc_s[...] = part_s
+
+        @pl.when(step > 0)
+        def _():
+            acc[...] += part
+            acc_s[...] += part_s
+
+    @pl.when(start + block <= rel)
     def _():
-        acc[...] = part
-        acc_s[...] = part_s
-
-    @pl.when(step > 0)
+        add(table_t[...], student[...])
+
+    @pl.when(start + block > rel)
     def _():
-        acc[...] += part
-        acc_s[...] += part_s
+        lanes = lax.broadcasted_iota(jnp.int32, table_t.shape, 1)
+        rows = lax.broadcasted_iota(jnp.int32, student.shape, 0)
+        add(
+            jnp.where(lanes < rel - start, table_t[...], jnp.zeros_like(table_t)),
+            jnp.where(rows < rel - start, student[...], jnp.zeros_like(student)),
+        )
 
     @pl.when(step == pl.num_programs(0) - 1)
     def _():
@@ -387,7 +404,7 @@
     sums = add_blocks(terms)
     total = sums[0]
     for e in range(1, far):
-        pairs = [(h * near + r, (h ^ e if far & (far - 1) == 0 else (h + e) % far) * near + r) for h in range(far) for r in range(near)]
+        pairs = [(h * near + r, (h + e) % far * near + r) for h in range(far) for r in range(near)]
         total = total + lax.ppermute(sums[e], "query", pairs).astype(F32)
     return total, beside
 
@@ -398,8 +415,7 @@
     table = owners(place, held, n)
     near = next(k for k in (4, 2, 1) if n % k == 0)
     me = np.arange(n)[:, None]
-    far_move = (table // near) ^ (me // near) if n // near & (n // near - 1) == 0 else (table // near - me // near) % (n // near)
-    position = ((table % near) ^ (me % near)) * (n // near) + far_move
+    position = ((table % near) ^ (me % near)) * (n // near) + (table // near - me // near) % (n // near)
 
     def per_device(
         anchor_ids,
@@ -414,9 +430,10 @@
         shape = Shape(tw, student_entities.shape[1])
         owner, order = jnp.asarray(np.stack([table, position], axis=1))[lax.axis_index("query")]
         bases = (owner + lax.axis_index("entity") * n) * own
-        cols = jnp.stack([anchor_ids, relation_ids, side_flags], axis=1)
-
-        have = {(0, 0): pack(teacher_entities, student_entities, shape)}
+        packed, cols = pack(
+            teacher_entities, student_entities, (anchor_ids, relation_ids, side_flags), shape
+        )
+        have = {(0, 0): packed}
         block = 768
         per_core = -(-teacher_relations.shape[0] // (2 * block))
         base = (lax.axis_index("entity") % 2 * per_core).astype(jnp.int32)[None]
@@ -425,25 +442,13 @@
         anchors, counted = None, 0
         for number, step in enumerate(steps):
             got = {new: move(have[old], place, shift) for shift, old, new in step}
-            beside = None
             if number == 0:
                 relation = relation_rows(base, cols, teacher_relations, student_relations, per_core, block, shape)
-                beside = relation
-            elif number >= len(steps) // 2:
-                names = held[counted : len(have)]
-                anchors = anchor_rows(bases[counted:], cols, [have[h] for h in names], anchors, shape)
+                got, relation = lax.optimization_barrier((got, relation))
+                relation_b = partner(relation, groups, 1)
+            if number == len(steps) - 1:
                 counted = len(have)
-                beside = anchors
-            sent = [old for _, old, _ in steps[number + 1] if old in got] if number + 1 < len(steps) else []
-            if sent and beside is not None:
-                gate = sent[len(sent) // 2]
-                got[gate], beside = lax.optimization_barrier((got[gate], beside))
-                if number == 0:
-                    relation = beside
-                else:
-                    anchors = beside
-            if number == 0:
-                relation_b = partner(relation, groups, 1)
+                anchors = anchor_rows(bases, cols, [have[h] for h in held[:counted]], None, shape)
             have.update(got)
         shards = [have[h] for h in held]
         mine = anchor_rows(bases[counted:], cols, shards[counted:], anchors, shape)

time: 89 us -> 86.2 us (0.969)
  local copies, waits for them, and re-layouts: 3.46 us -> 0.76 us
  starting transfers between devices: 26.7 us -> 27.8 us
    ppermute x15, waiting for transfers between devices: 15.1 us -> 18.3 us  [move(): return lax.ppermute(x, 'query', sorted(pairs))]
    ppermute x3, waiting for transfers between devices: 5.48 us -> 2.58 us  [reduce_blocks(): total = total + lax.ppermute(sums[e], 'query', pairs).astype(F32)]
    pallas_call x4 -> x2, Pallas kernels: 8.57 us -> 6.76 us  [anchor_rows(): pl.pallas_call(functools.partial(anchor_kernel, count, own, acc is not No...]
    pallas_call x1, Pallas kernels: 0.26 us -> 2.04 us  [pack(): pl.pallas_call(functools.partial(pack_kernel, shape), out_shape=(jax.Shap...]
    unnamed x8 -> x6, local copies, waits for them, and re-layouts: 1.71 us -> 0.01 us
    ppermute x3, starting transfers between devices: 4.45 us -> 5.58 us  [reduce_blocks(): total = total + lax.ppermute(sums[e], 'query', pairs).astype(F32)]
    ppermute x15, starting transfers between devices: 18.3 us -> 17.3 us  [move(): return lax.ppermute(x, 'query', sorted(pairs))]
    ppermute x4, starting transfers between devices: 0.51 us -> 1.42 us  [partner(): return lax.ppermute(x, 'entity', [(i, i ^ far) for i in range(size)])]
  transfers between devices with their start and end apart: 25 -> 25, of which waited for: 11 -> 13; matrix products, arithmetic and copies ran while one was open for 4% -> 2% of each run, Pallas kernels for 18% -> 17%
where the time goes in v1:
time: 86.2 us; the launch traced here: 86 us
  waiting for transfers between devices  29.2 us (34%)
  starting transfers between devices  27.8 us (32%)
  Pallas kernels  26.1 us (30%)
  other arithmetic  1.38 us (2%)
    ppermute x15, waiting for transfers between devices, move(): return lax.ppermute(x, 'query', sorted(pairs))  18.3 us
    ppermute x15, starting transfers between devices, move(): return lax.ppermute(x, 'query', sorted(pairs))  17.3 us
    pallas_call x1, Pallas kernels, relation_rows(): pl.pallas_call(functools.partial(relation_kernel, shape, rel, block), out...  7.86 us
    pallas_call x2, Pallas kernels, anchor_rows(): pl.pallas_call(functools.partial(anchor_kernel, count, own, acc is not No...  6.76 us
    pallas_call x1, Pallas kernels, scores(): pl.pallas_call(functools.partial(score_kernel, shape, own, n, chunk), out...  6.37 us
    ppermute x3, starting transfers between devices, reduce_blocks(): total = total + lax.ppermute(sums[e], 'query', pairs).astype(F32)  5.58 us
    ppermute x3, waiting for transfers between devices, reduce_blocks(): lax.ppermute(blocks[d], 'query', [(i, i ^ d) for i in range(n)])  5.05 us
    ppermute x3, starting transfers between devices, reduce_blocks(): lax.ppermute(blocks[d], 'query', [(i, i ^ d) for i in range(n)])  3.49 us
  transfers between devices with their start and end apart: 25, of which 13 were waited for; matrix products, arithmetic and copies ran while one was open for 2% of the time, Pallas kernels for 17%

profile of v1, /device:TPU:0, one launch (start us, length us, event | category | flops | bytes accessed | tf_op | source)
XLA Modules:
  0.0 86.0 jit_solution(9525037577831500132)
XLA Ops:
  0.6 2.0 %pack_rows.1 = (bf16[128,1152]{1,0:T(8,128)(2,1)}, s32[512,8]{1,0:T(8,128)}) custom-call(bf16[1000,128]{1,0:T(8,128)(2,1)} %bitcast.14, bf16[128,128]{1,0:T(8,128)(2,1)} %student.2, s32[1,512]{1,0:T(1,128)} %bitcast.15, s32[1,512]{1,0:T(1,128)} %bitcast.16, s32[1,512]{1,0:T(1,128)} %bitcast.17), custom_call_target="tpu_custom_call" | custom-call | tf_op jit(solution)/shard_map/pack_rows/pallas_call | solution.py:98
  2.7 2.9 %collective-permute-start.2 = (bf16[128,1152]{1,0:T(8,128)(2,1)}, bf16[128,1152]{1,0:T(8,128)(2,1)S(1)}, u32[]{:S(2)}, u32[]{:S(2)}) collective-permute-start(bf16[128,1152]{1,0:T(8,128)(2,1)} %get-tuple-element.29.rest_0_), channel_id=1, source_target_pairs={{0,2},{2,0},{4,6},{6,4},{8,10},{10,8},{12,14},{14,12},{16,18},{18,... | collective-permute-start | bytes 884744 | tf_op jit(solution)/shard_map/ppermute | solution.py:57
  5.6 1.6 %collective-permute-start.1 = (bf16[128,1152]{1,0:T(8,128)(2,1)}, bf16[128,1152]{1,0:T(8,128)(2,1)S(1)}, u32[]{:S(2)}, u32[]{:S(2)}) collective-permute-start(bf16[128,1152]{1,0:T(8,128)(2,1)} %get-tuple-element.29.rest_0_), channel_id=1, source_target_pairs={{0,8},{2,10},{4,0},{6,2},{8,16},{10,18},{12,4},{14,6},{16,24},{18,... | collective-permute-start | bytes 884744 | tf_op jit(solution)/shard_map/ppermute | solution.py:57
  7.7 7.9 %relation_rows.1.relation = bf16[512,1152]{1,0:T(8,128)(2,1)} custom-call(s32[1]{0:T(128)} %bitcast.7.base, s32[512,8]{1,0:T(8,128)} %get-tuple-element.27.cols, bf16[1000,4131]{1,0:T(8,128)(2,1)} %bitcast.13, bf16[4131,128]{1,0:T(8,128)(2,1)} %student.3), custom_call_target="tpu_custom_call" | custom-call | flops 2359296000 | bytes 4608000 | tf_op jit(solution)/shard_map/relation_rows/pallas_call | solution.py:154
  15.6 1.5 %collective-permute-start.3 = (bf16[128,1152]{1,0:T(8,128)(2,1)S(1)}, bf16[128,1152]{1,0:T(8,128)(2,1)S(1)}, u32[]{:S(2)}, u32[]{:S(2)}) collective-permute-start(bf16[128,1152]{1,0:T(8,128)(2,1)S(1)} %collective-permute-done.rest_1_), channel_id=1, source_target_pairs={{0,4},{2,6},{4,12},{6,14},{8,0},{10,2},{12,20},{14,22},{16,8},{18,... | collective-permute-start | bytes 884744 | tf_op jit(solution)/shard_map/ppermute | solution.py:57
  17.6 5.9 %collective-permute-done.3.rest_4_ = bf16[128,1152]{1,0:T(8,128)(2,1)S(1)} collective-permute-done((bf16[128,1152]{1,0:T(8,128)(2,1)S(1)}, bf16[128,1152]{1,0:T(8,128)(2,1)S(1)}, u32[]{:S(2)}, u32[]{:S(2)}) %collective-permute-start.3) | collective-permute-done | bytes 294944 | tf_op jit(solution)/shard_map/ppermute | solution.py:57
  23.5 1.5 %collective-permute-start.6 = (bf16[128,1152]{1,0:T(8,128)(2,1)S(1)}, bf16[128,1152]{1,0:T(8,128)(2,1)S(1)}, u32[]{:S(2)}, u32[]{:S(2)}) collective-permute-start(bf16[128,1152]{1,0:T(8,128)(2,1)S(1)} %collective-permute-done.3.rest_4_), channel_id=1, source_target_pairs={{0,4},{2,6},{4,12},{6,14},{8,0},{10,2},{12,20},{14,22},{16,8},{18,... | collective-permute-start | bytes 884744 | tf_op jit(solution)/shard_map/ppermute | solution.py:57
  26.0 1.7 %collective-permute-start.7 = (bf16[128,1152]{1,0:T(8,128)(2,1)S(1)}, bf16[128,1152]{1,0:T(8,128)(2,1)S(1)}, u32[]{:S(2)}, u32[]{:S(2)}) collective-permute-start(bf16[128,1152]{1,0:T(8,128)(2,1)S(1)} %collective-permute-done.4.rest_5_), channel_id=1, source_target_pairs={{0,8},{2,10},{4,0},{6,2},{8,16},{10,18},{12,4},{14,6},{16,24},{18,... | collective-permute-start | bytes 884744 | tf_op jit(solution)/shard_map/ppermute | solution.py:57
  27.6 2.8 %collective-permute-done.6.rest_7_ = bf16[128,1152]{1,0:T(8,128)(2,1)S(1)} collective-permute-done((bf16[128,1152]{1,0:T(8,128)(2,1)S(1)}, bf16[128,1152]{1,0:T(8,128)(2,1)S(1)}, u32[]{:S(2)}, u32[]{:S(2)}) %collective-permute-start.6) | collective-permute-done | bytes 294944 | tf_op jit(solution)/shard_map/ppermute | solution.py:57
  30.8 0.7 constant_dynamic-slice_fusion
  31.5 1.7 %collective-permute-start.8 = (bf16[128,1152]{1,0:T(8,128)(2,1)S(1)}, bf16[128,1152]{1,0:T(8,128)(2,1)S(1)}, u32[]{:S(2)}, u32[]{:S(2)}) collective-permute-start(bf16[128,1152]{1,0:T(8,128)(2,1)S(1)} %collective-permute-done.3.rest_4_), channel_id=1, source_target_pairs={{0,2},{2,0},{4,6},{6,4},{8,10},{10,8},{12,14},{14,12},{16,18},{18,... | collective-permute-start | bytes 884744 | tf_op jit(solution)/shard_map/ppermute | solution.py:57
  33.2 1.8 %collective-permute-done.10.rest_11_ = bf16[128,1152]{1,0:T(8,128)(2,1)S(1)} collective-permute-done((bf16[128,1152]{1,0:T(8,128)(2,1)S(1)}, bf16[128,1152]{1,0:T(8,128)(2,1)S(1)}, u32[]{:S(2)}, u32[]{:S(2)}) %collective-permute-start.10) | collective-permute-done | bytes 294944 | tf_op jit(solution)/shard_map/ppermute | solution.py:57
  35.0 1.6 %collective-permute-start.9 = (bf16[128,1152]{1,0:T(8,128)(2,1)S(1)}, bf16[128,1152]{1,0:T(8,128)(2,1)S(1)}, u32[]{:S(2)}, u32[]{:S(2)}) collective-permute-start(bf16[128,1152]{1,0:T(8,128)(2,1)S(1)} %collective-permute-done.6.rest_7_), channel_id=1, source_target_pairs={{0,4},{2,6},{4,12},{6,14},{8,0},{10,2},{12,20},{14,22},{16,8},{18,... | collective-permute-start | bytes 884744 | tf_op jit(solution)/shard_map/ppermute | solution.py:57
  37.1 4.2 %collective-permute-done.7.rest_8_ = bf16[128,1152]{1,0:T(8,128)(2,1)S(1)} collective-permute-done((bf16[128,1152]{1,0:T(8,128)(2,1)S(1)}, bf16[128,1152]{1,0:T(8,128)(2,1)S(1)}, u32[]{:S(2)}, u32[]{:S(2)}) %collective-permute-start.7) | collective-permute-done | bytes 294944 | tf_op jit(solution)/shard_map/ppermute | solution.py:57
  41.8 1.6 %collective-permute-start.12 = (bf16[128,1152]{1,0:T(8,128)(2,1)S(1)}, bf16[128,1152]{1,0:T(8,128)(2,1)S(1)}, u32[]{:S(2)}, u32[]{:S(2)}) collective-permute-start(bf16[128,1152]{1,0:T(8,128)(2,1)S(1)} %collective-permute-done.11.rest_12_), channel_id=1, source_target_pairs={{0,4},{2,6},{4,12},{6,14},{8,0},{10,2},{12,20},{14,22},{16,8},{18,... | collective-permute-start | bytes 884744 | tf_op jit(solution)/shard_map/ppermute | solution.py:57
  43.4 3.5 %collective-permute-done.8.rest_9_ = bf16[128,1152]{1,0:T(8,128)(2,1)S(1)} collective-permute-done((bf16[128,1152]{1,0:T(8,128)(2,1)S(1)}, bf16[128,1152]{1,0:T(8,128)(2,1)S(1)}, u32[]{:S(2)}, u32[]{:S(2)}) %collective-permute-start.8) | collective-permute-done | bytes 294944 | tf_op jit(solution)/shard_map/ppermute | solution.py:57
  46.9 4.9 %anchor_rows.2.rest_0_ = bf16[512,1152]{1,0:T(8,128)(2,1)S(1)} custom-call(s32[16]{0:T(128)S(1)} %bitcast.12, s32[512,8]{1,0:T(8,128)S(1)} %copy-done.1, bf16[128,1152]{1,0:T(8,128)(2,1)S(1)} %copy-done.2, bf16[128,1152]{1,0:T(8,128)(2,1)S(1)} %collective-permute-done.rest_1_, bf16[128,1152]{1,0:T(8,128)(2,1)S(1)} %collective-permute-done.1.rest_2_, ...), custom_call_target="tpu_custom_call" | custom-call | flops 1962934272 | bytes 6193152 | tf_op jit(solution)/shard_map/anchor_rows/pallas_call | solution.py:204
  51.9 1.8 %anchor_rows.3.mine = bf16[512,1152]{1,0:T(8,128)(2,1)S(1)} custom-call(s32[3]{0:T(128)S(1)} %slice_bitcast_fusion.bases, s32[512,8]{1,0:T(8,128)S(1)} %copy-done.1, bf16[512,1152]{1,0:T(8,128)(2,1)S(1)} %anchor_rows.2.rest_0_, bf16[128,1152]{1,0:T(8,128)(2,1)S(1)} %collective-permute-done.12.rest_1_.rest_13_, ...), custom_call_target="tpu_custom_call" | custom-call | flops 452984832 | bytes 3244032 | tf_op jit(solution)/shard_map/anchor_rows/pallas_call | solution.py:204
  54.3 2.5 %collective-permute-done.15.other = bf16[512,1152]{1,0:T(8,128)(2,1)S(1)} collective-permute-done((bf16[512,1152]{1,0:T(8,128)(2,1)S(1)}, bf16[512,1152]{1,0:T(8,128)(2,1)S(1)}, u32[]{:S(2)}, u32[]{:S(2)}) %collective-permute-start.15) | collective-permute-done | bytes 1179680 | tf_op jit(solution)/shard_map/ppermute | solution.py:70
  56.8 6.4 %scores.1 = (f32[2048,512]{1,0:T(8,128)S(1)}, f32[2048,512]{1,0:T(8,128)S(1)}, f32[8,512]{1,0:T(8,128)S(1)}, bf16[512,128]{1,0:T(8,128)(2,1)S(1)}) custom-call(bf16[512,1152]{1,0:T(8,128)(2,1)S(1)} %anchor_rows.3.mine, bf16[512,1152]{1,0:T(8,128)(2,1)S(1)} %collective-permute-done.15.other, bf16[512,1152]{1,0:T(8,128)(2,1)S(1)} %copy-done, ...), custom_call_target="tpu_custom_call" | custom-call | flops 2415919104 | bytes 13107200 | tf_op jit(solution)/shard_map/scores/pallas_call | solution.py:280
  63.6 0.8 collective-permute-done.17.other
  64.5 3.0 %gradients.1 = (f32[1,512]{1,0:T(1,128)}, f32[512,128]{1,0:T(8,128)S(1)}, bf16[4,128,128]{2,1,0:T(8,128)(2,1)S(1)}, bf16[4,128,128]{2,1,0:T(8,128)(2,1)S(1)}, bf...) custom-call(s32[16]{0:T(128)S(1)} %get-tuple-element.52.order, f32[2048,512]{1,0:T(8,128)S(1)} %get-tuple-element.35.t_in, ...), custom_call_target="tpu_custom_call" | custom-call | flops 536870912 | bytes 8388608 | tf_op jit(solution)/shard_map/gradients/pallas_call | solution.py:354
  67.8 1.4 %collective-permute-start.20 = (bf16[4,128,128]{2,1,0:T(8,128)(2,1)S(1)}, bf16[4,128,128]{2,1,0:T(8,128)(2,1)S(1)}, u32[]{:S(2)}, u32[]{:S(2)}) collective-permute-start(bf16[4,128,128]{2,1,0:T(8,128)(2,1)S(1)} %get-tuple-element.43), channel_id=1, source_target_pairs={{0,6},{2,4},{4,2},{6,0},{8,14},{10,12},{12,10},{14,8},{16,22},{18,... | collective-permute-start | bytes 393224 | tf_op jit(solution)/shard_map/ppermute | solution.py:402
  69.3 1.5 %collective-permute-start.18 = (bf16[4,128,128]{2,1,0:T(8,128)(2,1)S(1)}, bf16[4,128,128]{2,1,0:T(8,128)(2,1)S(1)}, u32[]{:S(2)}, u32[]{:S(2)}) collective-permute-start(bf16[4,128,128]{2,1,0:T(8,128)(2,1)S(1)} %get-tuple-element.41), channel_id=1, source_target_pairs={{0,2},{2,0},{4,6},{6,4},{8,10},{10,8},{12,14},{14,12},{16,18},{18,... | collective-permute-start | bytes 393224 | tf_op jit(solution)/shard_map/ppermute | solution.py:402
  71.3 0.7 add.30
  72.1 3.0 %collective-permute-done.20.refs_3_ = bf16[4,128,128]{2,1,0:T(8,128)(2,1)S(1)} collective-permute-done((bf16[4,128,128]{2,1,0:T(8,128)(2,1)S(1)}, bf16[4,128,128]{2,1,0:T(8,128)(2,1)S(1)}, u32[]{:S(2)}, u32[]{:S(2)}) %collective-permute-start.20) | collective-permute-done | bytes 131104 | tf_op jit(solution)/shard_map/ppermute | solution.py:402
  75.1 2.0 %collective-permute-done.18.refs_1_ = bf16[4,128,128]{2,1,0:T(8,128)(2,1)S(1)} collective-permute-done((bf16[4,128,128]{2,1,0:T(8,128)(2,1)S(1)}, bf16[4,128,128]{2,1,0:T(8,128)(2,1)S(1)}, u32[]{:S(2)}, u32[]{:S(2)}) %collective-permute-start.18) | collective-permute-done | bytes 131104 | tf_op jit(solution)/shard_map/ppermute | solution.py:402
  77.2 1.7 %collective-permute-start.22 = (bf16[128,128]{1,0:T(8,128)(2,1)S(1)}, bf16[128,128]{1,0:T(8,128)(2,1)S(1)}, u32[]{:S(2)}, u32[]{:S(2)}) collective-permute-start(bf16[128,128]{1,0:T(8,128)(2,1)S(1)} %get-tuple-element.47), channel_id=1, source_target_pairs={{0,8},{2,10},{4,12},{6,14},{8,16},{10,18},{12,20},{14,22},{16,24},... | collective-permute-start | bytes 98312 | tf_op jit(solution)/shard_map/ppermute | solution.py:408
  78.8 2.6 %collective-permute-start.23 = (bf16[128,128]{1,0:T(8,128)(2,1)S(1)}, bf16[128,128]{1,0:T(8,128)(2,1)S(1)}, u32[]{:S(2)}, u32[]{:S(2)}) collective-permute-start(bf16[128,128]{1,0:T(8,128)(2,1)S(1)} %get-tuple-element.48), channel_id=1, source_target_pairs={{0,16},{2,18},{4,20},{6,22},{8,24},{10,26},{12,28},{14,30},{16,0},... | collective-permute-start | bytes 98312 | tf_op jit(solution)/shard_map/ppermute | solution.py:408
  81.4 1.3 %collective-permute-start.24 = (bf16[128,128]{1,0:T(8,128)(2,1)S(1)}, bf16[128,128]{1,0:T(8,128)(2,1)S(1)}, u32[]{:S(2)}, u32[]{:S(2)}) collective-permute-start(bf16[128,128]{1,0:T(8,128)(2,1)S(1)} %get-tuple-element.49), channel_id=1, source_target_pairs={{0,24},{2,26},{4,28},{6,30},{8,0},{10,2},{12,4},{14,6},{16,8},{18,... | collective-permute-start | bytes 98312 | tf_op jit(solution)/shard_map/ppermute | solution.py:408
  83.3 0.7 collective-permute-done.23
  84.0 1.3 %collective-permute-done.24 = bf16[128,128]{1,0:T(8,128)(2,1)S(1)} collective-permute-done((bf16[128,128]{1,0:T(8,128)(2,1)S(1)}, bf16[128,128]{1,0:T(8,128)(2,1)S(1)}, u32[]{:S(2)}, u32[]{:S(2)}) %collective-permute-start.24) | collective-permute-done | bytes 32800 | tf_op jit(solution)/shard_map/ppermute | solution.py:408
  (36 shorter events, 6.7 us)
Async XLA Ops:
  2.7 12.8 %collective-permute-start.2 = (bf16[128,1152]{1,0:T(8,128)(2,1)}, bf16[128,1152]{1,0:T(8,128)(2,1)S(1)}, u32[]{:S(2)}, u32[]{:S(2)}) collective-permute-start(bf16[128,1152]{1,0:T(8,128)(2,1)} %get-tuple-element.29.rest_0_), channel_id=1, source_target_pairs={{0,2},{2,0},{4,6},{6,4},{8,10},{10,8},{12,14},{14,12},{16,18},{18,... | collective-permute-start | bytes 884744 | tf_op jit(solution)/shard_map/ppermute | solution.py:57
  5.6 9.9 %collective-permute-start.1 = (bf16[128,1152]{1,0:T(8,128)(2,1)}, bf16[128,1152]{1,0:T(8,128)(2,1)S(1)}, u32[]{:S(2)}, u32[]{:S(2)}) collective-permute-start(bf16[128,1152]{1,0:T(8,128)(2,1)} %get-tuple-element.29.rest_0_), channel_id=1, source_target_pairs={{0,8},{2,10},{4,0},{6,2},{8,16},{10,18},{12,4},{14,6},{16,24},{18,... | collective-permute-start | bytes 884744 | tf_op jit(solution)/shard_map/ppermute | solution.py:57
  7.2 8.4 %collective-permute-start = (bf16[128,1152]{1,0:T(8,128)(2,1)}, bf16[128,1152]{1,0:T(8,128)(2,1)S(1)}, u32[]{:S(2)}, u32[]{:S(2)}) collective-permute-start(bf16[128,1152]{1,0:T(8,128)(2,1)} %get-tuple-element.29.rest_0_), channel_id=1, source_target_pairs={{0,4},{2,6},{4,12},{6,14},{8,0},{10,2},{12,20},{14,22},{16,8},{18,... | collective-permute-start | bytes 884744 | tf_op jit(solution)/shard_map/ppermute | solution.py:57
  7.7 39.3 %copy-start.1 = (s32[512,8]{1,0:T(8,128)S(1)}, s32[512,8]{1,0:T(8,128)}, u32[]{:S(2)}) copy-start(s32[512,8]{1,0:T(8,128)} %get-tuple-element.27.cols) | copy-start | bytes 49156
  7.7 39.3 %copy-start.2 = (bf16[128,1152]{1,0:T(8,128)(2,1)S(1)}, bf16[128,1152]{1,0:T(8,128)(2,1)}, u32[]{:S(2)}) copy-start(bf16[128,1152]{1,0:T(8,128)(2,1)} %get-tuple-element.29.rest_0_) | copy-start | bytes 884740
  15.6 7.9 %collective-permute-start.3 = (bf16[128,1152]{1,0:T(8,128)(2,1)S(1)}, bf16[128,1152]{1,0:T(8,128)(2,1)S(1)}, u32[]{:S(2)}, u32[]{:S(2)}) collective-permute-start(bf16[128,1152]{1,0:T(8,128)(2,1)S(1)} %collective-permute-done.rest_1_), channel_id=1, source_target_pairs={{0,4},{2,6},{4,12},{6,14},{8,0},{10,2},{12,20},{14,22},{16,8},{18,... | collective-permute-start | bytes 884744 | tf_op jit(solution)/shard_map/ppermute | solution.py:57
  17.1 8.8 %collective-permute-start.4 = (bf16[128,1152]{1,0:T(8,128)(2,1)S(1)}, bf16[128,1152]{1,0:T(8,128)(2,1)S(1)}, u32[]{:S(2)}, u32[]{:S(2)}) collective-permute-start(bf16[128,1152]{1,0:T(8,128)(2,1)S(1)} %collective-permute-done.1.rest_2_), channel_id=1, source_target_pairs={{0,8},{2,10},{4,0},{6,2},{8,16},{10,18},{12,4},{14,6},{16,24},{18,... | collective-permute-start | bytes 884744 | tf_op jit(solution)/shard_map/ppermute | solution.py:57
  23.5 7.0 %collective-permute-start.6 = (bf16[128,1152]{1,0:T(8,128)(2,1)S(1)}, bf16[128,1152]{1,0:T(8,128)(2,1)S(1)}, u32[]{:S(2)}, u32[]{:S(2)}) collective-permute-start(bf16[128,1152]{1,0:T(8,128)(2,1)S(1)} %collective-permute-done.3.rest_4_), channel_id=1, source_target_pairs={{0,4},{2,6},{4,12},{6,14},{8,0},{10,2},{12,20},{14,22},{16,8},{18,... | collective-permute-start | bytes 884744 | tf_op jit(solution)/shard_map/ppermute | solution.py:57
  25.0 9.9 %collective-permute-start.10 = (bf16[128,1152]{1,0:T(8,128)(2,1)S(1)}, bf16[128,1152]{1,0:T(8,128)(2,1)S(1)}, u32[]{:S(2)}, u32[]{:S(2)}) collective-permute-start(bf16[128,1152]{1,0:T(8,128)(2,1)S(1)} %collective-permute-done.2.rest_3_), channel_id=1, source_target_pairs={{0,8},{2,10},{4,0},{6,2},{8,16},{10,18},{12,4},{14,6},{16,24},{18,... | collective-permute-start | bytes 884744 | tf_op jit(solution)/shard_map/ppermute | solution.py:57
  25.5 11.0 %collective-permute-start.5 = (bf16[128,1152]{1,0:T(8,128)(2,1)S(1)}, bf16[128,1152]{1,0:T(8,128)(2,1)S(1)}, u32[]{:S(2)}, u32[]{:S(2)}) collective-permute-start(bf16[128,1152]{1,0:T(8,128)(2,1)S(1)} %collective-permute-done.rest_1_), channel_id=1, source_target_pairs={{0,2},{2,0},{4,6},{6,4},{8,10},{10,8},{12,14},{14,12},{16,18},{18,... | collective-permute-start | bytes 884744 | tf_op jit(solution)/shard_map/ppermute | solution.py:57
  26.0 15.3 %collective-permute-start.7 = (bf16[128,1152]{1,0:T(8,128)(2,1)S(1)}, bf16[128,1152]{1,0:T(8,128)(2,1)S(1)}, u32[]{:S(2)}, u32[]{:S(2)}) collective-permute-start(bf16[128,1152]{1,0:T(8,128)(2,1)S(1)} %collective-permute-done.4.rest_5_), channel_id=1, source_target_pairs={{0,8},{2,10},{4,0},{6,2},{8,16},{10,18},{12,4},{14,6},{16,24},{18,... | collective-permute-start | bytes 884744 | tf_op jit(solution)/shard_map/ppermute | solution.py:57
  30.5 11.3 %collective-permute-start.11 = (bf16[128,1152]{1,0:T(8,128)(2,1)S(1)}, bf16[128,1152]{1,0:T(8,128)(2,1)S(1)}, u32[]{:S(2)}, u32[]{:S(2)}) collective-permute-start(bf16[128,1152]{1,0:T(8,128)(2,1)S(1)} %collective-permute-done.6.rest_7_), channel_id=1, source_target_pairs={{0,2},{2,0},{4,6},{6,4},{8,10},{10,8},{12,14},{14,12},{16,18},{18,... | collective-permute-start | bytes 884744 | tf_op jit(solution)/shard_map/ppermute | solution.py:57
  31.5 15.4 %collective-permute-start.8 = (bf16[128,1152]{1,0:T(8,128)(2,1)S(1)}, bf16[128,1152]{1,0:T(8,128)(2,1)S(1)}, u32[]{:S(2)}, u32[]{:S(2)}) collective-permute-start(bf16[128,1152]{1,0:T(8,128)(2,1)S(1)} %collective-permute-done.3.rest_4_), channel_id=1, source_target_pairs={{0,2},{2,0},{4,6},{6,4},{8,10},{10,8},{12,14},{14,12},{16,18},{18,... | collective-permute-start | bytes 884744 | tf_op jit(solution)/shard_map/ppermute | solution.py:57
  35.0 12.0 %collective-permute-start.9 = (bf16[128,1152]{1,0:T(8,128)(2,1)S(1)}, bf16[128,1152]{1,0:T(8,128)(2,1)S(1)}, u32[]{:S(2)}, u32[]{:S(2)}) collective-permute-start(bf16[128,1152]{1,0:T(8,128)(2,1)S(1)} %collective-permute-done.6.rest_7_), channel_id=1, source_target_pairs={{0,4},{2,6},{4,12},{6,14},{8,0},{10,2},{12,20},{14,22},{16,8},{18,... | collective-permute-start | bytes 884744 | tf_op jit(solution)/shard_map/ppermute | solution.py:57
  36.5 15.3 %collective-permute-start.13 = (bf16[128,1152]{1,0:T(8,128)(2,1)S(1)}, bf16[128,1152]{1,0:T(8,128)(2,1)S(1)}, u32[]{:S(2)}, u32[]{:S(2)}) collective-permute-start(bf16[128,1152]{1,0:T(8,128)(2,1)S(1)} %collective-permute-done.10.rest_11_), channel_id=1, source_target_pairs={{0,8},{2,10},{4,0},{6,2},{8,16},{10,18},{12,4},{14,6},{16,24},{18,... | collective-permute-start | bytes 884744 | tf_op jit(solution)/shard_map/ppermute | solution.py:57
  41.2 10.7 %collective-permute-start.14 = (bf16[128,1152]{1,0:T(8,128)(2,1)S(1)}, bf16[128,1152]{1,0:T(8,128)(2,1)S(1)}, u32[]{:S(2)}, u32[]{:S(2)}) collective-permute-start(bf16[128,1152]{1,0:T(8,128)(2,1)S(1)} %collective-permute-done.7.rest_8_), channel_id=1, source_target_pairs={{0,2},{2,0},{4,6},{6,4},{8,10},{10,8},{12,14},{14,12},{16,18},{18,... | collective-permute-start | bytes 884744 | tf_op jit(solution)/shard_map/ppermute | solution.py:57
  41.8 10.2 %collective-permute-start.12 = (bf16[128,1152]{1,0:T(8,128)(2,1)S(1)}, bf16[128,1152]{1,0:T(8,128)(2,1)S(1)}, u32[]{:S(2)}, u32[]{:S(2)}) collective-permute-start(bf16[128,1152]{1,0:T(8,128)(2,1)S(1)} %collective-permute-done.11.rest_12_), channel_id=1, source_target_pairs={{0,4},{2,6},{4,12},{6,14},{8,0},{10,2},{12,20},{14,22},{16,8},{18,... | collective-permute-start | bytes 884744 | tf_op jit(solution)/shard_map/ppermute | solution.py:57
  46.9 7.4 %collective-permute-start.16 = (bf16[512,1152]{1,0:T(8,128)(2,1)}, bf16[512,1152]{1,0:T(8,128)(2,1)S(1)}, u32[]{:S(2)}, u32[]{:S(2)}) collective-permute-start(bf16[512,1152]{1,0:T(8,128)(2,1)} %relation_rows.1.relation), channel_id=1, source_target_pairs={{0,1},{1,0},{2,3},{3,2},{4,5},{5,4},{6,7},{7,6},{8,9},{9,8},{10,11... | collective-permute-start | bytes 3538952 | tf_op jit(solution)/shard_map/ppermute | solution.py:70
  51.9 4.9 %copy-start = (bf16[512,1152]{1,0:T(8,128)(2,1)S(1)}, bf16[512,1152]{1,0:T(8,128)(2,1)}, u32[]{:S(2)}) copy-start(bf16[512,1152]{1,0:T(8,128)(2,1)} %relation_rows.1.relation) | copy-start | bytes 3538948
  53.8 3.0 %collective-permute-start.15 = (bf16[512,1152]{1,0:T(8,128)(2,1)S(1)}, bf16[512,1152]{1,0:T(8,128)(2,1)S(1)}, u32[]{:S(2)}, u32[]{:S(2)}) collective-permute-start(bf16[512,1152]{1,0:T(8,128)(2,1)S(1)} %anchor_rows.3.mine), channel_id=1, source_target_pairs={{0,1},{1,0},{2,3},{3,2},{4,5},{5,4},{6,7},{7,6},{8,9},{9,8},{10,11... | collective-permute-start | bytes 3538952 | tf_op jit(solution)/shard_map/ppermute | solution.py:70
  63.2 1.3 %collective-permute-start.17 = (f32[8,512]{1,0:T(8,128)S(1)}, f32[8,512]{1,0:T(8,128)S(1)}, u32[]{:S(2)}, u32[]{:S(2)}) collective-permute-start(f32[8,512]{1,0:T(8,128)S(1)} %get-tuple-element.37.mine), channel_id=1, source_target_pairs={{0,1},{1,0},{2,3},{3,2},{4,5},{5,4},{6,7},{7,6},{8,9},{9,8},{10,11... | collective-permute-start | bytes 49160 | tf_op jit(solution)/shard_map/ppermute | solution.py:70
  67.4 3.9 %collective-permute-start.21 = (f32[512,128]{1,0:T(8,128)S(1)}, f32[512,128]{1,0:T(8,128)S(1)}, u32[]{:S(2)}, u32[]{:S(2)}) collective-permute-start(f32[512,128]{1,0:T(8,128)S(1)} %get-tuple-element.44), channel_id=1, source_target_pairs={{0,1},{1,0},{2,3},{3,2},{4,5},{5,4},{6,7},{7,6},{8,9},{9,8},{10,11... | collective-permute-start | bytes 786440 | tf_op jit(solution)/shard_map/ppermute | solution.py:70
  67.8 7.2 %collective-permute-start.20 = (bf16[4,128,128]{2,1,0:T(8,128)(2,1)S(1)}, bf16[4,128,128]{2,1,0:T(8,128)(2,1)S(1)}, u32[]{:S(2)}, u32[]{:S(2)}) collective-permute-start(bf16[4,128,128]{2,1,0:T(8,128)(2,1)S(1)} %get-tuple-element.43), channel_id=1, source_target_pairs={{0,6},{2,4},{4,2},{6,0},{8,14},{10,12},{12,10},{14,8},{16,22},{18,... | collective-permute-start | bytes 393224 | tf_op jit(solution)/shard_map/ppermute | solution.py:402
  69.3 7.8 %collective-permute-start.18 = (bf16[4,128,128]{2,1,0:T(8,128)(2,1)S(1)}, bf16[4,128,128]{2,1,0:T(8,128)(2,1)S(1)}, u32[]{:S(2)}, u32[]{:S(2)}) collective-permute-start(bf16[4,128,128]{2,1,0:T(8,128)(2,1)S(1)} %get-tuple-element.41), channel_id=1, source_target_pairs={{0,2},{2,0},{4,6},{6,4},{8,10},{10,8},{12,14},{14,12},{16,18},{18,... | collective-permute-start | bytes 393224 | tf_op jit(solution)/shard_map/ppermute | solution.py:402
  70.8 6.4 %collective-permute-start.19 = (bf16[4,128,128]{2,1,0:T(8,128)(2,1)S(1)}, bf16[4,128,128]{2,1,0:T(8,128)(2,1)S(1)}, u32[]{:S(2)}, u32[]{:S(2)}) collective-permute-start(bf16[4,128,128]{2,1,0:T(8,128)(2,1)S(1)} %get-tuple-element.42), channel_id=1, source_target_pairs={{0,4},{2,6},{4,0},{6,2},{8,12},{10,14},{12,8},{14,10},{16,20},{18,... | collective-permute-start | bytes 393224 | tf_op jit(solution)/shard_map/ppermute | solution.py:402
  77.2 6.1 %collective-permute-start.22 = (bf16[128,128]{1,0:T(8,128)(2,1)S(1)}, bf16[128,128]{1,0:T(8,128)(2,1)S(1)}, u32[]{:S(2)}, u32[]{:S(2)}) collective-permute-start(bf16[128,128]{1,0:T(8,128)(2,1)S(1)} %get-tuple-element.47), channel_id=1, source_target_pairs={{0,8},{2,10},{4,12},{6,14},{8,16},{10,18},{12,20},{14,22},{16,24},... | collective-permute-start | bytes 98312 | tf_op jit(solution)/shard_map/ppermute | solution.py:408
  78.8 5.2 %collective-permute-start.23 = (bf16[128,128]{1,0:T(8,128)(2,1)S(1)}, bf16[128,128]{1,0:T(8,128)(2,1)S(1)}, u32[]{:S(2)}, u32[]{:S(2)}) collective-permute-start(bf16[128,128]{1,0:T(8,128)(2,1)S(1)} %get-tuple-element.48), channel_id=1, source_target_pairs={{0,16},{2,18},{4,20},{6,22},{8,24},{10,26},{12,28},{14,30},{16,0},... | collective-permute-start | bytes 98312 | tf_op jit(solution)/shard_map/ppermute | solution.py:408
  81.4 3.9 %collective-permute-start.24 = (bf16[128,128]{1,0:T(8,128)(2,1)S(1)}, bf16[128,128]{1,0:T(8,128)(2,1)S(1)}, u32[]{:S(2)}, u32[]{:S(2)}) collective-permute-start(bf16[128,128]{1,0:T(8,128)(2,1)S(1)} %get-tuple-element.49), channel_id=1, source_target_pairs={{0,24},{2,26},{4,28},{6,30},{8,0},{10,2},{12,4},{14,6},{16,8},{18,... | collective-permute-start | bytes 98312 | tf_op jit(solution)/shard_map/ppermute | solution.py:408

commit v2 on v1

--- a/solution.py
+++ b/solution.py
@@ -108,66 +108,45 @@
     )(teacher.T, student, *[x[None] for x in ids])
 
 
-def relation_kernel(shape, rel, block, base, cols, table_t, student, out, acc, acc_s):
-    step = pl.program_id(0)
-    start = (base[0] + step) * block
+def relation_kernel(shape, rel, block, cut, base, cols, table_t, student, out):
+    start = base[0] * block
     ids = cols[:, 1:2] - start
     hot = (ids == lax.broadcasted_iota(jnp.int32, (cols.shape[0], block), 1)).astype(F32).astype(BF16)
-
-    def add(table, small):
-        part = lax.dot_general(hot, table, (((1,), (1,)), ((), ())), preferred_element_type=F32)
-        part_s = jnp.dot(hot, small, preferred_element_type=F32)
-
-        @pl.when(step == 0)
-        def _():
-            acc[...] = part
-            acc_s[...] = part_s
-
-        @pl.when(step > 0)
-        def _():
-            acc[...] += part
-            acc_s[...] += part_s
-
-    @pl.when(start + block <= rel)
-    def _():
-        add(table_t[...], student[...])
-
-    @pl.when(start + block > rel)
-    def _():
-        lanes = lax.broadcasted_iota(jnp.int32, table_t.shape, 1)
-        rows = lax.broadcasted_iota(jnp.int32, student.shape, 0)
-        add(
-            jnp.where(lanes < rel - start, table_t[...], jnp.zeros_like(table_t)),
-            jnp.where(rows < rel - start, student[...], jnp.zeros_like(student)),
-        )
-
-    @pl.when(step == pl.num_programs(0) - 1)
-    def _():
-        put_row(out, acc_s[...], acc[...], shape)
-
-
-def relation_rows(base, cols, table, student, count, block, shape):
+    tail = block - cut
+    lanes = lax.broadcasted_iota(jnp.int32, (shape.tw, tail), 1) + cut
+    rows = lax.broadcasted_iota(jnp.int32, (tail, shape.sw), 0) + cut
+    table = jnp.where(lanes < rel - start, table_t[:, cut:], jnp.zeros((shape.tw, tail), BF16))
+    small = jnp.where(rows < rel - start, student[cut:, :], jnp.zeros((tail, shape.sw), BF16))
+    dims = (((1,), (1,)), ((), ()))
+    found = lax.dot_general(hot[:, cut:], table, dims, preferred_element_type=F32)
+    found_s = jnp.dot(hot[:, cut:], small, preferred_element_type=F32)
+    if cut:
+        found += lax.dot_general(hot[:, :cut], table_t[:, :cut], dims, preferred_element_type=F32)
+        found_s += jnp.dot(hot[:, :cut], student[:cut, :], preferred_element_type=F32)
+    put_row(out, found_s, found, shape)
+
+
+def relation_rows(base, cols, table, student, block, shape):
     rel, tw = table.shape
     q = cols.shape[0]
-    final = -(-rel // block) - 1
+    cut = max(0, rel - rel // block * block) // 128 * 128
     whole = lambda i, base: (0, 0)
     return pl.pallas_call(
-        functools.partial(relation_kernel, shape, rel, block),
+        functools.partial(relation_kernel, shape, rel, block, cut),
         out_shape=jax.ShapeDtypeStruct((q, shape.total), BF16),
         grid_spec=pltpu.PrefetchScalarGridSpec(
             num_scalar_prefetch=1,
-            grid=(count,),
+            grid=(1,),
             in_specs=[
                 pl.BlockSpec((q, cols.shape[1]), whole),
-                pl.BlockSpec((tw, block), lambda i, base: (0, jnp.minimum(base[0] + i, final))),
-                pl.BlockSpec((block, shape.sw), lambda i, base: (jnp.minimum(base[0] + i, final), 0)),
+                pl.BlockSpec((tw, block), lambda i, base: (0, base[0])),
+                pl.BlockSpec((block, shape.sw), lambda i, base: (base[0], 0)),
             ],
             out_specs=pl.BlockSpec((q, shape.total), whole),
-            scratch_shapes=[pltpu.VMEM((q, tw), F32), pltpu.VMEM((q, shape.sw), F32)],
         ),
         compiler_params=pltpu.CompilerParams(vmem_limit_bytes=56 * MIB),
         cost_estimate=pl.CostEstimate(
-            flops=2 * q * tw * block * count, bytes_accessed=2 * tw * block * count, transcendentals=0
+            flops=2 * q * tw * block, bytes_accessed=2 * tw * block, transcendentals=0
         ),
         name="relation_rows",
     )(base, cols, table.T, student)
@@ -434,22 +413,31 @@
             teacher_entities, student_entities, (anchor_ids, relation_ids, side_flags), shape
         )
         have = {(0, 0): packed}
-        block = 768
-        per_core = -(-teacher_relations.shape[0] // (2 * block))
-        base = (lax.axis_index("entity") % 2 * per_core).astype(jnp.int32)[None]
+        block = -(-teacher_relations.shape[0] // 512) * 256
+        base = (lax.axis_index("entity") % 2).astype(jnp.int32)[None]
         own_key = (0, 0)
         have[own_key], base = lax.optimization_barrier((have[own_key], base))
         anchors, counted = None, 0
+        kept, last = {}, {}
         for number, step in enumerate(steps):
-            got = {new: move(have[old], place, shift) for shift, old, new in step}
+            got = {}
+            for shift, old, new in step:
+                operand = have[old]
+                if shift in last and last[shift] != old:
+                    before = last[shift]
+                    operand, kept[before] = lax.optimization_barrier((operand, have[before]))
+                got[new] = move(operand, place, shift)
+                last[shift] = new
             if number == 0:
-                relation = relation_rows(base, cols, teacher_relations, student_relations, per_core, block, shape)
+                relation = relation_rows(base, cols, teacher_relations, student_relations, block, shape)
                 got, relation = lax.optimization_barrier((got, relation))
                 relation_b = partner(relation, groups, 1)
             if number == len(steps) - 1:
                 counted = len(have)
-                anchors = anchor_rows(bases, cols, [have[h] for h in held[:counted]], None, shape)
+                names = held[:counted]
+                anchors = anchor_rows(bases, cols, [kept.get(h, have[h]) for h in names], None, shape)
             have.update(got)
+        have.update(kept)
         shards = [have[h] for h in held]
         mine = anchor_rows(bases[counted:], cols, shards[counted:], anchors, shape)
         far = 1

time: 86.2 us -> 84.6 us (0.981)
  starting transfers between devices: 27.8 us -> 25.4 us
  waiting for transfers between devices: 29.2 us -> 31 us
  Pallas kernels: 26.1 us -> 25.1 us
    ppermute x15, starting transfers between devices: 17.3 us -> 15.1 us  [move(): return lax.ppermute(x, 'query', sorted(pairs))]
    ppermute x15, waiting for transfers between devices: 18.3 us -> 20.1 us  [move(): return lax.ppermute(x, 'query', sorted(pairs))]
    pallas_call x1, Pallas kernels: 7.86 us -> 6.93 us  [relation_rows(): pl.pallas_call(functools.partial(relation_kernel, shape, rel, block, cut)...]
  transfers between devices with their start and end apart: 25 -> 25, of which waited for: 13 -> 14; matrix products, arithmetic and copies ran while one was open for 2% -> 2% of each run, Pallas kernels for 17% -> 16%
where the time goes in v2:
time: 84.6 us; the launch traced here: 84.4 us
  waiting for transfers between devices  31 us (37%)
  starting transfers between devices  25.4 us (30%)
  Pallas kernels  25.1 us (30%)
  other arithmetic  1.38 us (2%)
    ppermute x15, waiting for transfers between devices, move(): return lax.ppermute(x, 'query', sorted(pairs))  20.1 us
    ppermute x15, starting transfers between devices, move(): return lax.ppermute(x, 'query', sorted(pairs))  15.1 us
    pallas_call x1, Pallas kernels, relation_rows(): pl.pallas_call(functools.partial(relation_kernel, shape, rel, block, cut)...  6.93 us
    pallas_call x2, Pallas kernels, anchor_rows(): pl.pallas_call(functools.partial(anchor_kernel, count, own, acc is not No...  6.76 us
    pallas_call x1, Pallas kernels, scores(): pl.pallas_call(functools.partial(score_kernel, shape, own, n, chunk), out...  6.38 us
    ppermute x3, starting transfers between devices, reduce_blocks(): total = total + lax.ppermute(sums[e], 'query', pairs).astype(F32)  5.51 us
    ppermute x3, waiting for transfers between devices, reduce_blocks(): lax.ppermute(blocks[d], 'query', [(i, i ^ d) for i in range(n)])  5.05 us
    ppermute x3, starting transfers between devices, reduce_blocks(): lax.ppermute(blocks[d], 'query', [(i, i ^ d) for i in range(n)])  3.49 us
  transfers between devices with their start and end apart: 25, of which 14 were waited for; matrix products, arithmetic and copies ran while one was open for 2% of the time, Pallas kernels for 16%

profile of v2, /device:TPU:0, one launch (start us, length us, event | category | flops | bytes accessed | tf_op | source)
XLA Modules:
  0.0 84.4 jit_solution(4267015329111072712)
XLA Ops:
  0.6 2.0 %pack_rows.1 = (bf16[128,1152]{1,0:T(8,128)(2,1)}, s32[512,8]{1,0:T(8,128)}) custom-call(bf16[1000,128]{1,0:T(8,128)(2,1)} %bitcast.14, bf16[128,128]{1,0:T(8,128)(2,1)} %student.2, s32[1,512]{1,0:T(1,128)} %bitcast.15, s32[1,512]{1,0:T(1,128)} %bitcast.16, s32[1,512]{1,0:T(1,128)} %bitcast.17), custom_call_target="tpu_custom_call" | custom-call | tf_op jit(solution)/shard_map/pack_rows/pallas_call | solution.py:98
  2.7 2.9 %collective-permute-start.2 = (bf16[128,1152]{1,0:T(8,128)(2,1)}, bf16[128,1152]{1,0:T(8,128)(2,1)S(1)}, u32[]{:S(2)}, u32[]{:S(2)}) collective-permute-start(bf16[128,1152]{1,0:T(8,128)(2,1)} %get-tuple-element.41.rest_0_), channel_id=1, source_target_pairs={{0,2},{2,0},{4,6},{6,4},{8,10},{10,8},{12,14},{14,12},{16,18},{18,... | collective-permute-start | bytes 884744 | tf_op jit(solution)/shard_map/ppermute | solution.py:57
  5.6 1.6 %collective-permute-start.1 = (bf16[128,1152]{1,0:T(8,128)(2,1)}, bf16[128,1152]{1,0:T(8,128)(2,1)S(1)}, u32[]{:S(2)}, u32[]{:S(2)}) collective-permute-start(bf16[128,1152]{1,0:T(8,128)(2,1)} %get-tuple-element.41.rest_0_), channel_id=1, source_target_pairs={{0,8},{2,10},{4,0},{6,2},{8,16},{10,18},{12,4},{14,6},{16,24},{18,... | collective-permute-start | bytes 884744 | tf_op jit(solution)/shard_map/ppermute | solution.py:57
  7.7 6.9 %relation_rows.1.relation = bf16[512,1152]{1,0:T(8,128)(2,1)} custom-call(s32[1]{0:T(128)} %bitcast.7.base, s32[512,8]{1,0:T(8,128)} %get-tuple-element.39.cols, bf16[1000,4131]{1,0:T(8,128)(2,1)} %bitcast.13, bf16[4131,128]{1,0:T(8,128)(2,1)} %student.3), custom_call_target="tpu_custom_call" | custom-call | flops 2359296000 | bytes 4608000 | tf_op jit(solution)/shard_map/relation_rows/pallas_call | solution.py:134
  14.6 1.0 %collective-permute-done.rest_1_ = bf16[128,1152]{1,0:T(8,128)(2,1)S(1)} collective-permute-done((bf16[128,1152]{1,0:T(8,128)(2,1)}, bf16[128,1152]{1,0:T(8,128)(2,1)S(1)}, u32[]{:S(2)}, u32[]{:S(2)}) %collective-permute-start) | collective-permute-done | bytes 294944 | tf_op jit(solution)/shard_map/ppermute | solution.py:57
  15.6 1.6 %collective-permute-start.4 = (bf16[128,1152]{1,0:T(8,128)(2,1)S(1)}, bf16[128,1152]{1,0:T(8,128)(2,1)S(1)}, u32[]{:S(2)}, u32[]{:S(2)}) collective-permute-start(bf16[128,1152]{1,0:T(8,128)(2,1)S(1)} %collective-permute-done.1.rest_2_), channel_id=1, source_target_pairs={{0,8},{2,10},{4,0},{6,2},{8,16},{10,18},{12,4},{14,6},{16,24},{18,... | collective-permute-start | bytes 884744 | tf_op jit(solution)/shard_map/ppermute | solution.py:57
  18.2 4.7 %collective-permute-done.4.rest_5_ = bf16[128,1152]{1,0:T(8,128)(2,1)S(1)} collective-permute-done((bf16[128,1152]{1,0:T(8,128)(2,1)S(1)}, bf16[128,1152]{1,0:T(8,128)(2,1)S(1)}, u32[]{:S(2)}, u32[]{:S(2)}) %collective-permute-start.4) | collective-permute-done | bytes 294944 | tf_op jit(solution)/shard_map/ppermute | solution.py:57
  22.9 1.6 %collective-permute-start.7 = (bf16[128,1152]{1,0:T(8,128)(2,1)S(1)}, bf16[128,1152]{1,0:T(8,128)(2,1)S(1)}, u32[]{:S(2)}, u32[]{:S(2)}) collective-permute-start(bf16[128,1152]{1,0:T(8,128)(2,1)S(1)} %collective-permute-done.4.rest_5_), channel_id=1, source_target_pairs={{0,8},{2,10},{4,0},{6,2},{8,16},{10,18},{12,4},{14,6},{16,24},{18,... | collective-permute-start | bytes 884744 | tf_op jit(solution)/shard_map/ppermute | solution.py:57
  24.4 1.5 %collective-permute-start.8 = (bf16[128,1152]{1,0:T(8,128)(2,1)S(1)}, bf16[128,1152]{1,0:T(8,128)(2,1)S(1)}, u32[]{:S(2)}, u32[]{:S(2)}) collective-permute-start(bf16[128,1152]{1,0:T(8,128)(2,1)S(1)} %collective-permute-done.3.rest_4_), channel_id=1, source_target_pairs={{0,2},{2,0},{4,6},{6,4},{8,10},{10,8},{12,14},{14,12},{16,18},{18,... | collective-permute-start | bytes 884744 | tf_op jit(solution)/shard_map/ppermute | solution.py:57
  26.4 4.3 %collective-permute-done.7.rest_8_ = bf16[128,1152]{1,0:T(8,128)(2,1)S(1)} collective-permute-done((bf16[128,1152]{1,0:T(8,128)(2,1)S(1)}, bf16[128,1152]{1,0:T(8,128)(2,1)S(1)}, u32[]{:S(2)}, u32[]{:S(2)}) %collective-permute-start.7) | collective-permute-done | bytes 294944 | tf_op jit(solution)/shard_map/ppermute | solution.py:57
  30.6 1.6 %collective-permute-start.11 = (bf16[128,1152]{1,0:T(8,128)(2,1)S(1)}, bf16[128,1152]{1,0:T(8,128)(2,1)S(1)}, u32[]{:S(2)}, u32[]{:S(2)}) collective-permute-start(bf16[128,1152]{1,0:T(8,128)(2,1)S(1)} %collective-permute-done.2.rest_3_), channel_id=1, source_target_pairs={{0,8},{2,10},{4,0},{6,2},{8,16},{10,18},{12,4},{14,6},{16,24},{18,... | collective-permute-start | bytes 884744 | tf_op jit(solution)/shard_map/ppermute | solution.py:57
  32.2 1.5 %collective-permute-done.6.rest_7_ = bf16[128,1152]{1,0:T(8,128)(2,1)S(1)} collective-permute-done((bf16[128,1152]{1,0:T(8,128)(2,1)S(1)}, bf16[128,1152]{1,0:T(8,128)(2,1)S(1)}, u32[]{:S(2)}, u32[]{:S(2)}) %collective-permute-start.6) | collective-permute-done | bytes 294944 | tf_op jit(solution)/shard_map/ppermute | solution.py:57
  34.2 0.7 constant_dynamic-slice_fusion
  34.9 8.5 %collective-permute-done.9.rest_12_ = bf16[128,1152]{1,0:T(8,128)(2,1)S(1)} collective-permute-done((bf16[128,1152]{1,0:T(8,128)(2,1)S(1)}, bf16[128,1152]{1,0:T(8,128)(2,1)S(1)}, u32[]{:S(2)}, u32[]{:S(2)}) %collective-permute-start.9) | collective-permute-done | bytes 294944 | tf_op jit(solution)/shard_map/ppermute | solution.py:57
  43.8 1.6 %collective-permute-start.13 = (bf16[128,1152]{1,0:T(8,128)(2,1)S(1)}, bf16[128,1152]{1,0:T(8,128)(2,1)S(1)}, u32[]{:S(2)}, u32[]{:S(2)}) collective-permute-start(bf16[128,1152]{1,0:T(8,128)(2,1)S(1)} %collective-permute-done.11.rest_11_), channel_id=1, source_target_pairs={{0,8},{2,10},{4,0},{6,2},{8,16},{10,18},{12,4},{14,6},{16,24},{18,... | collective-permute-start | bytes 884744 | tf_op jit(solution)/shard_map/ppermute | solution.py:57
  45.5 4.9 %anchor_rows.2.rest_0_ = bf16[512,1152]{1,0:T(8,128)(2,1)S(1)} custom-call(s32[16]{0:T(128)S(1)} %bitcast.12, s32[512,8]{1,0:T(8,128)S(1)} %copy-done.1, bf16[128,1152]{1,0:T(8,128)(2,1)S(1)} %copy-done.2, bf16[128,1152]{1,0:T(8,128)(2,1)S(1)} %collective-permute-done.rest_1_, bf16[128,1152]{1,0:T(8,128)(2,1)S(1)} %collective-permute-done.1.rest_2_, ...), custom_call_target="tpu_custom_call" | custom-call | flops 1962934272 | bytes 6193152 | tf_op jit(solution)/shard_map/anchor_rows/pallas_call | solution.py:183
  50.6 1.8 %anchor_rows.3.mine = bf16[512,1152]{1,0:T(8,128)(2,1)S(1)} custom-call(s32[3]{0:T(128)S(1)} %slice_bitcast_fusion.bases, s32[512,8]{1,0:T(8,128)S(1)} %copy-done.1, bf16[512,1152]{1,0:T(8,128)(2,1)S(1)} %anchor_rows.2.rest_0_, bf16[128,1152]{1,0:T(8,128)(2,1)S(1)} %collective-permute-done.12.rest_1_.rest_13_, ...), custom_call_target="tpu_custom_call" | custom-call | flops 452984832 | bytes 3244032 | tf_op jit(solution)/shard_map/anchor_rows/pallas_call | solution.py:183
  52.9 2.5 %collective-permute-done.15.other = bf16[512,1152]{1,0:T(8,128)(2,1)S(1)} collective-permute-done((bf16[512,1152]{1,0:T(8,128)(2,1)S(1)}, bf16[512,1152]{1,0:T(8,128)(2,1)S(1)}, u32[]{:S(2)}, u32[]{:S(2)}) %collective-permute-start.15) | collective-permute-done | bytes 1179680 | tf_op jit(solution)/shard_map/ppermute | solution.py:70
  55.3 6.4 %scores.1 = (f32[2048,512]{1,0:T(8,128)S(1)}, f32[2048,512]{1,0:T(8,128)S(1)}, f32[8,512]{1,0:T(8,128)S(1)}, bf16[512,128]{1,0:T(8,128)(2,1)S(1)}) custom-call(bf16[512,1152]{1,0:T(8,128)(2,1)S(1)} %anchor_rows.3.mine, bf16[512,1152]{1,0:T(8,128)(2,1)S(1)} %collective-permute-done.15.other, bf16[512,1152]{1,0:T(8,128)(2,1)S(1)} %copy-done, ...), custom_call_target="tpu_custom_call" | custom-call | flops 2415919104 | bytes 13107200 | tf_op jit(solution)/shard_map/scores/pallas_call | solution.py:259
  62.2 0.8 collective-permute-done.17.other
  63.0 3.0 %gradients.1 = (f32[1,512]{1,0:T(1,128)}, f32[512,128]{1,0:T(8,128)S(1)}, bf16[4,128,128]{2,1,0:T(8,128)(2,1)S(1)}, bf16[4,128,128]{2,1,0:T(8,128)(2,1)S(1)}, bf...) custom-call(s32[16]{0:T(128)S(1)} %get-tuple-element.76.order, f32[2048,512]{1,0:T(8,128)S(1)} %get-tuple-element.59.t_in, ...), custom_call_target="tpu_custom_call" | custom-call | flops 536870912 | bytes 8388608 | tf_op jit(solution)/shard_map/gradients/pallas_call | solution.py:333
  66.4 1.9 %collective-permute-start.20 = (bf16[4,128,128]{2,1,0:T(8,128)(2,1)S(1)}, bf16[4,128,128]{2,1,0:T(8,128)(2,1)S(1)}, u32[]{:S(2)}, u32[]{:S(2)}) collective-permute-start(bf16[4,128,128]{2,1,0:T(8,128)(2,1)S(1)} %get-tuple-element.67), channel_id=1, source_target_pairs={{0,6},{2,4},{4,2},{6,0},{8,14},{10,12},{12,10},{14,8},{16,22},{18,... | collective-permute-start | bytes 393224 | tf_op jit(solution)/shard_map/ppermute | solution.py:381
  68.4 1.5 %collective-permute-start.19 = (bf16[4,128,128]{2,1,0:T(8,128)(2,1)S(1)}, bf16[4,128,128]{2,1,0:T(8,128)(2,1)S(1)}, u32[]{:S(2)}, u32[]{:S(2)}) collective-permute-start(bf16[4,128,128]{2,1,0:T(8,128)(2,1)S(1)} %get-tuple-element.66), channel_id=1, source_target_pairs={{0,4},{2,6},{4,0},{6,2},{8,12},{10,14},{12,8},{14,10},{16,20},{18,... | collective-permute-start | bytes 393224 | tf_op jit(solution)/shard_map/ppermute | solution.py:381
  69.9 0.7 add.30
  70.6 3.0 %collective-permute-done.20.refs_3_ = bf16[4,128,128]{2,1,0:T(8,128)(2,1)S(1)} collective-permute-done((bf16[4,128,128]{2,1,0:T(8,128)(2,1)S(1)}, bf16[4,128,128]{2,1,0:T(8,128)(2,1)S(1)}, u32[]{:S(2)}, u32[]{:S(2)}) %collective-permute-start.20) | collective-permute-done | bytes 131104 | tf_op jit(solution)/shard_map/ppermute | solution.py:381
  73.6 1.4 %collective-permute-done.18.refs_1_ = bf16[4,128,128]{2,1,0:T(8,128)(2,1)S(1)} collective-permute-done((bf16[4,128,128]{2,1,0:T(8,128)(2,1)S(1)}, bf16[4,128,128]{2,1,0:T(8,128)(2,1)S(1)}, u32[]{:S(2)}, u32[]{:S(2)}) %collective-permute-start.18) | collective-permute-done | bytes 131104 | tf_op jit(solution)/shard_map/ppermute | solution.py:381
  75.7 1.6 %collective-permute-start.22 = (bf16[128,128]{1,0:T(8,128)(2,1)S(1)}, bf16[128,128]{1,0:T(8,128)(2,1)S(1)}, u32[]{:S(2)}, u32[]{:S(2)}) collective-permute-start(bf16[128,128]{1,0:T(8,128)(2,1)S(1)} %get-tuple-element.71), channel_id=1, source_target_pairs={{0,8},{2,10},{4,12},{6,14},{8,16},{10,18},{12,20},{14,22},{16,24},... | collective-permute-start | bytes 98312 | tf_op jit(solution)/shard_map/ppermute | solution.py:387
  77.4 2.5 %collective-permute-start.23 = (bf16[128,128]{1,0:T(8,128)(2,1)S(1)}, bf16[128,128]{1,0:T(8,128)(2,1)S(1)}, u32[]{:S(2)}, u32[]{:S(2)}) collective-permute-start(bf16[128,128]{1,0:T(8,128)(2,1)S(1)} %get-tuple-element.72), channel_id=1, source_target_pairs={{0,16},{2,18},{4,20},{6,22},{8,24},{10,26},{12,28},{14,30},{16,0},... | collective-permute-start | bytes 98312 | tf_op jit(solution)/shard_map/ppermute | solution.py:387
  79.8 1.4 %collective-permute-start.24 = (bf16[128,128]{1,0:T(8,128)(2,1)S(1)}, bf16[128,128]{1,0:T(8,128)(2,1)S(1)}, u32[]{:S(2)}, u32[]{:S(2)}) collective-permute-start(bf16[128,128]{1,0:T(8,128)(2,1)S(1)} %get-tuple-element.73), channel_id=1, source_target_pairs={{0,24},{2,26},{4,28},{6,30},{8,0},{10,2},{12,4},{14,6},{16,8},{18,... | collective-permute-start | bytes 98312 | tf_op jit(solution)/shard_map/ppermute | solution.py:387
  81.5 1.1 %collective-permute-done.23 = bf16[128,128]{1,0:T(8,128)(2,1)S(1)} collective-permute-done((bf16[128,128]{1,0:T(8,128)(2,1)S(1)}, bf16[128,128]{1,0:T(8,128)(2,1)S(1)}, u32[]{:S(2)}, u32[]{:S(2)}) %collective-permute-start.23) | collective-permute-done | bytes 32800 | tf_op jit(solution)/shard_map/ppermute | solution.py:387
  82.6 1.1 %collective-permute-done.24 = bf16[128,128]{1,0:T(8,128)(2,1)S(1)} collective-permute-done((bf16[128,128]{1,0:T(8,128)(2,1)S(1)}, bf16[128,128]{1,0:T(8,128)(2,1)S(1)}, u32[]{:S(2)}, u32[]{:S(2)}) %collective-permute-start.24) | collective-permute-done | bytes 32800 | tf_op jit(solution)/shard_map/ppermute | solution.py:387
  83.8 0.6 convert_add_fusion
  (36 shorter events, 5.4 us)
Async XLA Ops:
  2.7 11.9 %collective-permute-start.2 = (bf16[128,1152]{1,0:T(8,128)(2,1)}, bf16[128,1152]{1,0:T(8,128)(2,1)S(1)}, u32[]{:S(2)}, u32[]{:S(2)}) collective-permute-start(bf16[128,1152]{1,0:T(8,128)(2,1)} %get-tuple-element.41.rest_0_), channel_id=1, source_target_pairs={{0,2},{2,0},{4,6},{6,4},{8,10},{10,8},{12,14},{14,12},{16,18},{18,... | collective-permute-start | bytes 884744 | tf_op jit(solution)/shard_map/ppermute | solution.py:57
  5.6 9.0 %collective-permute-start.1 = (bf16[128,1152]{1,0:T(8,128)(2,1)}, bf16[128,1152]{1,0:T(8,128)(2,1)S(1)}, u32[]{:S(2)}, u32[]{:S(2)}) collective-permute-start(bf16[128,1152]{1,0:T(8,128)(2,1)} %get-tuple-element.41.rest_0_), channel_id=1, source_target_pairs={{0,8},{2,10},{4,0},{6,2},{8,16},{10,18},{12,4},{14,6},{16,24},{18,... | collective-permute-start | bytes 884744 | tf_op jit(solution)/shard_map/ppermute | solution.py:57
  7.2 8.4 %collective-permute-start = (bf16[128,1152]{1,0:T(8,128)(2,1)}, bf16[128,1152]{1,0:T(8,128)(2,1)S(1)}, u32[]{:S(2)}, u32[]{:S(2)}) collective-permute-start(bf16[128,1152]{1,0:T(8,128)(2,1)} %get-tuple-element.41.rest_0_), channel_id=1, source_target_pairs={{0,4},{2,6},{4,12},{6,14},{8,0},{10,2},{12,20},{14,22},{16,8},{18,... | collective-permute-start | bytes 884744 | tf_op jit(solution)/shard_map/ppermute | solution.py:57
  7.7 37.8 %copy-start.1 = (s32[512,8]{1,0:T(8,128)S(1)}, s32[512,8]{1,0:T(8,128)}, u32[]{:S(2)}) copy-start(s32[512,8]{1,0:T(8,128)} %get-tuple-element.39.cols) | copy-start | bytes 49156
  7.7 37.8 %copy-start.2 = (bf16[128,1152]{1,0:T(8,128)(2,1)S(1)}, bf16[128,1152]{1,0:T(8,128)(2,1)}, u32[]{:S(2)}) copy-start(bf16[128,1152]{1,0:T(8,128)(2,1)} %get-tuple-element.41.rest_0_) | copy-start | bytes 884740
  15.6 7.3 %collective-permute-start.4 = (bf16[128,1152]{1,0:T(8,128)(2,1)S(1)}, bf16[128,1152]{1,0:T(8,128)(2,1)S(1)}, u32[]{:S(2)}, u32[]{:S(2)}) collective-permute-start(bf16[128,1152]{1,0:T(8,128)(2,1)S(1)} %collective-permute-done.1.rest_2_), channel_id=1, source_target_pairs={{0,8},{2,10},{4,0},{6,2},{8,16},{10,18},{12,4},{14,6},{16,24},{18,... | collective-permute-start | bytes 884744 | tf_op jit(solution)/shard_map/ppermute | solution.py:57
  17.2 7.3 %collective-permute-start.5 = (bf16[128,1152]{1,0:T(8,128)(2,1)S(1)}, bf16[128,1152]{1,0:T(8,128)(2,1)S(1)}, u32[]{:S(2)}, u32[]{:S(2)}) collective-permute-start(bf16[128,1152]{1,0:T(8,128)(2,1)S(1)} %collective-permute-done.rest_1_), channel_id=1, source_target_pairs={{0,2},{2,0},{4,6},{6,4},{8,10},{10,8},{12,14},{14,12},{16,18},{18,... | collective-permute-start | bytes 884744 | tf_op jit(solution)/shard_map/ppermute | solution.py:57
  17.7 6.7 %collective-permute-start.3 = (bf16[128,1152]{1,0:T(8,128)(2,1)S(1)}, bf16[128,1152]{1,0:T(8,128)(2,1)S(1)}, u32[]{:S(2)}, u32[]{:S(2)}) collective-permute-start(bf16[128,1152]{1,0:T(8,128)(2,1)S(1)} %collective-permute-done.rest_1_), channel_id=1, source_target_pairs={{0,4},{2,6},{4,12},{6,14},{8,0},{10,2},{12,20},{14,22},{16,8},{18,... | collective-permute-start | bytes 884744 | tf_op jit(solution)/shard_map/ppermute | solution.py:57
  22.9 7.8 %collective-permute-start.7 = (bf16[128,1152]{1,0:T(8,128)(2,1)S(1)}, bf16[128,1152]{1,0:T(8,128)(2,1)S(1)}, u32[]{:S(2)}, u32[]{:S(2)}) collective-permute-start(bf16[128,1152]{1,0:T(8,128)(2,1)S(1)} %collective-permute-done.4.rest_5_), channel_id=1, source_target_pairs={{0,8},{2,10},{4,0},{6,2},{8,16},{10,18},{12,4},{14,6},{16,24},{18,... | collective-permute-start | bytes 884744 | tf_op jit(solution)/shard_map/ppermute | solution.py:57
  24.4 7.8 %collective-permute-start.8 = (bf16[128,1152]{1,0:T(8,128)(2,1)S(1)}, bf16[128,1152]{1,0:T(8,128)(2,1)S(1)}, u32[]{:S(2)}, u32[]{:S(2)}) collective-permute-start(bf16[128,1152]{1,0:T(8,128)(2,1)S(1)} %collective-permute-done.3.rest_4_), channel_id=1, source_target_pairs={{0,2},{2,0},{4,6},{6,4},{8,10},{10,8},{12,14},{14,12},{16,18},{18,... | collective-permute-start | bytes 884744 | tf_op jit(solution)/shard_map/ppermute | solution.py:57
  25.9 7.8 %collective-permute-start.6 = (bf16[128,1152]{1,0:T(8,128)(2,1)S(1)}, bf16[128,1152]{1,0:T(8,128)(2,1)S(1)}, u32[]{:S(2)}, u32[]{:S(2)}) collective-permute-start(bf16[128,1152]{1,0:T(8,128)(2,1)S(1)} %collective-permute-done.3.rest_4_), channel_id=1, source_target_pairs={{0,4},{2,6},{4,12},{6,14},{8,0},{10,2},{12,20},{14,22},{16,8},{18,... | collective-permute-start | bytes 884744 | tf_op jit(solution)/shard_map/ppermute | solution.py:57
  30.6 13.2 %collective-permute-start.11 = (bf16[128,1152]{1,0:T(8,128)(2,1)S(1)}, bf16[128,1152]{1,0:T(8,128)(2,1)S(1)}, u32[]{:S(2)}, u32[]{:S(2)}) collective-permute-start(bf16[128,1152]{1,0:T(8,128)(2,1)S(1)} %collective-permute-done.2.rest_3_), channel_id=1, source_target_pairs={{0,8},{2,10},{4,0},{6,2},{8,16},{10,18},{12,4},{14,6},{16,24},{18,... | collective-permute-start | bytes 884744 | tf_op jit(solution)/shard_map/ppermute | solution.py:57
  33.7 9.6 %collective-permute-start.9 = (bf16[128,1152]{1,0:T(8,128)(2,1)S(1)}, bf16[128,1152]{1,0:T(8,128)(2,1)S(1)}, u32[]{:S(2)}, u32[]{:S(2)}) collective-permute-start(bf16[128,1152]{1,0:T(8,128)(2,1)S(1)} %collective-permute-done.6.rest_7_), channel_id=1, source_target_pairs={{0,2},{2,0},{4,6},{6,4},{8,10},{10,8},{12,14},{14,12},{16,18},{18,... | collective-permute-start | bytes 884744 | tf_op jit(solution)/shard_map/ppermute | solution.py:57
  33.7 9.7 %collective-permute-start.10 = (bf16[128,1152]{1,0:T(8,128)(2,1)S(1)}, bf16[128,1152]{1,0:T(8,128)(2,1)S(1)}, u32[]{:S(2)}, u32[]{:S(2)}) collective-permute-start(bf16[128,1152]{1,0:T(8,128)(2,1)S(1)} %collective-permute-done.6.rest_7_), channel_id=1, source_target_pairs={{0,4},{2,6},{4,12},{6,14},{8,0},{10,2},{12,20},{14,22},{16,8},{18,... | collective-permute-start | bytes 884744 | tf_op jit(solution)/shard_map/ppermute | solution.py:57
  43.4 7.2 %collective-permute-start.14 = (bf16[128,1152]{1,0:T(8,128)(2,1)S(1)}, bf16[128,1152]{1,0:T(8,128)(2,1)S(1)}, u32[]{:S(2)}, u32[]{:S(2)}) collective-permute-start(bf16[128,1152]{1,0:T(8,128)(2,1)S(1)} %collective-permute-done.7.rest_8_), channel_id=1, source_target_pairs={{0,2},{2,0},{4,6},{6,4},{8,10},{10,8},{12,14},{14,12},{16,18},{18,... | collective-permute-start | bytes 884744 | tf_op jit(solution)/shard_map/ppermute | solution.py:57
  43.4 7.2 %collective-permute-start.12 = (bf16[128,1152]{1,0:T(8,128)(2,1)S(1)}, bf16[128,1152]{1,0:T(8,128)(2,1)S(1)}, u32[]{:S(2)}, u32[]{:S(2)}) collective-permute-start(bf16[128,1152]{1,0:T(8,128)(2,1)S(1)} %collective-permute-done.9.rest_12_), channel_id=1, source_target_pairs={{0,4},{2,6},{4,12},{6,14},{8,0},{10,2},{12,20},{14,22},{16,8},{18,... | collective-permute-start | bytes 884744 | tf_op jit(solution)/shard_map/ppermute | solution.py:57
  43.8 6.7 %collective-permute-start.13 = (bf16[128,1152]{1,0:T(8,128)(2,1)S(1)}, bf16[128,1152]{1,0:T(8,128)(2,1)S(1)}, u32[]{:S(2)}, u32[]{:S(2)}) collective-permute-start(bf16[128,1152]{1,0:T(8,128)(2,1)S(1)} %collective-permute-done.11.rest_11_), channel_id=1, source_target_pairs={{0,8},{2,10},{4,0},{6,2},{8,16},{10,18},{12,4},{14,6},{16,24},{18,... | collective-permute-start | bytes 884744 | tf_op jit(solution)/shard_map/ppermute | solution.py:57
  45.5 7.4 %collective-permute-start.16 = (bf16[512,1152]{1,0:T(8,128)(2,1)}, bf16[512,1152]{1,0:T(8,128)(2,1)S(1)}, u32[]{:S(2)}, u32[]{:S(2)}) collective-permute-start(bf16[512,1152]{1,0:T(8,128)(2,1)} %relation_rows.1.relation), channel_id=1, source_target_pairs={{0,1},{1,0},{2,3},{3,2},{4,5},{5,4},{6,7},{7,6},{8,9},{9,8},{10,11... | collective-permute-start | bytes 3538952 | tf_op jit(solution)/shard_map/ppermute | solution.py:70
  50.4 4.9 %copy-start = (bf16[512,1152]{1,0:T(8,128)(2,1)S(1)}, bf16[512,1152]{1,0:T(8,128)(2,1)}, u32[]{:S(2)}) copy-start(bf16[512,1152]{1,0:T(8,128)(2,1)} %relation_rows.1.relation) | copy-start | bytes 3538948
  52.4 2.9 %collective-permute-start.15 = (bf16[512,1152]{1,0:T(8,128)(2,1)S(1)}, bf16[512,1152]{1,0:T(8,128)(2,1)S(1)}, u32[]{:S(2)}, u32[]{:S(2)}) collective-permute-start(bf16[512,1152]{1,0:T(8,128)(2,1)S(1)} %anchor_rows.3.mine), channel_id=1, source_target_pairs={{0,1},{1,0},{2,3},{3,2},{4,5},{5,4},{6,7},{7,6},{8,9},{9,8},{10,11... | collective-permute-start | bytes 3538952 | tf_op jit(solution)/shard_map/ppermute | solution.py:70
  61.7 1.3 %collective-permute-start.17 = (f32[8,512]{1,0:T(8,128)S(1)}, f32[8,512]{1,0:T(8,128)S(1)}, u32[]{:S(2)}, u32[]{:S(2)}) collective-permute-start(f32[8,512]{1,0:T(8,128)S(1)} %get-tuple-element.61.mine), channel_id=1, source_target_pairs={{0,1},{1,0},{2,3},{3,2},{4,5},{5,4},{6,7},{7,6},{8,9},{9,8},{10,11... | collective-permute-start | bytes 49160 | tf_op jit(solution)/shard_map/ppermute | solution.py:70
  66.0 3.9 %collective-permute-start.21 = (f32[512,128]{1,0:T(8,128)S(1)}, f32[512,128]{1,0:T(8,128)S(1)}, u32[]{:S(2)}, u32[]{:S(2)}) collective-permute-start(f32[512,128]{1,0:T(8,128)S(1)} %get-tuple-element.68), channel_id=1, source_target_pairs={{0,1},{1,0},{2,3},{3,2},{4,5},{5,4},{6,7},{7,6},{8,9},{9,8},{10,11... | collective-permute-start | bytes 786440 | tf_op jit(solution)/shard_map/ppermute | solution.py:70
  66.4 7.2 %collective-permute-start.20 = (bf16[4,128,128]{2,1,0:T(8,128)(2,1)S(1)}, bf16[4,128,128]{2,1,0:T(8,128)(2,1)S(1)}, u32[]{:S(2)}, u32[]{:S(2)}) collective-permute-start(bf16[4,128,128]{2,1,0:T(8,128)(2,1)S(1)} %get-tuple-element.67), channel_id=1, source_target_pairs={{0,6},{2,4},{4,2},{6,0},{8,14},{10,12},{12,10},{14,8},{16,22},{18,... | collective-permute-start | bytes 393224 | tf_op jit(solution)/shard_map/ppermute | solution.py:381
  68.3 6.7 %collective-permute-start.18 = (bf16[4,128,128]{2,1,0:T(8,128)(2,1)S(1)}, bf16[4,128,128]{2,1,0:T(8,128)(2,1)S(1)}, u32[]{:S(2)}, u32[]{:S(2)}) collective-permute-start(bf16[4,128,128]{2,1,0:T(8,128)(2,1)S(1)} %get-tuple-element.65), channel_id=1, source_target_pairs={{0,2},{2,0},{4,6},{6,4},{8,10},{10,8},{12,14},{14,12},{16,18},{18,... | collective-permute-start | bytes 393224 | tf_op jit(solution)/shard_map/ppermute | solution.py:381
  68.4 7.2 %collective-permute-start.19 = (bf16[4,128,128]{2,1,0:T(8,128)(2,1)S(1)}, bf16[4,128,128]{2,1,0:T(8,128)(2,1)S(1)}, u32[]{:S(2)}, u32[]{:S(2)}) collective-permute-start(bf16[4,128,128]{2,1,0:T(8,128)(2,1)S(1)} %get-tuple-element.66), channel_id=1, source_target_pairs={{0,4},{2,6},{4,0},{6,2},{8,12},{10,14},{12,8},{14,10},{16,20},{18,... | collective-permute-start | bytes 393224 | tf_op jit(solution)/shard_map/ppermute | solution.py:381
  75.7 5.8 %collective-permute-start.22 = (bf16[128,128]{1,0:T(8,128)(2,1)S(1)}, bf16[128,128]{1,0:T(8,128)(2,1)S(1)}, u32[]{:S(2)}, u32[]{:S(2)}) collective-permute-start(bf16[128,128]{1,0:T(8,128)(2,1)S(1)} %get-tuple-element.71), channel_id=1, source_target_pairs={{0,8},{2,10},{4,12},{6,14},{8,16},{10,18},{12,20},{14,22},{16,24},... | collective-permute-start | bytes 98312 | tf_op jit(solution)/shard_map/ppermute | solution.py:387
  77.4 5.2 %collective-permute-start.23 = (bf16[128,128]{1,0:T(8,128)(2,1)S(1)}, bf16[128,128]{1,0:T(8,128)(2,1)S(1)}, u32[]{:S(2)}, u32[]{:S(2)}) collective-permute-start(bf16[128,128]{1,0:T(8,128)(2,1)S(1)} %get-tuple-element.72), channel_id=1, source_target_pairs={{0,16},{2,18},{4,20},{6,22},{8,24},{10,26},{12,28},{14,30},{16,0},... | collective-permute-start | bytes 98312 | tf_op jit(solution)/shard_map/ppermute | solution.py:387
  79.8 3.9 %collective-permute-start.24 = (bf16[128,128]{1,0:T(8,128)(2,1)S(1)}, bf16[128,128]{1,0:T(8,128)(2,1)S(1)}, u32[]{:S(2)}, u32[]{:S(2)}) collective-permute-start(bf16[128,128]{1,0:T(8,128)(2,1)S(1)} %get-tuple-element.73), channel_id=1, source_target_pairs={{0,24},{2,26},{4,28},{6,30},{8,0},{10,2},{12,4},{14,6},{16,8},{18,... | collective-permute-start | bytes 98312 | tf_op jit(solution)/shard_map/ppermute | solution.py:387

commit v3 on v2

--- a/solution.py
+++ b/solution.py
@@ -12,7 +12,6 @@
 BF16 = jnp.bfloat16
 VMEM = pl.BlockSpec(memory_space=pltpu.VMEM)
 SMEM = pl.BlockSpec(memory_space=pltpu.SMEM)
-ANY = pl.BlockSpec(memory_space=pl.ANY)
 MIB = 1 << 20
 
 
@@ -152,44 +151,35 @@
     )(base, cols, table.T, student)
 
 
-def load_shards(shards, table, sems, own):
-    copies = [
-        pltpu.make_async_copy(shard, table.at[pl.ds(j * own, own)], sems.at[j]) for j, shard in enumerate(shards)
-    ]
-    for copy in copies:
-        copy.start()
-    return copies
+def joined(shards, columns):
+    return jnp.concatenate([shard[:, columns] for shard in shards], axis=0)
 
 
 def anchor_kernel(count, own, has_acc, bases, cols, *rest):
     acc_in, rest = (rest[0], rest[1:]) if has_acc else (None, rest)
-    shards, (out, table, hot, sems) = rest[:count], rest[count:]
-    copies = load_shards(shards, table, sems, own)
-    q = cols.shape[0]
+    shards, out = rest[:count], rest[count]
     ids = cols[:, 0:1]
-    lane = lax.broadcasted_iota(jnp.int32, (q, own), 1)
-    for j in range(count):
-        hot[:, j * own : (j + 1) * own] = (ids - bases[j] == lane).astype(F32).astype(BF16)
-    for copy in copies:
-        copy.wait()
-    found = jnp.dot(hot[...], table[...], preferred_element_type=F32).astype(BF16)
-    out[...] = found + acc_in[...] if has_acc else found
-
-
-def anchor_rows(bases, ids, shards, acc, shape):
+    lane = lax.broadcasted_iota(jnp.int32, (cols.shape[0], own), 1)
+    group = max(1, 512 // own)
+    total = None
+    for first in range(0, count, group):
+        last = min(count, first + group)
+        hot = jnp.concatenate([(ids - bases[j] == lane).astype(F32).astype(BF16) for j in range(first, last)], axis=1)
+        found = jnp.dot(hot, joined(shards[first:last], slice(None)), preferred_element_type=F32)
+        total = found if total is None else total + found
+    total = total.astype(BF16)
+    out[...] = total + acc_in[...] if has_acc else total
+
+
+def anchor_rows(bases, cols, shards, acc, shape):
     own = shards[0].shape[0]
-    q, count = ids.shape[0], len(shards)
-    operands = [bases, ids] + ([] if acc is None else [acc]) + list(shards)
+    q, count = cols.shape[0], len(shards)
+    operands = [bases, cols] + ([] if acc is None else [acc]) + list(shards)
     return pl.pallas_call(
         functools.partial(anchor_kernel, count, own, acc is not None),
         out_shape=jax.ShapeDtypeStruct((q, shape.total), BF16),
-        in_specs=[SMEM, VMEM] + ([] if acc is None else [VMEM]) + [ANY] * count,
+        in_specs=[SMEM, VMEM] + ([] if acc is None else [VMEM]) + [VMEM] * count,
         out_specs=VMEM,
-        scratch_shapes=[
-            pltpu.VMEM((count * own, shape.total), BF16),
-            pltpu.VMEM((q, count * own), BF16),
-            pltpu.SemaphoreType.DMA((count,)),
-        ],
         compiler_params=pltpu.CompilerParams(vmem_limit_bytes=2 * count * own * (shape.total + q) + 12 * MIB),
         cost_estimate=pl.CostEstimate(
             flops=2 * q * count * own * shape.total,
@@ -201,8 +191,7 @@
 
 
 def score_kernel(shape, own, n, chunk, mine, other, relation, relation_b, cols, *rest):
-    shards, (t_out, s_out, stats, q_student, table, q_teacher, sems) = rest[:n], rest[n:]
-    copies = load_shards(shards, table, sems, own)
+    shards, (t_out, s_out, stats, q_student, q_teacher) = rest[:n], rest[n:]
     q = mine.shape[0]
     sw, wide = shape.sw, shape.wide
     rows = 128
@@ -224,16 +213,14 @@
         return 0
 
     lax.fori_loop(0, q // rows, build, 0)
-    for copy in copies:
-        copy.wait()
-
     dims = (((1,), (1,)), ((), ()))
 
     def score(c, carry):
         top_t, total_t, weighted, top_s, total_s = carry
-        at = pl.ds(pl.multiple_of(c * chunk, chunk), chunk)
-        t = lax.dot_general(table[at, sw:], q_teacher[...], dims, preferred_element_type=F32)
-        s = lax.dot_general(table[at, :sw], q_student[...], dims, preferred_element_type=F32)
+        at = slice(c * chunk, (c + 1) * chunk)
+        group = shards[c * chunk // own : (c + 1) * chunk // own]
+        t = lax.dot_general(joined(group, slice(sw, None)), q_teacher[...], dims, preferred_element_type=F32)
+        s = lax.dot_general(joined(group, slice(0, sw)), q_student[...], dims, preferred_element_type=F32)
         t_out[at, :] = t
         s_out[at, :] = s
         new_t = jnp.maximum(top_t, jnp.max(t, axis=0, keepdims=True))
@@ -247,7 +234,9 @@
 
     lowest = jnp.full((1, q), -jnp.inf, F32)
     nothing = jnp.zeros((1, q), F32)
-    found = lax.fori_loop(0, n * own // chunk, score, (lowest, nothing, nothing, lowest, nothing), unroll=True)
+    found = (lowest, nothing, nothing, lowest, nothing)
+    for c in range(n * own // chunk):
+        found = score(c, found)
     stats[...] = jnp.concatenate(list(found) + [nothing] * 3, axis=0)
 
 
@@ -264,13 +253,9 @@
             jax.ShapeDtypeStruct((8, q), F32),
             jax.ShapeDtypeStruct((q, shape.sw), BF16),
         ),
-        in_specs=[VMEM] * 5 + [ANY] * n,
+        in_specs=[VMEM] * (5 + n),
         out_specs=(VMEM,) * 4,
-        scratch_shapes=[
-            pltpu.VMEM((slab, shape.total), BF16),
-            pltpu.VMEM((q, 2 * shape.wide), BF16),
-            pltpu.SemaphoreType.DMA((n,)),
-        ],
+        scratch_shapes=[pltpu.VMEM((q, 2 * shape.wide), BF16)],
         compiler_params=pltpu.CompilerParams(vmem_limit_bytes=8 * slab * q + 2 * slab * shape.total + 10 * MIB),
         cost_estimate=pl.CostEstimate(
             flops=2 * q * slab * shape.total, bytes_accessed=2 * slab * shape.total + 8 * slab * q, transcendentals=2 * slab * q
@@ -290,23 +275,15 @@
 
 
 def grad_kernel(n, own, chunk, sw, order, t_in, s_in, mine, other, q_student, *rest):
-    shards, (divergence, q_grad), outs = rest[:n], rest[n : n + 2], rest[n + 2 : -3]
-    table, e_grad, sems = rest[-3:]
-    copies = [
-        pltpu.make_async_copy(shard.at[:, pl.ds(0, sw)], table.at[pl.ds(j * own, own)], sems.at[j])
-        for j, shard in enumerate(shards)
-    ]
-    for copy in copies:
-        copy.start()
+    shards, (divergence, q_grad), outs = rest[:n], rest[n : n + 2], rest[n + 2 : -1]
+    e_grad = rest[-1]
     top_t, total_t, weighted, top_s, total_s = combine(mine[...], other[...])
     divergence[...] = weighted / total_t - top_t - jnp.log(total_t) + top_s + jnp.log(total_s)
     over_t, over_s = 1.0 / total_t, 1.0 / total_s
-    for copy in copies:
-        copy.wait()
     per = chunk // own
 
     def step(c, total):
-        at = pl.ds(pl.multiple_of(c * chunk, chunk), chunk)
+        at = slice(c * chunk, (c + 1) * chunk)
         prob_t = jnp.exp(t_in[at, :] - top_t) * over_t
         prob_s = jnp.exp(s_in[at, :] - top_s) * over_s
         weights = (prob_s - prob_t).astype(BF16)
@@ -314,11 +291,16 @@
         for k in range(per):
             e_grad[order[c * per + k]] = grad[k * own : (k + 1) * own, :]
         return total + lax.dot_general(
-            table[at, :], weights, (((0,), (0,)), ((), ())), preferred_element_type=F32
+            joined(shards[c * per : (c + 1) * per], slice(0, sw)),
+            weights,
+            (((0,), (0,)), ((), ())),
+            preferred_element_type=F32,
         )
 
     q = q_student.shape[0]
-    total = lax.fori_loop(0, n * own // chunk, step, jnp.zeros((sw, q), F32), unroll=True)
+    total = jnp.zeros((sw, q), F32)
+    for c in range(n * own // chunk):
+        total = step(c, total)
     q_grad[...] = total.T
     count = n // len(outs)
     for d, out in enumerate(outs):
@@ -329,6 +311,7 @@
     n, own = len(shards), shards[0].shape[0]
     q, sw = q_student.shape
     slab = n * own
+    shape_total = shards[0].shape[1]
     chunk = 512 if slab % 512 == 0 else own
     return pl.pallas_call(
         functools.partial(grad_kernel, n, own, chunk, sw),
@@ -337,14 +320,10 @@
             jax.ShapeDtypeStruct((q, sw), F32),
         )
         + (jax.ShapeDtypeStruct((n // near, own, sw), BF16),) * near,
-        in_specs=[SMEM] + [VMEM] * 5 + [ANY] * n,
+        in_specs=[SMEM] + [VMEM] * (5 + n),
         out_specs=(VMEM,) * (2 + near),
-        scratch_shapes=[
-            pltpu.VMEM((slab, sw), BF16),
-            pltpu.VMEM((n, own, sw), BF16),
-            pltpu.SemaphoreType.DMA((n,)),
-        ],
-        compiler_params=pltpu.CompilerParams(vmem_limit_bytes=8 * slab * q + 10 * MIB),
+        scratch_shapes=[pltpu.VMEM((n, own, sw), BF16)],
+        compiler_params=pltpu.CompilerParams(vmem_limit_bytes=8 * slab * q + 2 * slab * shape_total + 10 * MIB),
         cost_estimate=pl.CostEstimate(
             flops=4 * q * slab * sw, bytes_accessed=8 * slab * q, transcendentals=2 * slab * q
         ),

time: 84.6 us -> 82.6 us (0.976)
  Pallas kernels: 25.1 us -> 21.6 us
  waiting for transfers between devices: 31 us -> 33.5 us
    pallas_call x2, Pallas kernels: 6.76 us -> 4.6 us  [anchor_rows(): pl.pallas_call(functools.partial(anchor_kernel, count, own, acc is not No...]
    ppermute x15, waiting for transfers between devices: 20.1 us -> 21.8 us  [move(): return lax.ppermute(x, 'query', sorted(pairs))]
    pallas_call x1, Pallas kernels: 6.38 us -> 5.2 us  [scores(): pl.pallas_call(functools.partial(score_kernel, shape, own, n, chunk), out...]
    ppermute x4, starting transfers between devices: 1.31 us -> 0.44 us  [partner(): return lax.ppermute(x, 'entity', [(i, i ^ far) for i in range(size)])]
  transfers between devices with their start and end apart: 25 -> 25, of which waited for: 14 -> 14; matrix products, arithmetic and copies ran while one was open for 2% -> 2% of each run, Pallas kernels for 16% -> 14%
where the time goes in v3:
time: 82.6 us; the launch traced here: 82.5 us
  waiting for transfers between devices  33.5 us (41%)
  starting transfers between devices  24.6 us (30%)
  Pallas kernels  21.6 us (26%)
  other arithmetic  1.38 us (2%)
    ppermute x15, waiting for transfers between devices, move(): return lax.ppermute(x, 'query', sorted(pairs))  21.8 us
    ppermute x15, starting transfers between devices, move(): return lax.ppermute(x, 'query', sorted(pairs))  15.1 us
    pallas_call x1, Pallas kernels, relation_rows(): pl.pallas_call(functools.partial(relation_kernel, shape, rel, block, cut)...  6.93 us
    ppermute x3, starting transfers between devices, reduce_blocks(): total = total + lax.ppermute(sums[e], 'query', pairs).astype(F32)  5.56 us
    ppermute x3, waiting for transfers between devices, reduce_blocks(): lax.ppermute(blocks[d], 'query', [(i, i ^ d) for i in range(n)])  5.23 us
    pallas_call x1, Pallas kernels, scores(): pl.pallas_call(functools.partial(score_kernel, shape, own, n, chunk), out...  5.2 us
    pallas_call x2, Pallas kernels, anchor_rows(): pl.pallas_call(functools.partial(anchor_kernel, count, own, acc is not No...  4.6 us
    ppermute x4, waiting for transfers between devices, partner(): return lax.ppermute(x, 'entity', [(i, i ^ far) for i in range(size)])  3.88 us
  transfers between devices with their start and end apart: 25, of which 14 were waited for; matrix products, arithmetic and copies ran while one was open for 2% of the time, Pallas kernels for 14%

profile of v3, /device:TPU:0, one launch (start us, length us, event | category | flops | bytes accessed | tf_op | source)
XLA Modules:
  0.0 82.5 jit_solution(13019780945075497693)
XLA Ops:
  0.6 2.0 %pack_rows.1 = (bf16[128,1152]{1,0:T(8,128)(2,1)}, s32[512,8]{1,0:T(8,128)}) custom-call(bf16[1000,128]{1,0:T(8,128)(2,1)} %bitcast.14, bf16[128,128]{1,0:T(8,128)(2,1)} %student.2, s32[1,512]{1,0:T(1,128)} %bitcast.15, s32[1,512]{1,0:T(1,128)} %bitcast.16, s32[1,512]{1,0:T(1,128)} %bitcast.17), custom_call_target="tpu_custom_call" | custom-call | tf_op jit(solution)/shard_map/pack_rows/pallas_call | solution.py:97
  2.7 2.9 %collective-permute-start.2 = (bf16[128,1152]{1,0:T(8,128)(2,1)}, bf16[128,1152]{1,0:T(8,128)(2,1)S(1)}, u32[]{:S(2)}, u32[]{:S(2)}) collective-permute-start(bf16[128,1152]{1,0:T(8,128)(2,1)} %get-tuple-element.41.rest_0_), channel_id=1, source_target_pairs={{0,2},{2,0},{4,6},{6,4},{8,10},{10,8},{12,14},{14,12},{16,18},{18,... | collective-permute-start | bytes 884744 | tf_op jit(solution)/shard_map/ppermute | solution.py:56
  5.6 1.6 %collective-permute-start.1 = (bf16[128,1152]{1,0:T(8,128)(2,1)}, bf16[128,1152]{1,0:T(8,128)(2,1)S(1)}, u32[]{:S(2)}, u32[]{:S(2)}) collective-permute-start(bf16[128,1152]{1,0:T(8,128)(2,1)} %get-tuple-element.41.rest_0_), channel_id=1, source_target_pairs={{0,8},{2,10},{4,0},{6,2},{8,16},{10,18},{12,4},{14,6},{16,24},{18,... | collective-permute-start | bytes 884744 | tf_op jit(solution)/shard_map/ppermute | solution.py:56
  7.7 6.9 %relation_rows.1.relation = bf16[512,1152]{1,0:T(8,128)(2,1)} custom-call(s32[1]{0:T(128)} %bitcast.7.base, s32[512,8]{1,0:T(8,128)} %get-tuple-element.39.cols, bf16[1000,4131]{1,0:T(8,128)(2,1)} %bitcast.13, bf16[4131,128]{1,0:T(8,128)(2,1)} %student.3), custom_call_target="tpu_custom_call" | custom-call | flops 2359296000 | bytes 4608000 | tf_op jit(solution)/shard_map/relation_rows/pallas_call | solution.py:133
  14.6 1.0 %collective-permute-done.rest_1_ = bf16[128,1152]{1,0:T(8,128)(2,1)S(1)} collective-permute-done((bf16[128,1152]{1,0:T(8,128)(2,1)}, bf16[128,1152]{1,0:T(8,128)(2,1)S(1)}, u32[]{:S(2)}, u32[]{:S(2)}) %collective-permute-start) | collective-permute-done | bytes 294944 | tf_op jit(solution)/shard_map/ppermute | solution.py:56
  15.6 1.6 %collective-permute-start.4 = (bf16[128,1152]{1,0:T(8,128)(2,1)S(1)}, bf16[128,1152]{1,0:T(8,128)(2,1)S(1)}, u32[]{:S(2)}, u32[]{:S(2)}) collective-permute-start(bf16[128,1152]{1,0:T(8,128)(2,1)S(1)} %collective-permute-done.1.rest_2_), channel_id=1, source_target_pairs={{0,8},{2,10},{4,0},{6,2},{8,16},{10,18},{12,4},{14,6},{16,24},{18,... | collective-permute-start | bytes 884744 | tf_op jit(solution)/shard_map/ppermute | solution.py:56
  18.2 4.7 %collective-permute-done.4.rest_5_ = bf16[128,1152]{1,0:T(8,128)(2,1)S(1)} collective-permute-done((bf16[128,1152]{1,0:T(8,128)(2,1)S(1)}, bf16[128,1152]{1,0:T(8,128)(2,1)S(1)}, u32[]{:S(2)}, u32[]{:S(2)}) %collective-permute-start.4) | collective-permute-done | bytes 294944 | tf_op jit(solution)/shard_map/ppermute | solution.py:56
  22.9 1.6 %collective-permute-start.7 = (bf16[128,1152]{1,0:T(8,128)(2,1)S(1)}, bf16[128,1152]{1,0:T(8,128)(2,1)S(1)}, u32[]{:S(2)}, u32[]{:S(2)}) collective-permute-start(bf16[128,1152]{1,0:T(8,128)(2,1)S(1)} %collective-permute-done.4.rest_5_), channel_id=1, source_target_pairs={{0,8},{2,10},{4,0},{6,2},{8,16},{10,18},{12,4},{14,6},{16,24},{18,... | collective-permute-start | bytes 884744 | tf_op jit(solution)/shard_map/ppermute | solution.py:56
  24.4 1.5 %collective-permute-start.8 = (bf16[128,1152]{1,0:T(8,128)(2,1)S(1)}, bf16[128,1152]{1,0:T(8,128)(2,1)S(1)}, u32[]{:S(2)}, u32[]{:S(2)}) collective-permute-start(bf16[128,1152]{1,0:T(8,128)(2,1)S(1)} %collective-permute-done.3.rest_4_), channel_id=1, source_target_pairs={{0,2},{2,0},{4,6},{6,4},{8,10},{10,8},{12,14},{14,12},{16,18},{18,... | collective-permute-start | bytes 884744 | tf_op jit(solution)/shard_map/ppermute | solution.py:56
  26.4 4.3 %collective-permute-done.7.rest_8_ = bf16[128,1152]{1,0:T(8,128)(2,1)S(1)} collective-permute-done((bf16[128,1152]{1,0:T(8,128)(2,1)S(1)}, bf16[128,1152]{1,0:T(8,128)(2,1)S(1)}, u32[]{:S(2)}, u32[]{:S(2)}) %collective-permute-start.7) | collective-permute-done | bytes 294944 | tf_op jit(solution)/shard_map/ppermute | solution.py:56
  30.6 1.6 %collective-permute-start.11 = (bf16[128,1152]{1,0:T(8,128)(2,1)S(1)}, bf16[128,1152]{1,0:T(8,128)(2,1)S(1)}, u32[]{:S(2)}, u32[]{:S(2)}) collective-permute-start(bf16[128,1152]{1,0:T(8,128)(2,1)S(1)} %collective-permute-done.2.rest_3_), channel_id=1, source_target_pairs={{0,8},{2,10},{4,0},{6,2},{8,16},{10,18},{12,4},{14,6},{16,24},{18,... | collective-permute-start | bytes 884744 | tf_op jit(solution)/shard_map/ppermute | solution.py:56
  32.2 1.5 %collective-permute-done.6.rest_7_ = bf16[128,1152]{1,0:T(8,128)(2,1)S(1)} collective-permute-done((bf16[128,1152]{1,0:T(8,128)(2,1)S(1)}, bf16[128,1152]{1,0:T(8,128)(2,1)S(1)}, u32[]{:S(2)}, u32[]{:S(2)}) %collective-permute-start.6) | collective-permute-done | bytes 294944 | tf_op jit(solution)/shard_map/ppermute | solution.py:56
  34.2 0.7 constant_dynamic-slice_fusion
  34.9 8.5 %collective-permute-done.9.rest_12_ = bf16[128,1152]{1,0:T(8,128)(2,1)S(1)} collective-permute-done((bf16[128,1152]{1,0:T(8,128)(2,1)S(1)}, bf16[128,1152]{1,0:T(8,128)(2,1)S(1)}, u32[]{:S(2)}, u32[]{:S(2)}) %collective-permute-start.9) | collective-permute-done | bytes 294944 | tf_op jit(solution)/shard_map/ppermute | solution.py:56
  43.8 1.6 %collective-permute-start.13 = (bf16[128,1152]{1,0:T(8,128)(2,1)S(1)}, bf16[128,1152]{1,0:T(8,128)(2,1)S(1)}, u32[]{:S(2)}, u32[]{:S(2)}) collective-permute-start(bf16[128,1152]{1,0:T(8,128)(2,1)S(1)} %collective-permute-done.11.rest_11_), channel_id=1, source_target_pairs={{0,8},{2,10},{4,0},{6,2},{8,16},{10,18},{12,4},{14,6},{16,24},{18,... | collective-permute-start | bytes 884744 | tf_op jit(solution)/shard_map/ppermute | solution.py:56
  45.5 3.2 %anchor_rows.2.rest_0_ = bf16[512,1152]{1,0:T(8,128)(2,1)S(1)} custom-call(s32[16]{0:T(128)S(1)} %bitcast.12, s32[512,8]{1,0:T(8,128)S(1)} %copy-done.1, bf16[128,1152]{1,0:T(8,128)(2,1)S(1)} %copy-done.2, bf16[128,1152]{1,0:T(8,128)(2,1)S(1)} %collective-permute-done.rest_1_, bf16[128,1152]{1,0:T(8,128)(2,1)S(1)} %collective-permute-done.1.rest_2_, ...), custom_call_target="tpu_custom_call" | custom-call | flops 1962934272 | bytes 6193152 | tf_op jit(solution)/shard_map/anchor_rows/pallas_call | solution.py:178
  48.7 1.9 %collective-permute-done.13.rest_2_.rest_14_ = bf16[128,1152]{1,0:T(8,128)(2,1)S(1)} collective-permute-done((bf16[128,1152]{1,0:T(8,128)(2,1)S(1)}, bf16[128,1152]{1,0:T(8,128)(2,1)S(1)}, u32[]{:S(2)}, u32[]{:S(2)}) %collective-permute-start.13) | collective-permute-done | bytes 294944 | tf_op jit(solution)/shard_map/ppermute | solution.py:56
  50.6 1.4 %anchor_rows.3.mine = bf16[512,1152]{1,0:T(8,128)(2,1)S(1)} custom-call(s32[3]{0:T(128)S(1)} %slice_bitcast_fusion.bases, s32[512,8]{1,0:T(8,128)S(1)} %copy-done.1, bf16[512,1152]{1,0:T(8,128)(2,1)S(1)} %anchor_rows.2.rest_0_, bf16[128,1152]{1,0:T(8,128)(2,1)S(1)} %collective-permute-done.12.rest_1_.rest_13_, ...), custom_call_target="tpu_custom_call" | custom-call | flops 452984832 | bytes 3244032 | tf_op jit(solution)/shard_map/anchor_rows/pallas_call | solution.py:178
  52.0 2.8 %collective-permute-done.15.other = bf16[512,1152]{1,0:T(8,128)(2,1)S(1)} collective-permute-done((bf16[512,1152]{1,0:T(8,128)(2,1)S(1)}, bf16[512,1152]{1,0:T(8,128)(2,1)S(1)}, u32[]{:S(2)}, u32[]{:S(2)}) %collective-permute-start.15) | collective-permute-done | bytes 1179680 | tf_op jit(solution)/shard_map/ppermute | solution.py:69
  54.9 5.2 %scores.1 = (f32[2048,512]{1,0:T(8,128)S(1)}, f32[2048,512]{1,0:T(8,128)S(1)}, f32[8,512]{1,0:T(8,128)S(1)}, bf16[512,128]{1,0:T(8,128)(2,1)S(1)}) custom-call(bf16[512,1152]{1,0:T(8,128)(2,1)S(1)} %anchor_rows.3.mine, bf16[512,1152]{1,0:T(8,128)(2,1)S(1)} %collective-permute-done.15.other, bf16[512,1152]{1,0:T(8,128)(2,1)S(1)} %copy-done, ...), custom_call_target="tpu_custom_call" | custom-call | flops 2415919104 | bytes 13107200 | tf_op jit(solution)/shard_map/scores/pallas_call | solution.py:248
  60.3 1.0 %collective-permute-done.17.other = f32[8,512]{1,0:T(8,128)S(1)} collective-permute-done((f32[8,512]{1,0:T(8,128)S(1)}, f32[8,512]{1,0:T(8,128)S(1)}, u32[]{:S(2)}, u32[]{:S(2)}) %collective-permute-start.17) | collective-permute-done | bytes 16416 | tf_op jit(solution)/shard_map/ppermute | solution.py:69
  61.3 2.7 %gradients.1 = (f32[1,512]{1,0:T(1,128)}, f32[512,128]{1,0:T(8,128)S(1)}, bf16[4,128,128]{2,1,0:T(8,128)(2,1)S(1)}, bf16[4,128,128]{2,1,0:T(8,128)(2,1)S(1)}, bf...) custom-call(s32[16]{0:T(128)S(1)} %get-tuple-element.76.order, f32[2048,512]{1,0:T(8,128)S(1)} %get-tuple-element.59.t_in, ...), custom_call_target="tpu_custom_call" | custom-call | flops 536870912 | bytes 8388608 | tf_op jit(solution)/shard_map/gradients/pallas_call | solution.py:316
  64.2 2.1 %collective-permute-start.20 = (bf16[4,128,128]{2,1,0:T(8,128)(2,1)S(1)}, bf16[4,128,128]{2,1,0:T(8,128)(2,1)S(1)}, u32[]{:S(2)}, u32[]{:S(2)}) collective-permute-start(bf16[4,128,128]{2,1,0:T(8,128)(2,1)S(1)} %get-tuple-element.67), channel_id=1, source_target_pairs={{0,6},{2,4},{4,2},{6,0},{8,14},{10,12},{12,10},{14,8},{16,22},{18,... | collective-permute-start | bytes 393224 | tf_op jit(solution)/shard_map/ppermute | solution.py:360
  66.4 1.3 %collective-permute-start.19 = (bf16[4,128,128]{2,1,0:T(8,128)(2,1)S(1)}, bf16[4,128,128]{2,1,0:T(8,128)(2,1)S(1)}, u32[]{:S(2)}, u32[]{:S(2)}) collective-permute-start(bf16[4,128,128]{2,1,0:T(8,128)(2,1)S(1)} %get-tuple-element.66), channel_id=1, source_target_pairs={{0,4},{2,6},{4,0},{6,2},{8,12},{10,14},{12,8},{14,10},{16,20},{18,... | collective-permute-start | bytes 393224 | tf_op jit(solution)/shard_map/ppermute | solution.py:360
  67.7 0.7 add.30
  68.5 3.0 %collective-permute-done.20.refs_3_ = bf16[4,128,128]{2,1,0:T(8,128)(2,1)S(1)} collective-permute-done((bf16[4,128,128]{2,1,0:T(8,128)(2,1)S(1)}, bf16[4,128,128]{2,1,0:T(8,128)(2,1)S(1)}, u32[]{:S(2)}, u32[]{:S(2)}) %collective-permute-start.20) | collective-permute-done | bytes 131104 | tf_op jit(solution)/shard_map/ppermute | solution.py:360
  71.4 1.6 %collective-permute-done.18.refs_1_ = bf16[4,128,128]{2,1,0:T(8,128)(2,1)S(1)} collective-permute-done((bf16[4,128,128]{2,1,0:T(8,128)(2,1)S(1)}, bf16[4,128,128]{2,1,0:T(8,128)(2,1)S(1)}, u32[]{:S(2)}, u32[]{:S(2)}) %collective-permute-start.18) | collective-permute-done | bytes 131104 | tf_op jit(solution)/shard_map/ppermute | solution.py:360
  73.8 1.6 %collective-permute-start.22 = (bf16[128,128]{1,0:T(8,128)(2,1)S(1)}, bf16[128,128]{1,0:T(8,128)(2,1)S(1)}, u32[]{:S(2)}, u32[]{:S(2)}) collective-permute-start(bf16[128,128]{1,0:T(8,128)(2,1)S(1)} %get-tuple-element.71), channel_id=1, source_target_pairs={{0,8},{2,10},{4,12},{6,14},{8,16},{10,18},{12,20},{14,22},{16,24},... | collective-permute-start | bytes 98312 | tf_op jit(solution)/shard_map/ppermute | solution.py:366
  75.4 2.5 %collective-permute-start.23 = (bf16[128,128]{1,0:T(8,128)(2,1)S(1)}, bf16[128,128]{1,0:T(8,128)(2,1)S(1)}, u32[]{:S(2)}, u32[]{:S(2)}) collective-permute-start(bf16[128,128]{1,0:T(8,128)(2,1)S(1)} %get-tuple-element.72), channel_id=1, source_target_pairs={{0,16},{2,18},{4,20},{6,22},{8,24},{10,26},{12,28},{14,30},{16,0},... | collective-permute-start | bytes 98312 | tf_op jit(solution)/shard_map/ppermute | solution.py:366
  77.9 1.4 %collective-permute-start.24 = (bf16[128,128]{1,0:T(8,128)(2,1)S(1)}, bf16[128,128]{1,0:T(8,128)(2,1)S(1)}, u32[]{:S(2)}, u32[]{:S(2)}) collective-permute-start(bf16[128,128]{1,0:T(8,128)(2,1)S(1)} %get-tuple-element.73), channel_id=1, source_target_pairs={{0,24},{2,26},{4,28},{6,30},{8,0},{10,2},{12,4},{14,6},{16,8},{18,... | collective-permute-start | bytes 98312 | tf_op jit(solution)/shard_map/ppermute | solution.py:366
  79.5 1.2 %collective-permute-done.23 = bf16[128,128]{1,0:T(8,128)(2,1)S(1)} collective-permute-done((bf16[128,128]{1,0:T(8,128)(2,1)S(1)}, bf16[128,128]{1,0:T(8,128)(2,1)S(1)}, u32[]{:S(2)}, u32[]{:S(2)}) %collective-permute-start.23) | collective-permute-done | bytes 32800 | tf_op jit(solution)/shard_map/ppermute | solution.py:366
  80.7 1.1 %collective-permute-done.24 = bf16[128,128]{1,0:T(8,128)(2,1)S(1)} collective-permute-done((bf16[128,128]{1,0:T(8,128)(2,1)S(1)}, bf16[128,128]{1,0:T(8,128)(2,1)S(1)}, u32[]{:S(2)}, u32[]{:S(2)}) %collective-permute-start.24) | collective-permute-done | bytes 32800 | tf_op jit(solution)/shard_map/ppermute | solution.py:366
  (36 shorter events, 4.9 us)
Async XLA Ops:
  2.7 11.9 %collective-permute-start.2 = (bf16[128,1152]{1,0:T(8,128)(2,1)}, bf16[128,1152]{1,0:T(8,128)(2,1)S(1)}, u32[]{:S(2)}, u32[]{:S(2)}) collective-permute-start(bf16[128,1152]{1,0:T(8,128)(2,1)} %get-tuple-element.41.rest_0_), channel_id=1, source_target_pairs={{0,2},{2,0},{4,6},{6,4},{8,10},{10,8},{12,14},{14,12},{16,18},{18,... | collective-permute-start | bytes 884744 | tf_op jit(solution)/shard_map/ppermute | solution.py:56
  5.6 9.0 %collective-permute-start.1 = (bf16[128,1152]{1,0:T(8,128)(2,1)}, bf16[128,1152]{1,0:T(8,128)(2,1)S(1)}, u32[]{:S(2)}, u32[]{:S(2)}) collective-permute-start(bf16[128,1152]{1,0:T(8,128)(2,1)} %get-tuple-element.41.rest_0_), channel_id=1, source_target_pairs={{0,8},{2,10},{4,0},{6,2},{8,16},{10,18},{12,4},{14,6},{16,24},{18,... | collective-permute-start | bytes 884744 | tf_op jit(solution)/shard_map/ppermute | solution.py:56
  7.2 8.4 %collective-permute-start = (bf16[128,1152]{1,0:T(8,128)(2,1)}, bf16[128,1152]{1,0:T(8,128)(2,1)S(1)}, u32[]{:S(2)}, u32[]{:S(2)}) collective-permute-start(bf16[128,1152]{1,0:T(8,128)(2,1)} %get-tuple-element.41.rest_0_), channel_id=1, source_target_pairs={{0,4},{2,6},{4,12},{6,14},{8,0},{10,2},{12,20},{14,22},{16,8},{18,... | collective-permute-start | bytes 884744 | tf_op jit(solution)/shard_map/ppermute | solution.py:56
  7.7 37.8 %copy-start.1 = (s32[512,8]{1,0:T(8,128)S(1)}, s32[512,8]{1,0:T(8,128)}, u32[]{:S(2)}) copy-start(s32[512,8]{1,0:T(8,128)} %get-tuple-element.39.cols) | copy-start | bytes 49156
  7.7 37.8 %copy-start.2 = (bf16[128,1152]{1,0:T(8,128)(2,1)S(1)}, bf16[128,1152]{1,0:T(8,128)(2,1)}, u32[]{:S(2)}) copy-start(bf16[128,1152]{1,0:T(8,128)(2,1)} %get-tuple-element.41.rest_0_) | copy-start | bytes 884740
  15.6 7.3 %collective-permute-start.4 = (bf16[128,1152]{1,0:T(8,128)(2,1)S(1)}, bf16[128,1152]{1,0:T(8,128)(2,1)S(1)}, u32[]{:S(2)}, u32[]{:S(2)}) collective-permute-start(bf16[128,1152]{1,0:T(8,128)(2,1)S(1)} %collective-permute-done.1.rest_2_), channel_id=1, source_target_pairs={{0,8},{2,10},{4,0},{6,2},{8,16},{10,18},{12,4},{14,6},{16,24},{18,... | collective-permute-start | bytes 884744 | tf_op jit(solution)/shard_map/ppermute | solution.py:56
  17.2 7.3 %collective-permute-start.5 = (bf16[128,1152]{1,0:T(8,128)(2,1)S(1)}, bf16[128,1152]{1,0:T(8,128)(2,1)S(1)}, u32[]{:S(2)}, u32[]{:S(2)}) collective-permute-start(bf16[128,1152]{1,0:T(8,128)(2,1)S(1)} %collective-permute-done.rest_1_), channel_id=1, source_target_pairs={{0,2},{2,0},{4,6},{6,4},{8,10},{10,8},{12,14},{14,12},{16,18},{18,... | collective-permute-start | bytes 884744 | tf_op jit(solution)/shard_map/ppermute | solution.py:56
  17.7 6.7 %collective-permute-start.3 = (bf16[128,1152]{1,0:T(8,128)(2,1)S(1)}, bf16[128,1152]{1,0:T(8,128)(2,1)S(1)}, u32[]{:S(2)}, u32[]{:S(2)}) collective-permute-start(bf16[128,1152]{1,0:T(8,128)(2,1)S(1)} %collective-permute-done.rest_1_), channel_id=1, source_target_pairs={{0,4},{2,6},{4,12},{6,14},{8,0},{10,2},{12,20},{14,22},{16,8},{18,... | collective-permute-start | bytes 884744 | tf_op jit(solution)/shard_map/ppermute | solution.py:56
  22.9 7.8 %collective-permute-start.7 = (bf16[128,1152]{1,0:T(8,128)(2,1)S(1)}, bf16[128,1152]{1,0:T(8,128)(2,1)S(1)}, u32[]{:S(2)}, u32[]{:S(2)}) collective-permute-start(bf16[128,1152]{1,0:T(8,128)(2,1)S(1)} %collective-permute-done.4.rest_5_), channel_id=1, source_target_pairs={{0,8},{2,10},{4,0},{6,2},{8,16},{10,18},{12,4},{14,6},{16,24},{18,... | collective-permute-start | bytes 884744 | tf_op jit(solution)/shard_map/ppermute | solution.py:56
  24.4 7.8 %collective-permute-start.8 = (bf16[128,1152]{1,0:T(8,128)(2,1)S(1)}, bf16[128,1152]{1,0:T(8,128)(2,1)S(1)}, u32[]{:S(2)}, u32[]{:S(2)}) collective-permute-start(bf16[128,1152]{1,0:T(8,128)(2,1)S(1)} %collective-permute-done.3.rest_4_), channel_id=1, source_target_pairs={{0,2},{2,0},{4,6},{6,4},{8,10},{10,8},{12,14},{14,12},{16,18},{18,... | collective-permute-start | bytes 884744 | tf_op jit(solution)/shard_map/ppermute | solution.py:56
  25.9 7.8 %collective-permute-start.6 = (bf16[128,1152]{1,0:T(8,128)(2,1)S(1)}, bf16[128,1152]{1,0:T(8,128)(2,1)S(1)}, u32[]{:S(2)}, u32[]{:S(2)}) collective-permute-start(bf16[128,1152]{1,0:T(8,128)(2,1)S(1)} %collective-permute-done.3.rest_4_), channel_id=1, source_target_pairs={{0,4},{2,6},{4,12},{6,14},{8,0},{10,2},{12,20},{14,22},{16,8},{18,... | collective-permute-start | bytes 884744 | tf_op jit(solution)/shard_map/ppermute | solution.py:56
  30.6 13.2 %collective-permute-start.11 = (bf16[128,1152]{1,0:T(8,128)(2,1)S(1)}, bf16[128,1152]{1,0:T(8,128)(2,1)S(1)}, u32[]{:S(2)}, u32[]{:S(2)}) collective-permute-start(bf16[128,1152]{1,0:T(8,128)(2,1)S(1)} %collective-permute-done.2.rest_3_), channel_id=1, source_target_pairs={{0,8},{2,10},{4,0},{6,2},{8,16},{10,18},{12,4},{14,6},{16,24},{18,... | collective-permute-start | bytes 884744 | tf_op jit(solution)/shard_map/ppermute | solution.py:56
  33.7 9.6 %collective-permute-start.9 = (bf16[128,1152]{1,0:T(8,128)(2,1)S(1)}, bf16[128,1152]{1,0:T(8,128)(2,1)S(1)}, u32[]{:S(2)}, u32[]{:S(2)}) collective-permute-start(bf16[128,1152]{1,0:T(8,128)(2,1)S(1)} %collective-permute-done.6.rest_7_), channel_id=1, source_target_pairs={{0,2},{2,0},{4,6},{6,4},{8,10},{10,8},{12,14},{14,12},{16,18},{18,... | collective-permute-start | bytes 884744 | tf_op jit(solution)/shard_map/ppermute | solution.py:56
  33.7 9.7 %collective-permute-start.10 = (bf16[128,1152]{1,0:T(8,128)(2,1)S(1)}, bf16[128,1152]{1,0:T(8,128)(2,1)S(1)}, u32[]{:S(2)}, u32[]{:S(2)}) collective-permute-start(bf16[128,1152]{1,0:T(8,128)(2,1)S(1)} %collective-permute-done.6.rest_7_), channel_id=1, source_target_pairs={{0,4},{2,6},{4,12},{6,14},{8,0},{10,2},{12,20},{14,22},{16,8},{18,... | collective-permute-start | bytes 884744 | tf_op jit(solution)/shard_map/ppermute | solution.py:56
  43.4 7.2 %collective-permute-start.14 = (bf16[128,1152]{1,0:T(8,128)(2,1)S(1)}, bf16[128,1152]{1,0:T(8,128)(2,1)S(1)}, u32[]{:S(2)}, u32[]{:S(2)}) collective-permute-start(bf16[128,1152]{1,0:T(8,128)(2,1)S(1)} %collective-permute-done.7.rest_8_), channel_id=1, source_target_pairs={{0,2},{2,0},{4,6},{6,4},{8,10},{10,8},{12,14},{14,12},{16,18},{18,... | collective-permute-start | bytes 884744 | tf_op jit(solution)/shard_map/ppermute | solution.py:56
  43.4 7.2 %collective-permute-start.12 = (bf16[128,1152]{1,0:T(8,128)(2,1)S(1)}, bf16[128,1152]{1,0:T(8,128)(2,1)S(1)}, u32[]{:S(2)}, u32[]{:S(2)}) collective-permute-start(bf16[128,1152]{1,0:T(8,128)(2,1)S(1)} %collective-permute-done.9.rest_12_), channel_id=1, source_target_pairs={{0,4},{2,6},{4,12},{6,14},{8,0},{10,2},{12,20},{14,22},{16,8},{18,... | collective-permute-start | bytes 884744 | tf_op jit(solution)/shard_map/ppermute | solution.py:56
  43.8 6.7 %collective-permute-start.13 = (bf16[128,1152]{1,0:T(8,128)(2,1)S(1)}, bf16[128,1152]{1,0:T(8,128)(2,1)S(1)}, u32[]{:S(2)}, u32[]{:S(2)}) collective-permute-start(bf16[128,1152]{1,0:T(8,128)(2,1)S(1)} %collective-permute-done.11.rest_11_), channel_id=1, source_target_pairs={{0,8},{2,10},{4,0},{6,2},{8,16},{10,18},{12,4},{14,6},{16,24},{18,... | collective-permute-start | bytes 884744 | tf_op jit(solution)/shard_map/ppermute | solution.py:56
  45.5 6.6 %collective-permute-start.16 = (bf16[512,1152]{1,0:T(8,128)(2,1)}, bf16[512,1152]{1,0:T(8,128)(2,1)S(1)}, u32[]{:S(2)}, u32[]{:S(2)}) collective-permute-start(bf16[512,1152]{1,0:T(8,128)(2,1)} %relation_rows.1.relation), channel_id=1, source_target_pairs={{0,1},{1,0},{2,3},{3,2},{4,5},{5,4},{6,7},{7,6},{8,9},{9,8},{10,11... | collective-permute-start | bytes 3538952 | tf_op jit(solution)/shard_map/ppermute | solution.py:69
  48.7 6.2 %copy-start = (bf16[512,1152]{1,0:T(8,128)(2,1)S(1)}, bf16[512,1152]{1,0:T(8,128)(2,1)}, u32[]{:S(2)}) copy-start(bf16[512,1152]{1,0:T(8,128)(2,1)} %relation_rows.1.relation) | copy-start | bytes 3538948
  52.0 2.9 %collective-permute-start.15 = (bf16[512,1152]{1,0:T(8,128)(2,1)S(1)}, bf16[512,1152]{1,0:T(8,128)(2,1)S(1)}, u32[]{:S(2)}, u32[]{:S(2)}) collective-permute-start(bf16[512,1152]{1,0:T(8,128)(2,1)S(1)} %anchor_rows.3.mine), channel_id=1, source_target_pairs={{0,1},{1,0},{2,3},{3,2},{4,5},{5,4},{6,7},{7,6},{8,9},{9,8},{10,11... | collective-permute-start | bytes 3538952 | tf_op jit(solution)/shard_map/ppermute | solution.py:69
  60.1 1.2 %collective-permute-start.17 = (f32[8,512]{1,0:T(8,128)S(1)}, f32[8,512]{1,0:T(8,128)S(1)}, u32[]{:S(2)}, u32[]{:S(2)}) collective-permute-start(f32[8,512]{1,0:T(8,128)S(1)} %get-tuple-element.61.mine), channel_id=1, source_target_pairs={{0,1},{1,0},{2,3},{3,2},{4,5},{5,4},{6,7},{7,6},{8,9},{9,8},{10,11... | collective-permute-start | bytes 49160 | tf_op jit(solution)/shard_map/ppermute | solution.py:69
  64.1 3.7 %collective-permute-start.21 = (f32[512,128]{1,0:T(8,128)S(1)}, f32[512,128]{1,0:T(8,128)S(1)}, u32[]{:S(2)}, u32[]{:S(2)}) collective-permute-start(f32[512,128]{1,0:T(8,128)S(1)} %get-tuple-element.68), channel_id=1, source_target_pairs={{0,1},{1,0},{2,3},{3,2},{4,5},{5,4},{6,7},{7,6},{8,9},{9,8},{10,11... | collective-permute-start | bytes 786440 | tf_op jit(solution)/shard_map/ppermute | solution.py:69
  64.2 7.2 %collective-permute-start.20 = (bf16[4,128,128]{2,1,0:T(8,128)(2,1)S(1)}, bf16[4,128,128]{2,1,0:T(8,128)(2,1)S(1)}, u32[]{:S(2)}, u32[]{:S(2)}) collective-permute-start(bf16[4,128,128]{2,1,0:T(8,128)(2,1)S(1)} %get-tuple-element.67), channel_id=1, source_target_pairs={{0,6},{2,4},{4,2},{6,0},{8,14},{10,12},{12,10},{14,8},{16,22},{18,... | collective-permute-start | bytes 393224 | tf_op jit(solution)/shard_map/ppermute | solution.py:360
  66.4 6.7 %collective-permute-start.18 = (bf16[4,128,128]{2,1,0:T(8,128)(2,1)S(1)}, bf16[4,128,128]{2,1,0:T(8,128)(2,1)S(1)}, u32[]{:S(2)}, u32[]{:S(2)}) collective-permute-start(bf16[4,128,128]{2,1,0:T(8,128)(2,1)S(1)} %get-tuple-element.65), channel_id=1, source_target_pairs={{0,2},{2,0},{4,6},{6,4},{8,10},{10,8},{12,14},{14,12},{16,18},{18,... | collective-permute-start | bytes 393224 | tf_op jit(solution)/shard_map/ppermute | solution.py:360
  66.4 7.3 %collective-permute-start.19 = (bf16[4,128,128]{2,1,0:T(8,128)(2,1)S(1)}, bf16[4,128,128]{2,1,0:T(8,128)(2,1)S(1)}, u32[]{:S(2)}, u32[]{:S(2)}) collective-permute-start(bf16[4,128,128]{2,1,0:T(8,128)(2,1)S(1)} %get-tuple-element.66), channel_id=1, source_target_pairs={{0,4},{2,6},{4,0},{6,2},{8,12},{10,14},{12,8},{14,10},{16,20},{18,... | collective-permute-start | bytes 393224 | tf_op jit(solution)/shard_map/ppermute | solution.py:360
  73.8 5.8 %collective-permute-start.22 = (bf16[128,128]{1,0:T(8,128)(2,1)S(1)}, bf16[128,128]{1,0:T(8,128)(2,1)S(1)}, u32[]{:S(2)}, u32[]{:S(2)}) collective-permute-start(bf16[128,128]{1,0:T(8,128)(2,1)S(1)} %get-tuple-element.71), channel_id=1, source_target_pairs={{0,8},{2,10},{4,12},{6,14},{8,16},{10,18},{12,20},{14,22},{16,24},... | collective-permute-start | bytes 98312 | tf_op jit(solution)/shard_map/ppermute | solution.py:366
  75.4 5.3 %collective-permute-start.23 = (bf16[128,128]{1,0:T(8,128)(2,1)S(1)}, bf16[128,128]{1,0:T(8,128)(2,1)S(1)}, u32[]{:S(2)}, u32[]{:S(2)}) collective-permute-start(bf16[128,128]{1,0:T(8,128)(2,1)S(1)} %get-tuple-element.72), channel_id=1, source_target_pairs={{0,16},{2,18},{4,20},{6,22},{8,24},{10,26},{12,28},{14,30},{16,0},... | collective-permute-start | bytes 98312 | tf_op jit(solution)/shard_map/ppermute | solution.py:366
  77.9 3.9 %collective-permute-start.24 = (bf16[128,128]{1,0:T(8,128)(2,1)S(1)}, bf16[128,128]{1,0:T(8,128)(2,1)S(1)}, u32[]{:S(2)}, u32[]{:S(2)}) collective-permute-start(bf16[128,128]{1,0:T(8,128)(2,1)S(1)} %get-tuple-element.73), channel_id=1, source_target_pairs={{0,24},{2,26},{4,28},{6,30},{8,0},{10,2},{12,4},{14,6},{16,8},{18,... | collective-permute-start | bytes 98312 | tf_op jit(solution)/shard_map/ppermute | solution.py:366

commit v4 on v3

--- a/solution.py
+++ b/solution.py
@@ -155,30 +155,32 @@
     return jnp.concatenate([shard[:, columns] for shard in shards], axis=0)
 
 
-def anchor_kernel(count, own, has_acc, bases, cols, *rest):
-    acc_in, rest = (rest[0], rest[1:]) if has_acc else (None, rest)
-    shards, out = rest[:count], rest[count]
+def anchor_kernel(spots, own, bases, cols, *rest):
+    count = len(spots)
+    shards, accs, out = rest[:count], rest[count:-1], rest[-1]
     ids = cols[:, 0:1]
     lane = lax.broadcasted_iota(jnp.int32, (cols.shape[0], own), 1)
     group = max(1, 512 // own)
     total = None
     for first in range(0, count, group):
         last = min(count, first + group)
-        hot = jnp.concatenate([(ids - bases[j] == lane).astype(F32).astype(BF16) for j in range(first, last)], axis=1)
+        hot = jnp.concatenate([(ids - bases[spots[j]] == lane).astype(F32).astype(BF16) for j in range(first, last)], axis=1)
         found = jnp.dot(hot, joined(shards[first:last], slice(None)), preferred_element_type=F32)
         total = found if total is None else total + found
     total = total.astype(BF16)
-    out[...] = total + acc_in[...] if has_acc else total
-
-
-def anchor_rows(bases, cols, shards, acc, shape):
+    for acc in accs:
+        total = total + acc[...]
+    out[...] = total
+
+
+def anchor_rows(bases, spots, cols, shards, accs, shape):
     own = shards[0].shape[0]
     q, count = cols.shape[0], len(shards)
-    operands = [bases, cols] + ([] if acc is None else [acc]) + list(shards)
-    return pl.pallas_call(
-        functools.partial(anchor_kernel, count, own, acc is not None),
+    operands = [bases, cols] + list(shards) + list(accs)
+    return pl.pallas_call(
+        functools.partial(anchor_kernel, spots, own),
         out_shape=jax.ShapeDtypeStruct((q, shape.total), BF16),
-        in_specs=[SMEM, VMEM] + ([] if acc is None else [VMEM]) + [VMEM] * count,
+        in_specs=[SMEM] + [VMEM] * (len(operands) - 1),
         out_specs=VMEM,
         compiler_params=pltpu.CompilerParams(vmem_limit_bytes=2 * count * own * (shape.total + q) + 12 * MIB),
         cost_estimate=pl.CostEstimate(
@@ -190,17 +192,17 @@
     )(*operands)
 
 
-def score_kernel(shape, own, n, chunk, mine, other, relation, relation_b, cols, *rest):
-    shards, (t_out, s_out, stats, q_student, q_teacher) = rest[:n], rest[n:]
-    q = mine.shape[0]
+def score_kernel(shape, own, n, chunk, anchor, other, relation, cols, *rest):
+    shards, (t_out, s_out, tops, stats, q_student, q_teacher) = rest[:n], rest[n:]
+    q = anchor.shape[0]
     sw, wide = shape.sw, shape.wide
     rows = 128
 
     def build(i, _):
         at = pl.ds(pl.multiple_of(i * rows, rows), rows)
         g = (2 * cols[at, 2:3] - 1).astype(F32)
-        a = mine[at, :].astype(F32) + other[at, :].astype(F32)
-        r = relation[at, :].astype(F32) + relation_b[at, :].astype(F32)
+        a = anchor[at, :].astype(F32) + other[at, :].astype(F32)
+        r = relation[at, :].astype(F32)
         a_re, a_im = a[:, shape.re : shape.re + wide], a[:, shape.im : shape.im + wide]
         r_re, r_im = r[:, shape.re : shape.re + wide], r[:, shape.im : shape.im + wide]
         q_teacher[at, :wide] = (a_re * r_re - g * a_im * r_im).astype(BF16)
@@ -221,15 +223,18 @@
         group = shards[c * chunk // own : (c + 1) * chunk // own]
         t = lax.dot_general(joined(group, slice(sw, None)), q_teacher[...], dims, preferred_element_type=F32)
         s = lax.dot_general(joined(group, slice(0, sw)), q_student[...], dims, preferred_element_type=F32)
-        t_out[at, :] = t
-        s_out[at, :] = s
         new_t = jnp.maximum(top_t, jnp.max(t, axis=0, keepdims=True))
         new_s = jnp.maximum(top_s, jnp.max(s, axis=0, keepdims=True))
         scale_t, scale_s = jnp.exp(top_t - new_t), jnp.exp(top_s - new_s)
         e = jnp.exp(t - new_t)
+        f = jnp.exp(s - new_s)
+        t_out[at, :] = e
+        s_out[at, :] = f
+        tops[2 * c : 2 * c + 1, :] = new_t
+        tops[2 * c + 1 : 2 * c + 2, :] = new_s
         total_t = total_t * scale_t + jnp.sum(e, axis=0, keepdims=True)
         weighted = weighted * scale_t + jnp.sum(e * (t - s), axis=0, keepdims=True)
-        total_s = total_s * scale_s + jnp.sum(jnp.exp(s - new_s), axis=0, keepdims=True)
+        total_s = total_s * scale_s + jnp.sum(f, axis=0, keepdims=True)
         return new_t, total_t, weighted, new_s, total_s
 
     lowest = jnp.full((1, q), -jnp.inf, F32)
@@ -240,9 +245,9 @@
     stats[...] = jnp.concatenate(list(found) + [nothing] * 3, axis=0)
 
 
-def scores(mine, other, relation, relation_b, cols, shards, shape):
+def scores(anchor, other, relation, cols, shards, shape):
     n, own = len(shards), shards[0].shape[0]
-    q = mine.shape[0]
+    q = anchor.shape[0]
     slab = n * own
     chunk = 512 if slab % 512 == 0 else own
     return pl.pallas_call(
@@ -250,18 +255,19 @@
         out_shape=(
             jax.ShapeDtypeStruct((slab, q), F32),
             jax.ShapeDtypeStruct((slab, q), F32),
+            jax.ShapeDtypeStruct((2 * slab // chunk, q), F32),
             jax.ShapeDtypeStruct((8, q), F32),
             jax.ShapeDtypeStruct((q, shape.sw), BF16),
         ),
-        in_specs=[VMEM] * (5 + n),
-        out_specs=(VMEM,) * 4,
+        in_specs=[VMEM] * (4 + n),
+        out_specs=(VMEM,) * 5,
         scratch_shapes=[pltpu.VMEM((q, 2 * shape.wide), BF16)],
         compiler_params=pltpu.CompilerParams(vmem_limit_bytes=8 * slab * q + 2 * slab * shape.total + 10 * MIB),
         cost_estimate=pl.CostEstimate(
             flops=2 * q * slab * shape.total, bytes_accessed=2 * slab * shape.total + 8 * slab * q, transcendentals=2 * slab * q
         ),
         name="scores",
-    )(mine, other, relation, relation_b, cols, *shards)
+    )(anchor, other, relation, cols, *shards)
 
 
 def combine(a, b):
@@ -274,7 +280,7 @@
     return top_t, total_t, weighted, top_s, total_s
 
 
-def grad_kernel(n, own, chunk, sw, order, t_in, s_in, mine, other, q_student, *rest):
+def grad_kernel(n, own, chunk, sw, order, t_in, s_in, tops, mine, other, q_student, *rest):
     shards, (divergence, q_grad), outs = rest[:n], rest[n : n + 2], rest[n + 2 : -1]
     e_grad = rest[-1]
     top_t, total_t, weighted, top_s, total_s = combine(mine[...], other[...])
@@ -284,9 +290,9 @@
 
     def step(c, total):
         at = slice(c * chunk, (c + 1) * chunk)
-        prob_t = jnp.exp(t_in[at, :] - top_t) * over_t
-        prob_s = jnp.exp(s_in[at, :] - top_s) * over_s
-        weights = (prob_s - prob_t).astype(BF16)
+        scale_t = jnp.exp(tops[2 * c : 2 * c + 1, :] - top_t) * over_t
+        scale_s = jnp.exp(tops[2 * c + 1 : 2 * c + 2, :] - top_s) * over_s
+        weights = (s_in[at, :] * scale_s - t_in[at, :] * scale_t).astype(BF16)
         grad = jnp.dot(weights, q_student[...], preferred_element_type=F32).astype(BF16)
         for k in range(per):
             e_grad[order[c * per + k]] = grad[k * own : (k + 1) * own, :]
@@ -307,7 +313,7 @@
         out[...] = e_grad[d * count : (d + 1) * count]
 
 
-def gradients(order, near, t, s, mine, other, q_student, shards):
+def gradients(order, near, t, s, tops, mine, other, q_student, shards):
     n, own = len(shards), shards[0].shape[0]
     q, sw = q_student.shape
     slab = n * own
@@ -320,7 +326,7 @@
             jax.ShapeDtypeStruct((q, sw), F32),
         )
         + (jax.ShapeDtypeStruct((n // near, own, sw), BF16),) * near,
-        in_specs=[SMEM] + [VMEM] * (5 + n),
+        in_specs=[SMEM] + [VMEM] * (6 + n),
         out_specs=(VMEM,) * (2 + near),
         scratch_shapes=[pltpu.VMEM((n, own, sw), BF16)],
         compiler_params=pltpu.CompilerParams(vmem_limit_bytes=8 * slab * q + 2 * slab * shape_total + 10 * MIB),
@@ -328,7 +334,7 @@
             flops=4 * q * slab * sw, bytes_accessed=8 * slab * q, transcendentals=2 * slab * q
         ),
         name="gradients",
-    )(order, t, s, mine, other, q_student, *shards)
+    )(order, t, s, tops, mine, other, q_student, *shards)
 
 
 def add_kernel(count, *refs):
@@ -410,28 +416,28 @@
             if number == 0:
                 relation = relation_rows(base, cols, teacher_relations, student_relations, block, shape)
                 got, relation = lax.optimization_barrier((got, relation))
-                relation_b = partner(relation, groups, 1)
+                relation = relation + partner(relation, groups, 1)
             if number == len(steps) - 1:
                 counted = len(have)
                 names = held[:counted]
-                anchors = anchor_rows(bases, cols, [kept.get(h, have[h]) for h in names], None, shape)
+                anchors = anchor_rows(bases, range(counted), cols, [kept.get(h, have[h]) for h in names], [], shape)
             have.update(got)
         have.update(kept)
         shards = [have[h] for h in held]
-        mine = anchor_rows(bases[counted:], cols, shards[counted:], anchors, shape)
+        anchor = anchor_rows(bases, range(counted, n), cols, shards[counted:], [anchors], shape)
         far = 1
         while far < groups // 2:
-            mine = mine + partner(mine, groups, far)
+            anchor = anchor + partner(anchor, groups, far)
             far *= 2
-        other = partner(mine, groups, far)
-        t, s, stats, q_student = scores(mine, other, relation, relation_b, cols, shards, shape)
+        other = partner(anchor, groups, far)
+        expo_t, expo_s, tops, stats, q_student = scores(anchor, other, relation, cols, shards, shape)
         far = 1
         while far < groups // 2:
             found = combine(stats, partner(stats, groups, far))
             stats = jnp.concatenate(list(found) + [jnp.zeros_like(found[0])] * 3, axis=0)
             far *= 2
         divergence, q_grad, *blocks = gradients(
-            order, near, t, s, stats, partner(stats, groups, far), q_student, shards
+            order, near, expo_t, expo_s, tops, stats, partner(stats, groups, far), q_student, shards
         )
         far = 1
         while far < groups:

time: 82.6 us -> 83.4 us (level)
  waiting for transfers between devices: 33.5 us -> 31.8 us
  Pallas kernels: 21.6 us -> 23.2 us
    ppermute x15, waiting for transfers between devices: 21.8 us -> 20.1 us  [move(): return lax.ppermute(x, 'query', sorted(pairs))]
    pallas_call x1, Pallas kernels: 5.2 us -> 6.3 us  [scores(): pl.pallas_call(functools.partial(score_kernel, shape, own, n, chunk), out...]
  transfers between devices with their start and end apart: 25 -> 25, of which waited for: 14 -> 16; matrix products, arithmetic and copies ran while one was open for 2% -> 2% of each run, Pallas kernels for 14% -> 14%
where the time goes in v4:
time: 83.4 us; the launch traced here: 83.2 us
  waiting for transfers between devices  31.8 us (38%)
  starting transfers between devices  25.1 us (30%)
  Pallas kernels  23.2 us (28%)
  other arithmetic  1.66 us (2%)
    ppermute x15, waiting for transfers between devices, move(): return lax.ppermute(x, 'query', sorted(pairs))  20.1 us
    ppermute x15, starting transfers between devices, move(): return lax.ppermute(x, 'query', sorted(pairs))  15.2 us
    pallas_call x1, Pallas kernels, relation_rows(): pl.pallas_call(functools.partial(relation_kernel, shape, rel, block, cut)...  6.93 us
    pallas_call x1, Pallas kernels, scores(): pl.pallas_call(functools.partial(score_kernel, shape, own, n, chunk), out...  6.3 us
    ppermute x3, starting transfers between devices, reduce_blocks(): total = total + lax.ppermute(sums[e], 'query', pairs).astype(F32)  5.52 us
    ppermute x3, waiting for transfers between devices, reduce_blocks(): lax.ppermute(blocks[d], 'query', [(i, i ^ d) for i in range(n)])  5.51 us
    pallas_call x2, Pallas kernels, anchor_rows(): pl.pallas_call(functools.partial(anchor_kernel, spots, own), out_shape=ja...  5.12 us
    ppermute x3, starting transfers between devices, reduce_blocks(): lax.ppermute(blocks[d], 'query', [(i, i ^ d) for i in range(n)])  3.94 us
  transfers between devices with their start and end apart: 25, of which 16 were waited for; matrix products, arithmetic and copies ran while one was open for 2% of the time, Pallas kernels for 14%

profile of v4, /device:TPU:0, one launch (start us, length us, event | category | flops | bytes accessed | tf_op | source)
XLA Modules:
  0.0 83.2 jit_solution(1219540454442804354)
XLA Ops:
  0.6 2.0 %pack_rows.1 = (bf16[128,1152]{1,0:T(8,128)(2,1)}, s32[512,8]{1,0:T(8,128)}) custom-call(bf16[1000,128]{1,0:T(8,128)(2,1)} %bitcast.12, bf16[128,128]{1,0:T(8,128)(2,1)} %student.2, s32[1,512]{1,0:T(1,128)} %bitcast.13, s32[1,512]{1,0:T(1,128)} %bitcast.14, s32[1,512]{1,0:T(1,128)} %bitcast.15), custom_call_target="tpu_custom_call" | custom-call | tf_op jit(solution)/shard_map/pack_rows/pallas_call | solution.py:97
  2.7 2.9 %collective-permute-start.2 = (bf16[128,1152]{1,0:T(8,128)(2,1)}, bf16[128,1152]{1,0:T(8,128)(2,1)S(1)}, u32[]{:S(2)}, u32[]{:S(2)}) collective-permute-start(bf16[128,1152]{1,0:T(8,128)(2,1)} %get-tuple-element.42.rest_0_), channel_id=1, source_target_pairs={{0,2},{2,0},{4,6},{6,4},{8,10},{10,8},{12,14},{14,12},{16,18},{18,... | collective-permute-start | bytes 884744 | tf_op jit(solution)/shard_map/ppermute | solution.py:56
  5.6 1.6 %collective-permute-start.1 = (bf16[128,1152]{1,0:T(8,128)(2,1)}, bf16[128,1152]{1,0:T(8,128)(2,1)S(1)}, u32[]{:S(2)}, u32[]{:S(2)}) collective-permute-start(bf16[128,1152]{1,0:T(8,128)(2,1)} %get-tuple-element.42.rest_0_), channel_id=1, source_target_pairs={{0,8},{2,10},{4,0},{6,2},{8,16},{10,18},{12,4},{14,6},{16,24},{18,... | collective-permute-start | bytes 884744 | tf_op jit(solution)/shard_map/ppermute | solution.py:56
  7.7 6.9 %relation_rows.1 = bf16[512,1152]{1,0:T(8,128)(2,1)} custom-call(s32[1]{0:T(128)} %bitcast.6.base, s32[512,8]{1,0:T(8,128)} %get-tuple-element.40.cols, bf16[1000,4131]{1,0:T(8,128)(2,1)} %bitcast.11, bf16[4131,128]{1,0:T(8,128)(2,1)} %student.3), custom_call_target="tpu_custom_call" | custom-call | flops 2359296000 | bytes 4608000 | tf_op jit(solution)/shard_map/relation_rows/pallas_call | solution.py:133
  14.6 1.0 %collective-permute-done.rest_1_ = bf16[128,1152]{1,0:T(8,128)(2,1)S(1)} collective-permute-done((bf16[128,1152]{1,0:T(8,128)(2,1)}, bf16[128,1152]{1,0:T(8,128)(2,1)S(1)}, u32[]{:S(2)}, u32[]{:S(2)}) %collective-permute-start) | collective-permute-done | bytes 294944 | tf_op jit(solution)/shard_map/ppermute | solution.py:56
  16.7 1.4 %collective-permute-start.10 = (bf16[128,1152]{1,0:T(8,128)(2,1)S(1)}, bf16[128,1152]{1,0:T(8,128)(2,1)S(1)}, u32[]{:S(2)}, u32[]{:S(2)}) collective-permute-start(bf16[128,1152]{1,0:T(8,128)(2,1)S(1)} %collective-permute-done.1.rest_2_), channel_id=1, source_target_pairs={{0,8},{2,10},{4,0},{6,2},{8,16},{10,18},{12,4},{14,6},{16,24},{18,... | collective-permute-start | bytes 884744 | tf_op jit(solution)/shard_map/ppermute | solution.py:56
  18.2 4.7 %collective-permute-done.5.rest_6_ = bf16[128,1152]{1,0:T(8,128)(2,1)S(1)} collective-permute-done((bf16[128,1152]{1,0:T(8,128)(2,1)S(1)}, bf16[128,1152]{1,0:T(8,128)(2,1)S(1)}, u32[]{:S(2)}, u32[]{:S(2)}) %collective-permute-start.5) | collective-permute-done | bytes 294944 | tf_op jit(solution)/shard_map/ppermute | solution.py:56
  23.1 1.5 %collective-permute-start.6 = (bf16[128,1152]{1,0:T(8,128)(2,1)S(1)}, bf16[128,1152]{1,0:T(8,128)(2,1)S(1)}, u32[]{:S(2)}, u32[]{:S(2)}) collective-permute-start(bf16[128,1152]{1,0:T(8,128)(2,1)S(1)} %collective-permute-done.3.rest_4_), channel_id=1, source_target_pairs={{0,2},{2,0},{4,6},{6,4},{8,10},{10,8},{12,14},{14,12},{16,18},{18,... | collective-permute-start | bytes 884744 | tf_op jit(solution)/shard_map/ppermute | solution.py:56
  24.6 1.0 %collective-permute-start.4 = (bf16[128,1152]{1,0:T(8,128)(2,1)S(1)}, bf16[128,1152]{1,0:T(8,128)(2,1)S(1)}, u32[]{:S(2)}, u32[]{:S(2)}) collective-permute-start(bf16[128,1152]{1,0:T(8,128)(2,1)S(1)} %collective-permute-done.3.rest_4_), channel_id=1, source_target_pairs={{0,4},{2,6},{4,12},{6,14},{8,0},{10,2},{12,20},{14,22},{16,8},{18,... | collective-permute-start | bytes 884744 | tf_op jit(solution)/shard_map/ppermute | solution.py:56
  25.6 1.1 %collective-permute-start.11 = (bf16[128,1152]{1,0:T(8,128)(2,1)S(1)}, bf16[128,1152]{1,0:T(8,128)(2,1)S(1)}, u32[]{:S(2)}, u32[]{:S(2)}) collective-permute-start(bf16[128,1152]{1,0:T(8,128)(2,1)S(1)} %collective-permute-done.10.rest_5_), channel_id=1, source_target_pairs={{0,8},{2,10},{4,0},{6,2},{8,16},{10,18},{12,4},{14,6},{16,24},{18,... | collective-permute-start | bytes 884744 | tf_op jit(solution)/shard_map/ppermute | solution.py:56
  26.6 3.3 %collective-permute-done.6.rest_9_ = bf16[128,1152]{1,0:T(8,128)(2,1)S(1)} collective-permute-done((bf16[128,1152]{1,0:T(8,128)(2,1)S(1)}, bf16[128,1152]{1,0:T(8,128)(2,1)S(1)}, u32[]{:S(2)}, u32[]{:S(2)}) %collective-permute-start.6) | collective-permute-done | bytes 294944 | tf_op jit(solution)/shard_map/ppermute | solution.py:56
  29.9 2.8 %collective-permute-done.4.rest_7_ = bf16[128,1152]{1,0:T(8,128)(2,1)S(1)} collective-permute-done((bf16[128,1152]{1,0:T(8,128)(2,1)S(1)}, bf16[128,1152]{1,0:T(8,128)(2,1)S(1)}, u32[]{:S(2)}, u32[]{:S(2)}) %collective-permute-start.4) | collective-permute-done | bytes 294944 | tf_op jit(solution)/shard_map/ppermute | solution.py:56
  33.2 1.7 %collective-permute-start.12 = (bf16[128,1152]{1,0:T(8,128)(2,1)S(1)}, bf16[128,1152]{1,0:T(8,128)(2,1)}, u32[]{:S(2)}, u32[]{:S(2)}) collective-permute-start(bf16[128,1152]{1,0:T(8,128)(2,1)S(1)} %collective-permute-done.2.rest_3_), channel_id=1, source_target_pairs={{0,8},{2,10},{4,0},{6,2},{8,16},{10,18},{12,4},{14,6},{16,24},{18,... | collective-permute-start | bytes 884744 | tf_op jit(solution)/shard_map/ppermute | solution.py:56
  35.0 0.7 constant_dynamic-slice_fusion
  35.6 6.5 %collective-permute-done.7.rest_12_ = bf16[128,1152]{1,0:T(8,128)(2,1)S(1)} collective-permute-done((bf16[128,1152]{1,0:T(8,128)(2,1)S(1)}, bf16[128,1152]{1,0:T(8,128)(2,1)S(1)}, u32[]{:S(2)}, u32[]{:S(2)}) %collective-permute-start.7) | collective-permute-done | bytes 294944 | tf_op jit(solution)/shard_map/ppermute | solution.py:56
  42.3 2.0 %collective-permute-start.13 = (bf16[128,1152]{1,0:T(8,128)(2,1)}, bf16[128,1152]{1,0:T(8,128)(2,1)S(1)}, u32[]{:S(2)}, u32[]{:S(2)}) collective-permute-start(bf16[128,1152]{1,0:T(8,128)(2,1)} %collective-permute-done.12.rest_11_), channel_id=1, source_target_pairs={{0,8},{2,10},{4,0},{6,2},{8,16},{10,18},{12,4},{14,6},{16,24},{18,... | collective-permute-start | bytes 884744 | tf_op jit(solution)/shard_map/ppermute | solution.py:56
  44.3 3.7 %anchor_rows.2.rest_3_ = bf16[512,1152]{1,0:T(8,128)(2,1)S(1)} custom-call(s32[16]{0:T(128)S(1)} %get-tuple-element.77.bases, s32[512,8]{1,0:T(8,128)S(1)} %copy-done, bf16[128,1152]{1,0:T(8,128)(2,1)S(1)} %copy-done.1, bf16[128,1152]{1,0:T(8,128)(2,1)S(1)} %collective-permute-done.rest_1_, bf16[128,1152]{1,0:T(8,128)(2,1)S(1)} %collective-permute-done.1.rest_2_, ...), custom_call_target="tpu_custom_call" | custom-call | flops 1962934272 | bytes 6193152 | tf_op jit(solution)/shard_map/anchor_rows/pallas_call | solution.py:180
  48.0 1.3 %collective-permute-done.13.rest_1_.rest_14_ = bf16[128,1152]{1,0:T(8,128)(2,1)S(1)} collective-permute-done((bf16[128,1152]{1,0:T(8,128)(2,1)}, bf16[128,1152]{1,0:T(8,128)(2,1)S(1)}, u32[]{:S(2)}, u32[]{:S(2)}) %collective-permute-start.13) | collective-permute-done | bytes 294944 | tf_op jit(solution)/shard_map/ppermute | solution.py:56
  49.3 1.4 %anchor_rows.3.anchor = bf16[512,1152]{1,0:T(8,128)(2,1)S(1)} custom-call(s32[16]{0:T(128)S(1)} %get-tuple-element.77.bases, s32[512,8]{1,0:T(8,128)S(1)} %copy-done, bf16[128,1152]{1,0:T(8,128)(2,1)S(1)} %collective-permute-done.9.rest_0_.rest_13_, bf16[128,1152]{1,0:T(8,128)(2,1)S(1)} %collective-permute-done.13.rest_1_.rest_14_, ...), custom_call_target="tpu_custom_call" | custom-call | flops 452984832 | bytes 3244032 | tf_op jit(solution)/shard_map/anchor_rows/pallas_call | solution.py:180
  51.1 2.5 %collective-permute-done.15.other = bf16[512,1152]{1,0:T(8,128)(2,1)S(1)} collective-permute-done((bf16[512,1152]{1,0:T(8,128)(2,1)S(1)}, bf16[512,1152]{1,0:T(8,128)(2,1)S(1)}, u32[]{:S(2)}, u32[]{:S(2)}) %collective-permute-start.15) | collective-permute-done | bytes 1179680 | tf_op jit(solution)/shard_map/ppermute | solution.py:69
  53.7 6.3 %scores.1 = (f32[2048,512]{1,0:T(8,128)S(1)}, f32[2048,512]{1,0:T(8,128)S(1)}, f32[8,512]{1,0:T(8,128)S(1)}, f32[8,512]{1,0:T(8,128)S(1)}, bf16[512,128]{1,0:T(8,128)(2,1)S(1)}) custom-call(bf16[512,1152]{1,0:T(8,128)(2,1)S(1)} %anchor_rows.3.anchor, bf16[512,1152]{1,0:T(8,128)(2,1)S(1)} %collective-permute-done.15.other, ...), custom_call_target="tpu_custom_call" | custom-call | flops 2415919104 | bytes 13107200 | tf_op jit(solution)/shard_map/scores/pallas_call | solution.py:253
  60.1 1.0 %collective-permute-done.17.other = f32[8,512]{1,0:T(8,128)S(1)} collective-permute-done((f32[8,512]{1,0:T(8,128)S(1)}, f32[8,512]{1,0:T(8,128)S(1)}, u32[]{:S(2)}, u32[]{:S(2)}) %collective-permute-start.17) | collective-permute-done | bytes 16416 | tf_op jit(solution)/shard_map/ppermute | solution.py:69
  61.2 2.8 %gradients.1 = (f32[1,512]{1,0:T(1,128)}, f32[512,128]{1,0:T(8,128)S(1)}, bf16[4,128,128]{2,1,0:T(8,128)(2,1)S(1)}, bf16[4,128,128]{2,1,0:T(8,128)(2,1)S(1)}, bf...) custom-call(s32[16]{0:T(128)S(1)} %get-tuple-element.78.order, f32[2048,512]{1,0:T(8,128)S(1)} %get-tuple-element.60.t_in, ...), custom_call_target="tpu_custom_call" | custom-call | flops 536870912 | bytes 8388608 | tf_op jit(solution)/shard_map/gradients/pallas_call | solution.py:322
  64.1 3.4 %collective-permute-start.20 = (bf16[4,128,128]{2,1,0:T(8,128)(2,1)S(1)}, bf16[4,128,128]{2,1,0:T(8,128)(2,1)S(1)}, u32[]{:S(2)}, u32[]{:S(2)}) collective-permute-start(bf16[4,128,128]{2,1,0:T(8,128)(2,1)S(1)} %get-tuple-element.69), channel_id=1, source_target_pairs={{0,6},{2,4},{4,2},{6,0},{8,14},{10,12},{12,10},{14,8},{16,22},{18,... | collective-permute-start | bytes 393224 | tf_op jit(solution)/shard_map/ppermute | solution.py:366
  68.1 0.7 add.34
  68.8 3.0 %collective-permute-done.20.refs_3_ = bf16[4,128,128]{2,1,0:T(8,128)(2,1)S(1)} collective-permute-done((bf16[4,128,128]{2,1,0:T(8,128)(2,1)S(1)}, bf16[4,128,128]{2,1,0:T(8,128)(2,1)S(1)}, u32[]{:S(2)}, u32[]{:S(2)}) %collective-permute-start.20) | collective-permute-done | bytes 131104 | tf_op jit(solution)/shard_map/ppermute | solution.py:366
  71.8 1.9 %collective-permute-done.18.refs_1_ = bf16[4,128,128]{2,1,0:T(8,128)(2,1)S(1)} collective-permute-done((bf16[4,128,128]{2,1,0:T(8,128)(2,1)S(1)}, bf16[4,128,128]{2,1,0:T(8,128)(2,1)S(1)}, u32[]{:S(2)}, u32[]{:S(2)}) %collective-permute-start.18) | collective-permute-done | bytes 131104 | tf_op jit(solution)/shard_map/ppermute | solution.py:366
  74.4 2.1 %collective-permute-start.22 = (bf16[128,128]{1,0:T(8,128)(2,1)S(1)}, bf16[128,128]{1,0:T(8,128)(2,1)S(1)}, u32[]{:S(2)}, u32[]{:S(2)}) collective-permute-start(bf16[128,128]{1,0:T(8,128)(2,1)S(1)} %get-tuple-element.73), channel_id=1, source_target_pairs={{0,8},{2,10},{4,12},{6,14},{8,16},{10,18},{12,20},{14,22},{16,24},... | collective-permute-start | bytes 98312 | tf_op jit(solution)/shard_map/ppermute | solution.py:372
  76.5 2.2 %collective-permute-start.23 = (bf16[128,128]{1,0:T(8,128)(2,1)S(1)}, bf16[128,128]{1,0:T(8,128)(2,1)S(1)}, u32[]{:S(2)}, u32[]{:S(2)}) collective-permute-start(bf16[128,128]{1,0:T(8,128)(2,1)S(1)} %get-tuple-element.74), channel_id=1, source_target_pairs={{0,16},{2,18},{4,20},{6,22},{8,24},{10,26},{12,28},{14,30},{16,0},... | collective-permute-start | bytes 98312 | tf_op jit(solution)/shard_map/ppermute | solution.py:372
  78.6 1.3 %collective-permute-start.24 = (bf16[128,128]{1,0:T(8,128)(2,1)S(1)}, bf16[128,128]{1,0:T(8,128)(2,1)S(1)}, u32[]{:S(2)}, u32[]{:S(2)}) collective-permute-start(bf16[128,128]{1,0:T(8,128)(2,1)S(1)} %get-tuple-element.75), channel_id=1, source_target_pairs={{0,24},{2,26},{4,28},{6,30},{8,0},{10,2},{12,4},{14,6},{16,8},{18,... | collective-permute-start | bytes 98312 | tf_op jit(solution)/shard_map/ppermute | solution.py:372
  80.2 1.2 %collective-permute-done.23 = bf16[128,128]{1,0:T(8,128)(2,1)S(1)} collective-permute-done((bf16[128,128]{1,0:T(8,128)(2,1)S(1)}, bf16[128,128]{1,0:T(8,128)(2,1)S(1)}, u32[]{:S(2)}, u32[]{:S(2)}) %collective-permute-start.23) | collective-permute-done | bytes 32800 | tf_op jit(solution)/shard_map/ppermute | solution.py:372
  81.5 1.1 %collective-permute-done.24 = bf16[128,128]{1,0:T(8,128)(2,1)S(1)} collective-permute-done((bf16[128,128]{1,0:T(8,128)(2,1)S(1)}, bf16[128,128]{1,0:T(8,128)(2,1)S(1)}, u32[]{:S(2)}, u32[]{:S(2)}) %collective-permute-start.24) | collective-permute-done | bytes 32800 | tf_op jit(solution)/shard_map/ppermute | solution.py:372
  (36 shorter events, 5.5 us)
Async XLA Ops:
  2.7 11.9 %collective-permute-start.2 = (bf16[128,1152]{1,0:T(8,128)(2,1)}, bf16[128,1152]{1,0:T(8,128)(2,1)S(1)}, u32[]{:S(2)}, u32[]{:S(2)}) collective-permute-start(bf16[128,1152]{1,0:T(8,128)(2,1)} %get-tuple-element.42.rest_0_), channel_id=1, source_target_pairs={{0,2},{2,0},{4,6},{6,4},{8,10},{10,8},{12,14},{14,12},{16,18},{18,... | collective-permute-start | bytes 884744 | tf_op jit(solution)/shard_map/ppermute | solution.py:56
  5.6 9.0 %collective-permute-start.1 = (bf16[128,1152]{1,0:T(8,128)(2,1)}, bf16[128,1152]{1,0:T(8,128)(2,1)S(1)}, u32[]{:S(2)}, u32[]{:S(2)}) collective-permute-start(bf16[128,1152]{1,0:T(8,128)(2,1)} %get-tuple-element.42.rest_0_), channel_id=1, source_target_pairs={{0,8},{2,10},{4,0},{6,2},{8,16},{10,18},{12,4},{14,6},{16,24},{18,... | collective-permute-start | bytes 884744 | tf_op jit(solution)/shard_map/ppermute | solution.py:56
  7.2 8.4 %collective-permute-start = (bf16[128,1152]{1,0:T(8,128)(2,1)}, bf16[128,1152]{1,0:T(8,128)(2,1)S(1)}, u32[]{:S(2)}, u32[]{:S(2)}) collective-permute-start(bf16[128,1152]{1,0:T(8,128)(2,1)} %get-tuple-element.42.rest_0_), channel_id=1, source_target_pairs={{0,4},{2,6},{4,12},{6,14},{8,0},{10,2},{12,20},{14,22},{16,8},{18,... | collective-permute-start | bytes 884744 | tf_op jit(solution)/shard_map/ppermute | solution.py:56
  7.7 36.6 %copy-start = (s32[512,8]{1,0:T(8,128)S(1)}, s32[512,8]{1,0:T(8,128)}, u32[]{:S(2)}) copy-start(s32[512,8]{1,0:T(8,128)} %get-tuple-element.40.cols) | copy-start | bytes 49156
  7.7 36.6 %copy-start.1 = (bf16[128,1152]{1,0:T(8,128)(2,1)S(1)}, bf16[128,1152]{1,0:T(8,128)(2,1)}, u32[]{:S(2)}) copy-start(bf16[128,1152]{1,0:T(8,128)(2,1)} %get-tuple-element.42.rest_0_) | copy-start | bytes 884740
  15.6 7.3 %collective-permute-start.5 = (bf16[128,1152]{1,0:T(8,128)(2,1)S(1)}, bf16[128,1152]{1,0:T(8,128)(2,1)S(1)}, u32[]{:S(2)}, u32[]{:S(2)}) collective-permute-start(bf16[128,1152]{1,0:T(8,128)(2,1)S(1)} %collective-permute-done.rest_1_), channel_id=1, source_target_pairs={{0,2},{2,0},{4,6},{6,4},{8,10},{10,8},{12,14},{14,12},{16,18},{18,... | collective-permute-start | bytes 884744 | tf_op jit(solution)/shard_map/ppermute | solution.py:56
  16.1 7.0 %collective-permute-start.3 = (bf16[128,1152]{1,0:T(8,128)(2,1)S(1)}, bf16[128,1152]{1,0:T(8,128)(2,1)S(1)}, u32[]{:S(2)}, u32[]{:S(2)}) collective-permute-start(bf16[128,1152]{1,0:T(8,128)(2,1)S(1)} %collective-permute-done.rest_1_), channel_id=1, source_target_pairs={{0,4},{2,6},{4,12},{6,14},{8,0},{10,2},{12,20},{14,22},{16,8},{18,... | collective-permute-start | bytes 884744 | tf_op jit(solution)/shard_map/ppermute | solution.py:56
  16.7 8.9 %collective-permute-start.10 = (bf16[128,1152]{1,0:T(8,128)(2,1)S(1)}, bf16[128,1152]{1,0:T(8,128)(2,1)S(1)}, u32[]{:S(2)}, u32[]{:S(2)}) collective-permute-start(bf16[128,1152]{1,0:T(8,128)(2,1)S(1)} %collective-permute-done.1.rest_2_), channel_id=1, source_target_pairs={{0,8},{2,10},{4,0},{6,2},{8,16},{10,18},{12,4},{14,6},{16,24},{18,... | collective-permute-start | bytes 884744 | tf_op jit(solution)/shard_map/ppermute | solution.py:56
  23.1 6.8 %collective-permute-start.6 = (bf16[128,1152]{1,0:T(8,128)(2,1)S(1)}, bf16[128,1152]{1,0:T(8,128)(2,1)S(1)}, u32[]{:S(2)}, u32[]{:S(2)}) collective-permute-start(bf16[128,1152]{1,0:T(8,128)(2,1)S(1)} %collective-permute-done.3.rest_4_), channel_id=1, source_target_pairs={{0,2},{2,0},{4,6},{6,4},{8,10},{10,8},{12,14},{14,12},{16,18},{18,... | collective-permute-start | bytes 884744 | tf_op jit(solution)/shard_map/ppermute | solution.py:56
  24.6 8.0 %collective-permute-start.4 = (bf16[128,1152]{1,0:T(8,128)(2,1)S(1)}, bf16[128,1152]{1,0:T(8,128)(2,1)S(1)}, u32[]{:S(2)}, u32[]{:S(2)}) collective-permute-start(bf16[128,1152]{1,0:T(8,128)(2,1)S(1)} %collective-permute-done.3.rest_4_), channel_id=1, source_target_pairs={{0,4},{2,6},{4,12},{6,14},{8,0},{10,2},{12,20},{14,22},{16,8},{18,... | collective-permute-start | bytes 884744 | tf_op jit(solution)/shard_map/ppermute | solution.py:56
  25.6 7.7 %collective-permute-start.11 = (bf16[128,1152]{1,0:T(8,128)(2,1)S(1)}, bf16[128,1152]{1,0:T(8,128)(2,1)S(1)}, u32[]{:S(2)}, u32[]{:S(2)}) collective-permute-start(bf16[128,1152]{1,0:T(8,128)(2,1)S(1)} %collective-permute-done.10.rest_5_), channel_id=1, source_target_pairs={{0,8},{2,10},{4,0},{6,2},{8,16},{10,18},{12,4},{14,6},{16,24},{18,... | collective-permute-start | bytes 884744 | tf_op jit(solution)/shard_map/ppermute | solution.py:56
  32.7 9.5 %collective-permute-start.7 = (bf16[128,1152]{1,0:T(8,128)(2,1)S(1)}, bf16[128,1152]{1,0:T(8,128)(2,1)S(1)}, u32[]{:S(2)}, u32[]{:S(2)}) collective-permute-start(bf16[128,1152]{1,0:T(8,128)(2,1)S(1)} %collective-permute-done.4.rest_7_), channel_id=1, source_target_pairs={{0,2},{2,0},{4,6},{6,4},{8,10},{10,8},{12,14},{14,12},{16,18},{18,... | collective-permute-start | bytes 884744 | tf_op jit(solution)/shard_map/ppermute | solution.py:56
  32.7 9.5 %collective-permute-start.8 = (bf16[128,1152]{1,0:T(8,128)(2,1)S(1)}, bf16[128,1152]{1,0:T(8,128)(2,1)}, u32[]{:S(2)}, u32[]{:S(2)}) collective-permute-start(bf16[128,1152]{1,0:T(8,128)(2,1)S(1)} %collective-permute-done.4.rest_7_), channel_id=1, source_target_pairs={{0,4},{2,6},{4,12},{6,14},{8,0},{10,2},{12,20},{14,22},{16,8},{18,... | collective-permute-start | bytes 884744 | tf_op jit(solution)/shard_map/ppermute | solution.py:56
  33.2 9.0 %collective-permute-start.12 = (bf16[128,1152]{1,0:T(8,128)(2,1)S(1)}, bf16[128,1152]{1,0:T(8,128)(2,1)}, u32[]{:S(2)}, u32[]{:S(2)}) collective-permute-start(bf16[128,1152]{1,0:T(8,128)(2,1)S(1)} %collective-permute-done.2.rest_3_), channel_id=1, source_target_pairs={{0,8},{2,10},{4,0},{6,2},{8,16},{10,18},{12,4},{14,6},{16,24},{18,... | collective-permute-start | bytes 884744 | tf_op jit(solution)/shard_map/ppermute | solution.py:56
  42.1 7.2 %collective-permute-start.14 = (bf16[128,1152]{1,0:T(8,128)(2,1)S(1)}, bf16[128,1152]{1,0:T(8,128)(2,1)S(1)}, u32[]{:S(2)}, u32[]{:S(2)}) collective-permute-start(bf16[128,1152]{1,0:T(8,128)(2,1)S(1)} %collective-permute-done.11.rest_8_), channel_id=1, source_target_pairs={{0,2},{2,0},{4,6},{6,4},{8,10},{10,8},{12,14},{14,12},{16,18},{18,... | collective-permute-start | bytes 884744 | tf_op jit(solution)/shard_map/ppermute | solution.py:56
  42.1 7.2 %collective-permute-start.9 = (bf16[128,1152]{1,0:T(8,128)(2,1)S(1)}, bf16[128,1152]{1,0:T(8,128)(2,1)S(1)}, u32[]{:S(2)}, u32[]{:S(2)}) collective-permute-start(bf16[128,1152]{1,0:T(8,128)(2,1)S(1)} %collective-permute-done.7.rest_12_), channel_id=1, source_target_pairs={{0,4},{2,6},{4,12},{6,14},{8,0},{10,2},{12,20},{14,22},{16,8},{18,... | collective-permute-start | bytes 884744 | tf_op jit(solution)/shard_map/ppermute | solution.py:56
  42.3 7.1 %collective-permute-start.13 = (bf16[128,1152]{1,0:T(8,128)(2,1)}, bf16[128,1152]{1,0:T(8,128)(2,1)S(1)}, u32[]{:S(2)}, u32[]{:S(2)}) collective-permute-start(bf16[128,1152]{1,0:T(8,128)(2,1)} %collective-permute-done.12.rest_11_), channel_id=1, source_target_pairs={{0,8},{2,10},{4,0},{6,2},{8,16},{10,18},{12,4},{14,6},{16,24},{18,... | collective-permute-start | bytes 884744 | tf_op jit(solution)/shard_map/ppermute | solution.py:56
  44.3 6.5 %collective-permute-start.16 = (bf16[512,1152]{1,0:T(8,128)(2,1)}, bf16[512,1152]{1,0:T(8,128)(2,1)S(1)}, u32[]{:S(2)}, u32[]{:S(2)}) collective-permute-start(bf16[512,1152]{1,0:T(8,128)(2,1)} %relation_rows.1), channel_id=1, source_target_pairs={{0,1},{1,0},{2,3},{3,2},{4,5},{5,4},{6,7},{7,6},{8,9},{9,8},{10,11... | collective-permute-start | bytes 3538952 | tf_op jit(solution)/shard_map/ppermute | solution.py:69
  48.0 2.8 %copy-start.2 = (bf16[512,1152]{1,0:T(8,128)(2,1)S(1)}, bf16[512,1152]{1,0:T(8,128)(2,1)}, u32[]{:S(2)}) copy-start(bf16[512,1152]{1,0:T(8,128)(2,1)} %relation_rows.1) | copy-start | bytes 3538948
  50.7 2.9 %collective-permute-start.15 = (bf16[512,1152]{1,0:T(8,128)(2,1)S(1)}, bf16[512,1152]{1,0:T(8,128)(2,1)S(1)}, u32[]{:S(2)}, u32[]{:S(2)}) collective-permute-start(bf16[512,1152]{1,0:T(8,128)(2,1)S(1)} %anchor_rows.3.anchor), channel_id=1, source_target_pairs={{0,1},{1,0},{2,3},{3,2},{4,5},{5,4},{6,7},{7,6},{8,9},{9,8},{10,11... | collective-permute-start | bytes 3538952 | tf_op jit(solution)/shard_map/ppermute | solution.py:69
  60.0 1.2 %collective-permute-start.17 = (f32[8,512]{1,0:T(8,128)S(1)}, f32[8,512]{1,0:T(8,128)S(1)}, u32[]{:S(2)}, u32[]{:S(2)}) collective-permute-start(f32[8,512]{1,0:T(8,128)S(1)} %get-tuple-element.63.mine), channel_id=1, source_target_pairs={{0,1},{1,0},{2,3},{3,2},{4,5},{5,4},{6,7},{7,6},{8,9},{9,8},{10,11... | collective-permute-start | bytes 49160 | tf_op jit(solution)/shard_map/ppermute | solution.py:69
  64.0 4.1 %collective-permute-start.21 = (f32[512,128]{1,0:T(8,128)S(1)}, f32[512,128]{1,0:T(8,128)S(1)}, u32[]{:S(2)}, u32[]{:S(2)}) collective-permute-start(f32[512,128]{1,0:T(8,128)S(1)} %get-tuple-element.70), channel_id=1, source_target_pairs={{0,1},{1,0},{2,3},{3,2},{4,5},{5,4},{6,7},{7,6},{8,9},{9,8},{10,11... | collective-permute-start | bytes 786440 | tf_op jit(solution)/shard_map/ppermute | solution.py:69
  64.1 7.7 %collective-permute-start.20 = (bf16[4,128,128]{2,1,0:T(8,128)(2,1)S(1)}, bf16[4,128,128]{2,1,0:T(8,128)(2,1)S(1)}, u32[]{:S(2)}, u32[]{:S(2)}) collective-permute-start(bf16[4,128,128]{2,1,0:T(8,128)(2,1)S(1)} %get-tuple-element.69), channel_id=1, source_target_pairs={{0,6},{2,4},{4,2},{6,0},{8,14},{10,12},{12,10},{14,8},{16,22},{18,... | collective-permute-start | bytes 393224 | tf_op jit(solution)/shard_map/ppermute | solution.py:366
  67.5 6.3 %collective-permute-start.18 = (bf16[4,128,128]{2,1,0:T(8,128)(2,1)S(1)}, bf16[4,128,128]{2,1,0:T(8,128)(2,1)S(1)}, u32[]{:S(2)}, u32[]{:S(2)}) collective-permute-start(bf16[4,128,128]{2,1,0:T(8,128)(2,1)S(1)} %get-tuple-element.67), channel_id=1, source_target_pairs={{0,2},{2,0},{4,6},{6,4},{8,10},{10,8},{12,14},{14,12},{16,18},{18,... | collective-permute-start | bytes 393224 | tf_op jit(solution)/shard_map/ppermute | solution.py:366
  67.5 6.8 %collective-permute-start.19 = (bf16[4,128,128]{2,1,0:T(8,128)(2,1)S(1)}, bf16[4,128,128]{2,1,0:T(8,128)(2,1)S(1)}, u32[]{:S(2)}, u32[]{:S(2)}) collective-permute-start(bf16[4,128,128]{2,1,0:T(8,128)(2,1)S(1)} %get-tuple-element.68), channel_id=1, source_target_pairs={{0,4},{2,6},{4,0},{6,2},{8,12},{10,14},{12,8},{14,10},{16,20},{18,... | collective-permute-start | bytes 393224 | tf_op jit(solution)/shard_map/ppermute | solution.py:366
  74.4 5.9 %collective-permute-start.22 = (bf16[128,128]{1,0:T(8,128)(2,1)S(1)}, bf16[128,128]{1,0:T(8,128)(2,1)S(1)}, u32[]{:S(2)}, u32[]{:S(2)}) collective-permute-start(bf16[128,128]{1,0:T(8,128)(2,1)S(1)} %get-tuple-element.73), channel_id=1, source_target_pairs={{0,8},{2,10},{4,12},{6,14},{8,16},{10,18},{12,20},{14,22},{16,24},... | collective-permute-start | bytes 98312 | tf_op jit(solution)/shard_map/ppermute | solution.py:372
  76.5 5.0 %collective-permute-start.23 = (bf16[128,128]{1,0:T(8,128)(2,1)S(1)}, bf16[128,128]{1,0:T(8,128)(2,1)S(1)}, u32[]{:S(2)}, u32[]{:S(2)}) collective-permute-start(bf16[128,128]{1,0:T(8,128)(2,1)S(1)} %get-tuple-element.74), channel_id=1, source_target_pairs={{0,16},{2,18},{4,20},{6,22},{8,24},{10,26},{12,28},{14,30},{16,0},... | collective-permute-start | bytes 98312 | tf_op jit(solution)/shard_map/ppermute | solution.py:372
  78.6 3.9 %collective-permute-start.24 = (bf16[128,128]{1,0:T(8,128)(2,1)S(1)}, bf16[128,128]{1,0:T(8,128)(2,1)S(1)}, u32[]{:S(2)}, u32[]{:S(2)}) collective-permute-start(bf16[128,128]{1,0:T(8,128)(2,1)S(1)} %get-tuple-element.75), channel_id=1, source_target_pairs={{0,24},{2,26},{4,28},{6,30},{8,0},{10,2},{12,4},{14,6},{16,8},{18,... | collective-permute-start | bytes 98312 | tf_op jit(solution)/shard_map/ppermute | solution.py:372

commit v5 on v3

--- a/solution.py
+++ b/solution.py
@@ -155,7 +155,7 @@
     return jnp.concatenate([shard[:, columns] for shard in shards], axis=0)
 
 
-def anchor_kernel(count, own, has_acc, bases, cols, *rest):
+def anchor_kernel(count, first_slot, own, has_acc, bases, cols, *rest):
     acc_in, rest = (rest[0], rest[1:]) if has_acc else (None, rest)
     shards, out = rest[:count], rest[count]
     ids = cols[:, 0:1]
@@ -164,19 +164,19 @@
     total = None
     for first in range(0, count, group):
         last = min(count, first + group)
-        hot = jnp.concatenate([(ids - bases[j] == lane).astype(F32).astype(BF16) for j in range(first, last)], axis=1)
+        hot = jnp.concatenate([(ids - bases[first_slot + j] == lane).astype(F32).astype(BF16) for j in range(first, last)], axis=1)
         found = jnp.dot(hot, joined(shards[first:last], slice(None)), preferred_element_type=F32)
         total = found if total is None else total + found
     total = total.astype(BF16)
     out[...] = total + acc_in[...] if has_acc else total
 
 
-def anchor_rows(bases, cols, shards, acc, shape):
+def anchor_rows(bases, first_slot, cols, shards, acc, shape):
     own = shards[0].shape[0]
     q, count = cols.shape[0], len(shards)
     operands = [bases, cols] + ([] if acc is None else [acc]) + list(shards)
     return pl.pallas_call(
-        functools.partial(anchor_kernel, count, own, acc is not None),
+        functools.partial(anchor_kernel, count, first_slot, own, acc is not None),
         out_shape=jax.ShapeDtypeStruct((q, shape.total), BF16),
         in_specs=[SMEM, VMEM] + ([] if acc is None else [VMEM]) + [VMEM] * count,
         out_specs=VMEM,
@@ -414,11 +414,11 @@
             if number == len(steps) - 1:
                 counted = len(have)
                 names = held[:counted]
-                anchors = anchor_rows(bases, cols, [kept.get(h, have[h]) for h in names], None, shape)
+                anchors = anchor_rows(bases, 0, cols, [kept.get(h, have[h]) for h in names], None, shape)
             have.update(got)
         have.update(kept)
         shards = [have[h] for h in held]
-        mine = anchor_rows(bases[counted:], cols, shards[counted:], anchors, shape)
+        mine = anchor_rows(bases, counted, cols, shards[counted:], anchors, shape)
         far = 1
         while far < groups // 2:
             mine = mine + partner(mine, groups, far)

time: 82.6 us -> 83.9 us (1.016)
  Pallas kernels: 21.6 us -> 23.7 us
  waiting for transfers between devices: 33.5 us -> 32.1 us
    ppermute x15, waiting for transfers between devices: 21.8 us -> 20.1 us  [move(): return lax.ppermute(x, 'query', sorted(pairs))]
    pallas_call x1, Pallas kernels: 5.2 us -> 6.26 us  [scores(): pl.pallas_call(functools.partial(score_kernel, shape, own, n, chunk), out...]
  transfers between devices with their start and end apart: 25 -> 25, of which waited for: 14 -> 16; matrix products, arithmetic and copies ran while one was open for 2% -> 2% of each run, Pallas kernels for 14% -> 14%
where the time goes in v5:
time: 83.9 us; the launch traced here: 83.6 us
  waiting for transfers between devices  32.1 us (38%)
  starting transfers between devices  25.1 us (30%)
  Pallas kernels  23.7 us (28%)
  other arithmetic  1.38 us (2%)
    ppermute x15, waiting for transfers between devices, move(): return lax.ppermute(x, 'query', sorted(pairs))  20.1 us
    ppermute x15, starting transfers between devices, move(): return lax.ppermute(x, 'query', sorted(pairs))  15.2 us
    pallas_call x1, Pallas kernels, relation_rows(): pl.pallas_call(functools.partial(relation_kernel, shape, rel, block, cut)...  6.93 us
    pallas_call x1, Pallas kernels, scores(): pl.pallas_call(functools.partial(score_kernel, shape, own, n, chunk), out...  6.26 us
    ppermute x3, starting transfers between devices, reduce_blocks(): total = total + lax.ppermute(sums[e], 'query', pairs).astype(F32)  5.52 us
    ppermute x3, waiting for transfers between devices, reduce_blocks(): lax.ppermute(blocks[d], 'query', [(i, i ^ d) for i in range(n)])  5.51 us
    pallas_call x2, Pallas kernels, anchor_rows(): pl.pallas_call(functools.partial(anchor_kernel, count, first_slot, own, a...  5.12 us
    ppermute x3, starting transfers between devices, reduce_blocks(): lax.ppermute(blocks[d], 'query', [(i, i ^ d) for i in range(n)])  3.94 us
  transfers between devices with their start and end apart: 25, of which 16 were waited for; matrix products, arithmetic and copies ran while one was open for 2% of the time, Pallas kernels for 14%

profile of v5, /device:TPU:0, one launch (start us, length us, event | category | flops | bytes accessed | tf_op | source)
XLA Modules:
  0.0 83.6 jit_solution(2841547859136639116)
XLA Ops:
  0.6 2.0 %pack_rows.1 = (bf16[128,1152]{1,0:T(8,128)(2,1)}, s32[512,8]{1,0:T(8,128)}) custom-call(bf16[1000,128]{1,0:T(8,128)(2,1)} %bitcast.12, bf16[128,128]{1,0:T(8,128)(2,1)} %student.2, s32[1,512]{1,0:T(1,128)} %bitcast.13, s32[1,512]{1,0:T(1,128)} %bitcast.14, s32[1,512]{1,0:T(1,128)} %bitcast.15), custom_call_target="tpu_custom_call" | custom-call | tf_op jit(solution)/shard_map/pack_rows/pallas_call | solution.py:97
  2.7 2.9 %collective-permute-start.2 = (bf16[128,1152]{1,0:T(8,128)(2,1)}, bf16[128,1152]{1,0:T(8,128)(2,1)S(1)}, u32[]{:S(2)}, u32[]{:S(2)}) collective-permute-start(bf16[128,1152]{1,0:T(8,128)(2,1)} %get-tuple-element.41.rest_0_), channel_id=1, source_target_pairs={{0,2},{2,0},{4,6},{6,4},{8,10},{10,8},{12,14},{14,12},{16,18},{18,... | collective-permute-start | bytes 884744 | tf_op jit(solution)/shard_map/ppermute | solution.py:56
  5.6 1.6 %collective-permute-start.1 = (bf16[128,1152]{1,0:T(8,128)(2,1)}, bf16[128,1152]{1,0:T(8,128)(2,1)S(1)}, u32[]{:S(2)}, u32[]{:S(2)}) collective-permute-start(bf16[128,1152]{1,0:T(8,128)(2,1)} %get-tuple-element.41.rest_0_), channel_id=1, source_target_pairs={{0,8},{2,10},{4,0},{6,2},{8,16},{10,18},{12,4},{14,6},{16,24},{18,... | collective-permute-start | bytes 884744 | tf_op jit(solution)/shard_map/ppermute | solution.py:56
  7.7 6.9 %relation_rows.1.relation = bf16[512,1152]{1,0:T(8,128)(2,1)} custom-call(s32[1]{0:T(128)} %bitcast.6.base, s32[512,8]{1,0:T(8,128)} %get-tuple-element.39.cols, bf16[1000,4131]{1,0:T(8,128)(2,1)} %bitcast.11, bf16[4131,128]{1,0:T(8,128)(2,1)} %student.3), custom_call_target="tpu_custom_call" | custom-call | flops 2359296000 | bytes 4608000 | tf_op jit(solution)/shard_map/relation_rows/pallas_call | solution.py:133
  14.6 1.0 %collective-permute-done.rest_1_ = bf16[128,1152]{1,0:T(8,128)(2,1)S(1)} collective-permute-done((bf16[128,1152]{1,0:T(8,128)(2,1)}, bf16[128,1152]{1,0:T(8,128)(2,1)S(1)}, u32[]{:S(2)}, u32[]{:S(2)}) %collective-permute-start) | collective-permute-done | bytes 294944 | tf_op jit(solution)/shard_map/ppermute | solution.py:56
  16.7 1.4 %collective-permute-start.4 = (bf16[128,1152]{1,0:T(8,128)(2,1)S(1)}, bf16[128,1152]{1,0:T(8,128)(2,1)S(1)}, u32[]{:S(2)}, u32[]{:S(2)}) collective-permute-start(bf16[128,1152]{1,0:T(8,128)(2,1)S(1)} %collective-permute-done.1.rest_2_), channel_id=1, source_target_pairs={{0,8},{2,10},{4,0},{6,2},{8,16},{10,18},{12,4},{14,6},{16,24},{18,... | collective-permute-start | bytes 884744 | tf_op jit(solution)/shard_map/ppermute | solution.py:56
  18.2 4.7 %collective-permute-done.5.rest_6_ = bf16[128,1152]{1,0:T(8,128)(2,1)S(1)} collective-permute-done((bf16[128,1152]{1,0:T(8,128)(2,1)S(1)}, bf16[128,1152]{1,0:T(8,128)(2,1)S(1)}, u32[]{:S(2)}, u32[]{:S(2)}) %collective-permute-start.5) | collective-permute-done | bytes 294944 | tf_op jit(solution)/shard_map/ppermute | solution.py:56
  23.1 1.5 %collective-permute-start.8 = (bf16[128,1152]{1,0:T(8,128)(2,1)S(1)}, bf16[128,1152]{1,0:T(8,128)(2,1)S(1)}, u32[]{:S(2)}, u32[]{:S(2)}) collective-permute-start(bf16[128,1152]{1,0:T(8,128)(2,1)S(1)} %collective-permute-done.3.rest_4_), channel_id=1, source_target_pairs={{0,2},{2,0},{4,6},{6,4},{8,10},{10,8},{12,14},{14,12},{16,18},{18,... | collective-permute-start | bytes 884744 | tf_op jit(solution)/shard_map/ppermute | solution.py:56
  24.6 1.0 %collective-permute-start.6 = (bf16[128,1152]{1,0:T(8,128)(2,1)S(1)}, bf16[128,1152]{1,0:T(8,128)(2,1)S(1)}, u32[]{:S(2)}, u32[]{:S(2)}) collective-permute-start(bf16[128,1152]{1,0:T(8,128)(2,1)S(1)} %collective-permute-done.3.rest_4_), channel_id=1, source_target_pairs={{0,4},{2,6},{4,12},{6,14},{8,0},{10,2},{12,20},{14,22},{16,8},{18,... | collective-permute-start | bytes 884744 | tf_op jit(solution)/shard_map/ppermute | solution.py:56
  25.6 1.1 %collective-permute-start.7 = (bf16[128,1152]{1,0:T(8,128)(2,1)S(1)}, bf16[128,1152]{1,0:T(8,128)(2,1)S(1)}, u32[]{:S(2)}, u32[]{:S(2)}) collective-permute-start(bf16[128,1152]{1,0:T(8,128)(2,1)S(1)} %collective-permute-done.4.rest_5_), channel_id=1, source_target_pairs={{0,8},{2,10},{4,0},{6,2},{8,16},{10,18},{12,4},{14,6},{16,24},{18,... | collective-permute-start | bytes 884744 | tf_op jit(solution)/shard_map/ppermute | solution.py:56
  26.6 3.3 %collective-permute-done.8.rest_9_ = bf16[128,1152]{1,0:T(8,128)(2,1)S(1)} collective-permute-done((bf16[128,1152]{1,0:T(8,128)(2,1)S(1)}, bf16[128,1152]{1,0:T(8,128)(2,1)S(1)}, u32[]{:S(2)}, u32[]{:S(2)}) %collective-permute-start.8) | collective-permute-done | bytes 294944 | tf_op jit(solution)/shard_map/ppermute | solution.py:56
  29.9 2.8 %collective-permute-done.6.rest_7_ = bf16[128,1152]{1,0:T(8,128)(2,1)S(1)} collective-permute-done((bf16[128,1152]{1,0:T(8,128)(2,1)S(1)}, bf16[128,1152]{1,0:T(8,128)(2,1)S(1)}, u32[]{:S(2)}, u32[]{:S(2)}) %collective-permute-start.6) | collective-permute-done | bytes 294944 | tf_op jit(solution)/shard_map/ppermute | solution.py:56
  33.2 1.7 %collective-permute-start.11 = (bf16[128,1152]{1,0:T(8,128)(2,1)S(1)}, bf16[128,1152]{1,0:T(8,128)(2,1)}, u32[]{:S(2)}, u32[]{:S(2)}) collective-permute-start(bf16[128,1152]{1,0:T(8,128)(2,1)S(1)} %collective-permute-done.2.rest_3_), channel_id=1, source_target_pairs={{0,8},{2,10},{4,0},{6,2},{8,16},{10,18},{12,4},{14,6},{16,24},{18,... | collective-permute-start | bytes 884744 | tf_op jit(solution)/shard_map/ppermute | solution.py:56
  35.0 0.7 constant_dynamic-slice_fusion
  35.6 6.5 %collective-permute-done.9.rest_12_ = bf16[128,1152]{1,0:T(8,128)(2,1)S(1)} collective-permute-done((bf16[128,1152]{1,0:T(8,128)(2,1)S(1)}, bf16[128,1152]{1,0:T(8,128)(2,1)S(1)}, u32[]{:S(2)}, u32[]{:S(2)}) %collective-permute-start.9) | collective-permute-done | bytes 294944 | tf_op jit(solution)/shard_map/ppermute | solution.py:56
  42.3 2.0 %collective-permute-start.13 = (bf16[128,1152]{1,0:T(8,128)(2,1)}, bf16[128,1152]{1,0:T(8,128)(2,1)S(1)}, u32[]{:S(2)}, u32[]{:S(2)}) collective-permute-start(bf16[128,1152]{1,0:T(8,128)(2,1)} %collective-permute-done.11.rest_11_), channel_id=1, source_target_pairs={{0,8},{2,10},{4,0},{6,2},{8,16},{10,18},{12,4},{14,6},{16,24},{18,... | collective-permute-start | bytes 884744 | tf_op jit(solution)/shard_map/ppermute | solution.py:56
  44.3 3.7 %anchor_rows.2.rest_0_ = bf16[512,1152]{1,0:T(8,128)(2,1)S(1)} custom-call(s32[16]{0:T(128)S(1)} %get-tuple-element.75.bases, s32[512,8]{1,0:T(8,128)S(1)} %copy-done.1, bf16[128,1152]{1,0:T(8,128)(2,1)S(1)} %copy-done.2, bf16[128,1152]{1,0:T(8,128)(2,1)S(1)} %collective-permute-done.rest_1_, bf16[128,1152]{1,0:T(8,128)(2,1)S(1)} %collective-permute-done.1.rest_2_, ...), custom_call_target="tpu_custom_call" | custom-call | flops 1962934272 | bytes 6193152 | tf_op jit(solution)/shard_map/anchor_rows/pallas_call | solution.py:178
  48.0 1.3 %collective-permute-done.13.rest_2_.rest_14_ = bf16[128,1152]{1,0:T(8,128)(2,1)S(1)} collective-permute-done((bf16[128,1152]{1,0:T(8,128)(2,1)}, bf16[128,1152]{1,0:T(8,128)(2,1)S(1)}, u32[]{:S(2)}, u32[]{:S(2)}) %collective-permute-start.13) | collective-permute-done | bytes 294944 | tf_op jit(solution)/shard_map/ppermute | solution.py:56
  49.3 1.4 %anchor_rows.3.mine = bf16[512,1152]{1,0:T(8,128)(2,1)S(1)} custom-call(s32[16]{0:T(128)S(1)} %get-tuple-element.75.bases, s32[512,8]{1,0:T(8,128)S(1)} %copy-done.1, bf16[512,1152]{1,0:T(8,128)(2,1)S(1)} %anchor_rows.2.rest_0_, bf16[128,1152]{1,0:T(8,128)(2,1)S(1)} %collective-permute-done.12.rest_1_.rest_13_, ...), custom_call_target="tpu_custom_call" | custom-call | flops 452984832 | bytes 3244032 | tf_op jit(solution)/shard_map/anchor_rows/pallas_call | solution.py:178
  50.8 2.8 %collective-permute-done.15.other = bf16[512,1152]{1,0:T(8,128)(2,1)S(1)} collective-permute-done((bf16[512,1152]{1,0:T(8,128)(2,1)S(1)}, bf16[512,1152]{1,0:T(8,128)(2,1)S(1)}, u32[]{:S(2)}, u32[]{:S(2)}) %collective-permute-start.15) | collective-permute-done | bytes 1179680 | tf_op jit(solution)/shard_map/ppermute | solution.py:69
  53.7 6.3 %scores.1 = (f32[2048,512]{1,0:T(8,128)S(1)}, f32[2048,512]{1,0:T(8,128)S(1)}, f32[8,512]{1,0:T(8,128)S(1)}, bf16[512,128]{1,0:T(8,128)(2,1)S(1)}) custom-call(bf16[512,1152]{1,0:T(8,128)(2,1)S(1)} %anchor_rows.3.mine, bf16[512,1152]{1,0:T(8,128)(2,1)S(1)} %collective-permute-done.15.other, bf16[512,1152]{1,0:T(8,128)(2,1)S(1)} %copy-done, ...), custom_call_target="tpu_custom_call" | custom-call | flops 2415919104 | bytes 13107200 | tf_op jit(solution)/shard_map/scores/pallas_call | solution.py:248
  60.1 1.0 %collective-permute-done.17.other = f32[8,512]{1,0:T(8,128)S(1)} collective-permute-done((f32[8,512]{1,0:T(8,128)S(1)}, f32[8,512]{1,0:T(8,128)S(1)}, u32[]{:S(2)}, u32[]{:S(2)}) %collective-permute-start.17) | collective-permute-done | bytes 16416 | tf_op jit(solution)/shard_map/ppermute | solution.py:69
  61.2 3.3 %gradients.1 = (f32[1,512]{1,0:T(1,128)}, f32[512,128]{1,0:T(8,128)S(1)}, bf16[4,128,128]{2,1,0:T(8,128)(2,1)S(1)}, bf16[4,128,128]{2,1,0:T(8,128)(2,1)S(1)}, bf...) custom-call(s32[16]{0:T(128)S(1)} %get-tuple-element.76.order, f32[2048,512]{1,0:T(8,128)S(1)} %get-tuple-element.59.t_in, ...), custom_call_target="tpu_custom_call" | custom-call | flops 536870912 | bytes 8388608 | tf_op jit(solution)/shard_map/gradients/pallas_call | solution.py:316
  64.6 3.4 %collective-permute-start.20 = (bf16[4,128,128]{2,1,0:T(8,128)(2,1)S(1)}, bf16[4,128,128]{2,1,0:T(8,128)(2,1)S(1)}, u32[]{:S(2)}, u32[]{:S(2)}) collective-permute-start(bf16[4,128,128]{2,1,0:T(8,128)(2,1)S(1)} %get-tuple-element.67), channel_id=1, source_target_pairs={{0,6},{2,4},{4,2},{6,0},{8,14},{10,12},{12,10},{14,8},{16,22},{18,... | collective-permute-start | bytes 393224 | tf_op jit(solution)/shard_map/ppermute | solution.py:360
  68.5 0.7 add.30
  69.3 3.0 %collective-permute-done.20.refs_3_ = bf16[4,128,128]{2,1,0:T(8,128)(2,1)S(1)} collective-permute-done((bf16[4,128,128]{2,1,0:T(8,128)(2,1)S(1)}, bf16[4,128,128]{2,1,0:T(8,128)(2,1)S(1)}, u32[]{:S(2)}, u32[]{:S(2)}) %collective-permute-start.20) | collective-permute-done | bytes 131104 | tf_op jit(solution)/shard_map/ppermute | solution.py:360
  72.3 1.9 %collective-permute-done.18.refs_1_ = bf16[4,128,128]{2,1,0:T(8,128)(2,1)S(1)} collective-permute-done((bf16[4,128,128]{2,1,0:T(8,128)(2,1)S(1)}, bf16[4,128,128]{2,1,0:T(8,128)(2,1)S(1)}, u32[]{:S(2)}, u32[]{:S(2)}) %collective-permute-start.18) | collective-permute-done | bytes 131104 | tf_op jit(solution)/shard_map/ppermute | solution.py:360
  74.8 2.1 %collective-permute-start.22 = (bf16[128,128]{1,0:T(8,128)(2,1)S(1)}, bf16[128,128]{1,0:T(8,128)(2,1)S(1)}, u32[]{:S(2)}, u32[]{:S(2)}) collective-permute-start(bf16[128,128]{1,0:T(8,128)(2,1)S(1)} %get-tuple-element.71), channel_id=1, source_target_pairs={{0,8},{2,10},{4,12},{6,14},{8,16},{10,18},{12,20},{14,22},{16,24},... | collective-permute-start | bytes 98312 | tf_op jit(solution)/shard_map/ppermute | solution.py:366
  76.9 2.2 %collective-permute-start.23 = (bf16[128,128]{1,0:T(8,128)(2,1)S(1)}, bf16[128,128]{1,0:T(8,128)(2,1)S(1)}, u32[]{:S(2)}, u32[]{:S(2)}) collective-permute-start(bf16[128,128]{1,0:T(8,128)(2,1)S(1)} %get-tuple-element.72), channel_id=1, source_target_pairs={{0,16},{2,18},{4,20},{6,22},{8,24},{10,26},{12,28},{14,30},{16,0},... | collective-permute-start | bytes 98312 | tf_op jit(solution)/shard_map/ppermute | solution.py:366
  79.1 1.3 %collective-permute-start.24 = (bf16[128,128]{1,0:T(8,128)(2,1)S(1)}, bf16[128,128]{1,0:T(8,128)(2,1)S(1)}, u32[]{:S(2)}, u32[]{:S(2)}) collective-permute-start(bf16[128,128]{1,0:T(8,128)(2,1)S(1)} %get-tuple-element.73), channel_id=1, source_target_pairs={{0,24},{2,26},{4,28},{6,30},{8,0},{10,2},{12,4},{14,6},{16,8},{18,... | collective-permute-start | bytes 98312 | tf_op jit(solution)/shard_map/ppermute | solution.py:366
  80.7 1.2 %collective-permute-done.23 = bf16[128,128]{1,0:T(8,128)(2,1)S(1)} collective-permute-done((bf16[128,128]{1,0:T(8,128)(2,1)S(1)}, bf16[128,128]{1,0:T(8,128)(2,1)S(1)}, u32[]{:S(2)}, u32[]{:S(2)}) %collective-permute-start.23) | collective-permute-done | bytes 32800 | tf_op jit(solution)/shard_map/ppermute | solution.py:366
  81.9 1.1 %collective-permute-done.24 = bf16[128,128]{1,0:T(8,128)(2,1)S(1)} collective-permute-done((bf16[128,128]{1,0:T(8,128)(2,1)S(1)}, bf16[128,128]{1,0:T(8,128)(2,1)S(1)}, u32[]{:S(2)}, u32[]{:S(2)}) %collective-permute-start.24) | collective-permute-done | bytes 32800 | tf_op jit(solution)/shard_map/ppermute | solution.py:366
  (35 shorter events, 5.2 us)
Async XLA Ops:
  2.7 11.9 %collective-permute-start.2 = (bf16[128,1152]{1,0:T(8,128)(2,1)}, bf16[128,1152]{1,0:T(8,128)(2,1)S(1)}, u32[]{:S(2)}, u32[]{:S(2)}) collective-permute-start(bf16[128,1152]{1,0:T(8,128)(2,1)} %get-tuple-element.41.rest_0_), channel_id=1, source_target_pairs={{0,2},{2,0},{4,6},{6,4},{8,10},{10,8},{12,14},{14,12},{16,18},{18,... | collective-permute-start | bytes 884744 | tf_op jit(solution)/shard_map/ppermute | solution.py:56
  5.6 9.0 %collective-permute-start.1 = (bf16[128,1152]{1,0:T(8,128)(2,1)}, bf16[128,1152]{1,0:T(8,128)(2,1)S(1)}, u32[]{:S(2)}, u32[]{:S(2)}) collective-permute-start(bf16[128,1152]{1,0:T(8,128)(2,1)} %get-tuple-element.41.rest_0_), channel_id=1, source_target_pairs={{0,8},{2,10},{4,0},{6,2},{8,16},{10,18},{12,4},{14,6},{16,24},{18,... | collective-permute-start | bytes 884744 | tf_op jit(solution)/shard_map/ppermute | solution.py:56
  7.2 8.4 %collective-permute-start = (bf16[128,1152]{1,0:T(8,128)(2,1)}, bf16[128,1152]{1,0:T(8,128)(2,1)S(1)}, u32[]{:S(2)}, u32[]{:S(2)}) collective-permute-start(bf16[128,1152]{1,0:T(8,128)(2,1)} %get-tuple-element.41.rest_0_), channel_id=1, source_target_pairs={{0,4},{2,6},{4,12},{6,14},{8,0},{10,2},{12,20},{14,22},{16,8},{18,... | collective-permute-start | bytes 884744 | tf_op jit(solution)/shard_map/ppermute | solution.py:56
  7.7 36.6 %copy-start.1 = (s32[512,8]{1,0:T(8,128)S(1)}, s32[512,8]{1,0:T(8,128)}, u32[]{:S(2)}) copy-start(s32[512,8]{1,0:T(8,128)} %get-tuple-element.39.cols) | copy-start | bytes 49156
  7.7 36.6 %copy-start.2 = (bf16[128,1152]{1,0:T(8,128)(2,1)S(1)}, bf16[128,1152]{1,0:T(8,128)(2,1)}, u32[]{:S(2)}) copy-start(bf16[128,1152]{1,0:T(8,128)(2,1)} %get-tuple-element.41.rest_0_) | copy-start | bytes 884740
  15.6 7.3 %collective-permute-start.5 = (bf16[128,1152]{1,0:T(8,128)(2,1)S(1)}, bf16[128,1152]{1,0:T(8,128)(2,1)S(1)}, u32[]{:S(2)}, u32[]{:S(2)}) collective-permute-start(bf16[128,1152]{1,0:T(8,128)(2,1)S(1)} %collective-permute-done.rest_1_), channel_id=1, source_target_pairs={{0,2},{2,0},{4,6},{6,4},{8,10},{10,8},{12,14},{14,12},{16,18},{18,... | collective-permute-start | bytes 884744 | tf_op jit(solution)/shard_map/ppermute | solution.py:56
  16.1 7.0 %collective-permute-start.3 = (bf16[128,1152]{1,0:T(8,128)(2,1)S(1)}, bf16[128,1152]{1,0:T(8,128)(2,1)S(1)}, u32[]{:S(2)}, u32[]{:S(2)}) collective-permute-start(bf16[128,1152]{1,0:T(8,128)(2,1)S(1)} %collective-permute-done.rest_1_), channel_id=1, source_target_pairs={{0,4},{2,6},{4,12},{6,14},{8,0},{10,2},{12,20},{14,22},{16,8},{18,... | collective-permute-start | bytes 884744 | tf_op jit(solution)/shard_map/ppermute | solution.py:56
  16.7 8.9 %collective-permute-start.4 = (bf16[128,1152]{1,0:T(8,128)(2,1)S(1)}, bf16[128,1152]{1,0:T(8,128)(2,1)S(1)}, u32[]{:S(2)}, u32[]{:S(2)}) collective-permute-start(bf16[128,1152]{1,0:T(8,128)(2,1)S(1)} %collective-permute-done.1.rest_2_), channel_id=1, source_target_pairs={{0,8},{2,10},{4,0},{6,2},{8,16},{10,18},{12,4},{14,6},{16,24},{18,... | collective-permute-start | bytes 884744 | tf_op jit(solution)/shard_map/ppermute | solution.py:56
  23.1 6.8 %collective-permute-start.8 = (bf16[128,1152]{1,0:T(8,128)(2,1)S(1)}, bf16[128,1152]{1,0:T(8,128)(2,1)S(1)}, u32[]{:S(2)}, u32[]{:S(2)}) collective-permute-start(bf16[128,1152]{1,0:T(8,128)(2,1)S(1)} %collective-permute-done.3.rest_4_), channel_id=1, source_target_pairs={{0,2},{2,0},{4,6},{6,4},{8,10},{10,8},{12,14},{14,12},{16,18},{18,... | collective-permute-start | bytes 884744 | tf_op jit(solution)/shard_map/ppermute | solution.py:56
  24.6 8.0 %collective-permute-start.6 = (bf16[128,1152]{1,0:T(8,128)(2,1)S(1)}, bf16[128,1152]{1,0:T(8,128)(2,1)S(1)}, u32[]{:S(2)}, u32[]{:S(2)}) collective-permute-start(bf16[128,1152]{1,0:T(8,128)(2,1)S(1)} %collective-permute-done.3.rest_4_), channel_id=1, source_target_pairs={{0,4},{2,6},{4,12},{6,14},{8,0},{10,2},{12,20},{14,22},{16,8},{18,... | collective-permute-start | bytes 884744 | tf_op jit(solution)/shard_map/ppermute | solution.py:56
  25.6 7.7 %collective-permute-start.7 = (bf16[128,1152]{1,0:T(8,128)(2,1)S(1)}, bf16[128,1152]{1,0:T(8,128)(2,1)S(1)}, u32[]{:S(2)}, u32[]{:S(2)}) collective-permute-start(bf16[128,1152]{1,0:T(8,128)(2,1)S(1)} %collective-permute-done.4.rest_5_), channel_id=1, source_target_pairs={{0,8},{2,10},{4,0},{6,2},{8,16},{10,18},{12,4},{14,6},{16,24},{18,... | collective-permute-start | bytes 884744 | tf_op jit(solution)/shard_map/ppermute | solution.py:56
  32.7 9.5 %collective-permute-start.9 = (bf16[128,1152]{1,0:T(8,128)(2,1)S(1)}, bf16[128,1152]{1,0:T(8,128)(2,1)S(1)}, u32[]{:S(2)}, u32[]{:S(2)}) collective-permute-start(bf16[128,1152]{1,0:T(8,128)(2,1)S(1)} %collective-permute-done.6.rest_7_), channel_id=1, source_target_pairs={{0,2},{2,0},{4,6},{6,4},{8,10},{10,8},{12,14},{14,12},{16,18},{18,... | collective-permute-start | bytes 884744 | tf_op jit(solution)/shard_map/ppermute | solution.py:56
  32.7 9.5 %collective-permute-start.10 = (bf16[128,1152]{1,0:T(8,128)(2,1)S(1)}, bf16[128,1152]{1,0:T(8,128)(2,1)}, u32[]{:S(2)}, u32[]{:S(2)}) collective-permute-start(bf16[128,1152]{1,0:T(8,128)(2,1)S(1)} %collective-permute-done.6.rest_7_), channel_id=1, source_target_pairs={{0,4},{2,6},{4,12},{6,14},{8,0},{10,2},{12,20},{14,22},{16,8},{18,... | collective-permute-start | bytes 884744 | tf_op jit(solution)/shard_map/ppermute | solution.py:56
  33.2 9.0 %collective-permute-start.11 = (bf16[128,1152]{1,0:T(8,128)(2,1)S(1)}, bf16[128,1152]{1,0:T(8,128)(2,1)}, u32[]{:S(2)}, u32[]{:S(2)}) collective-permute-start(bf16[128,1152]{1,0:T(8,128)(2,1)S(1)} %collective-permute-done.2.rest_3_), channel_id=1, source_target_pairs={{0,8},{2,10},{4,0},{6,2},{8,16},{10,18},{12,4},{14,6},{16,24},{18,... | collective-permute-start | bytes 884744 | tf_op jit(solution)/shard_map/ppermute | solution.py:56
  42.1 7.2 %collective-permute-start.14 = (bf16[128,1152]{1,0:T(8,128)(2,1)S(1)}, bf16[128,1152]{1,0:T(8,128)(2,1)S(1)}, u32[]{:S(2)}, u32[]{:S(2)}) collective-permute-start(bf16[128,1152]{1,0:T(8,128)(2,1)S(1)} %collective-permute-done.7.rest_8_), channel_id=1, source_target_pairs={{0,2},{2,0},{4,6},{6,4},{8,10},{10,8},{12,14},{14,12},{16,18},{18,... | collective-permute-start | bytes 884744 | tf_op jit(solution)/shard_map/ppermute | solution.py:56
  42.1 7.2 %collective-permute-start.12 = (bf16[128,1152]{1,0:T(8,128)(2,1)S(1)}, bf16[128,1152]{1,0:T(8,128)(2,1)S(1)}, u32[]{:S(2)}, u32[]{:S(2)}) collective-permute-start(bf16[128,1152]{1,0:T(8,128)(2,1)S(1)} %collective-permute-done.9.rest_12_), channel_id=1, source_target_pairs={{0,4},{2,6},{4,12},{6,14},{8,0},{10,2},{12,20},{14,22},{16,8},{18,... | collective-permute-start | bytes 884744 | tf_op jit(solution)/shard_map/ppermute | solution.py:56
  42.3 7.1 %collective-permute-start.13 = (bf16[128,1152]{1,0:T(8,128)(2,1)}, bf16[128,1152]{1,0:T(8,128)(2,1)S(1)}, u32[]{:S(2)}, u32[]{:S(2)}) collective-permute-start(bf16[128,1152]{1,0:T(8,128)(2,1)} %collective-permute-done.11.rest_11_), channel_id=1, source_target_pairs={{0,8},{2,10},{4,0},{6,2},{8,16},{10,18},{12,4},{14,6},{16,24},{18,... | collective-permute-start | bytes 884744 | tf_op jit(solution)/shard_map/ppermute | solution.py:56
  44.3 6.5 %collective-permute-start.16 = (bf16[512,1152]{1,0:T(8,128)(2,1)}, bf16[512,1152]{1,0:T(8,128)(2,1)S(1)}, u32[]{:S(2)}, u32[]{:S(2)}) collective-permute-start(bf16[512,1152]{1,0:T(8,128)(2,1)} %relation_rows.1.relation), channel_id=1, source_target_pairs={{0,1},{1,0},{2,3},{3,2},{4,5},{5,4},{6,7},{7,6},{8,9},{9,8},{10,11... | collective-permute-start | bytes 3538952 | tf_op jit(solution)/shard_map/ppermute | solution.py:69
  48.0 5.6 %copy-start = (bf16[512,1152]{1,0:T(8,128)(2,1)S(1)}, bf16[512,1152]{1,0:T(8,128)(2,1)}, u32[]{:S(2)}) copy-start(bf16[512,1152]{1,0:T(8,128)(2,1)} %relation_rows.1.relation) | copy-start | bytes 3538948
  50.7 2.9 %collective-permute-start.15 = (bf16[512,1152]{1,0:T(8,128)(2,1)S(1)}, bf16[512,1152]{1,0:T(8,128)(2,1)S(1)}, u32[]{:S(2)}, u32[]{:S(2)}) collective-permute-start(bf16[512,1152]{1,0:T(8,128)(2,1)S(1)} %anchor_rows.3.mine), channel_id=1, source_target_pairs={{0,1},{1,0},{2,3},{3,2},{4,5},{5,4},{6,7},{7,6},{8,9},{9,8},{10,11... | collective-permute-start | bytes 3538952 | tf_op jit(solution)/shard_map/ppermute | solution.py:69
  59.9 1.2 %collective-permute-start.17 = (f32[8,512]{1,0:T(8,128)S(1)}, f32[8,512]{1,0:T(8,128)S(1)}, u32[]{:S(2)}, u32[]{:S(2)}) collective-permute-start(f32[8,512]{1,0:T(8,128)S(1)} %get-tuple-element.61.mine), channel_id=1, source_target_pairs={{0,1},{1,0},{2,3},{3,2},{4,5},{5,4},{6,7},{7,6},{8,9},{9,8},{10,11... | collective-permute-start | bytes 49160 | tf_op jit(solution)/shard_map/ppermute | solution.py:69
  64.4 4.1 %collective-permute-start.21 = (f32[512,128]{1,0:T(8,128)S(1)}, f32[512,128]{1,0:T(8,128)S(1)}, u32[]{:S(2)}, u32[]{:S(2)}) collective-permute-start(f32[512,128]{1,0:T(8,128)S(1)} %get-tuple-element.68), channel_id=1, source_target_pairs={{0,1},{1,0},{2,3},{3,2},{4,5},{5,4},{6,7},{7,6},{8,9},{9,8},{10,11... | collective-permute-start | bytes 786440 | tf_op jit(solution)/shard_map/ppermute | solution.py:69
  64.6 7.7 %collective-permute-start.20 = (bf16[4,128,128]{2,1,0:T(8,128)(2,1)S(1)}, bf16[4,128,128]{2,1,0:T(8,128)(2,1)S(1)}, u32[]{:S(2)}, u32[]{:S(2)}) collective-permute-start(bf16[4,128,128]{2,1,0:T(8,128)(2,1)S(1)} %get-tuple-element.67), channel_id=1, source_target_pairs={{0,6},{2,4},{4,2},{6,0},{8,14},{10,12},{12,10},{14,8},{16,22},{18,... | collective-permute-start | bytes 393224 | tf_op jit(solution)/shard_map/ppermute | solution.py:360
  68.0 6.2 %collective-permute-start.18 = (bf16[4,128,128]{2,1,0:T(8,128)(2,1)S(1)}, bf16[4,128,128]{2,1,0:T(8,128)(2,1)S(1)}, u32[]{:S(2)}, u32[]{:S(2)}) collective-permute-start(bf16[4,128,128]{2,1,0:T(8,128)(2,1)S(1)} %get-tuple-element.65), channel_id=1, source_target_pairs={{0,2},{2,0},{4,6},{6,4},{8,10},{10,8},{12,14},{14,12},{16,18},{18,... | collective-permute-start | bytes 393224 | tf_op jit(solution)/shard_map/ppermute | solution.py:360
  68.0 6.8 %collective-permute-start.19 = (bf16[4,128,128]{2,1,0:T(8,128)(2,1)S(1)}, bf16[4,128,128]{2,1,0:T(8,128)(2,1)S(1)}, u32[]{:S(2)}, u32[]{:S(2)}) collective-permute-start(bf16[4,128,128]{2,1,0:T(8,128)(2,1)S(1)} %get-tuple-element.66), channel_id=1, source_target_pairs={{0,4},{2,6},{4,0},{6,2},{8,12},{10,14},{12,8},{14,10},{16,20},{18,... | collective-permute-start | bytes 393224 | tf_op jit(solution)/shard_map/ppermute | solution.py:360
  74.8 5.9 %collective-permute-start.22 = (bf16[128,128]{1,0:T(8,128)(2,1)S(1)}, bf16[128,128]{1,0:T(8,128)(2,1)S(1)}, u32[]{:S(2)}, u32[]{:S(2)}) collective-permute-start(bf16[128,128]{1,0:T(8,128)(2,1)S(1)} %get-tuple-element.71), channel_id=1, source_target_pairs={{0,8},{2,10},{4,12},{6,14},{8,16},{10,18},{12,20},{14,22},{16,24},... | collective-permute-start | bytes 98312 | tf_op jit(solution)/shard_map/ppermute | solution.py:366
  76.9 5.0 %collective-permute-start.23 = (bf16[128,128]{1,0:T(8,128)(2,1)S(1)}, bf16[128,128]{1,0:T(8,128)(2,1)S(1)}, u32[]{:S(2)}, u32[]{:S(2)}) collective-permute-start(bf16[128,128]{1,0:T(8,128)(2,1)S(1)} %get-tuple-element.72), channel_id=1, source_target_pairs={{0,16},{2,18},{4,20},{6,22},{8,24},{10,26},{12,28},{14,30},{16,0},... | collective-permute-start | bytes 98312 | tf_op jit(solution)/shard_map/ppermute | solution.py:366
  79.1 3.9 %collective-permute-start.24 = (bf16[128,128]{1,0:T(8,128)(2,1)S(1)}, bf16[128,128]{1,0:T(8,128)(2,1)S(1)}, u32[]{:S(2)}, u32[]{:S(2)}) collective-permute-start(bf16[128,128]{1,0:T(8,128)(2,1)S(1)} %get-tuple-element.73), channel_id=1, source_target_pairs={{0,24},{2,26},{4,28},{6,30},{8,0},{10,2},{12,4},{14,6},{16,8},{18,... | collective-permute-start | bytes 98312 | tf_op jit(solution)/shard_map/ppermute | solution.py:366

commit v6 on v3

--- a/solution.py
+++ b/solution.py
@@ -191,7 +191,7 @@
 
 
 def score_kernel(shape, own, n, chunk, mine, other, relation, relation_b, cols, *rest):
-    shards, (t_out, s_out, stats, q_student, q_teacher) = rest[:n], rest[n:]
+    shards, (t_out, s_out, tops, stats, q_student, q_teacher) = rest[:n], rest[n:]
     q = mine.shape[0]
     sw, wide = shape.sw, shape.wide
     rows = 128
@@ -221,15 +221,18 @@
         group = shards[c * chunk // own : (c + 1) * chunk // own]
         t = lax.dot_general(joined(group, slice(sw, None)), q_teacher[...], dims, preferred_element_type=F32)
         s = lax.dot_general(joined(group, slice(0, sw)), q_student[...], dims, preferred_element_type=F32)
-        t_out[at, :] = t
-        s_out[at, :] = s
         new_t = jnp.maximum(top_t, jnp.max(t, axis=0, keepdims=True))
         new_s = jnp.maximum(top_s, jnp.max(s, axis=0, keepdims=True))
         scale_t, scale_s = jnp.exp(top_t - new_t), jnp.exp(top_s - new_s)
         e = jnp.exp(t - new_t)
+        f = jnp.exp(s - new_s)
+        t_out[at, :] = e
+        s_out[at, :] = f
+        tops[2 * c : 2 * c + 1, :] = new_t
+        tops[2 * c + 1 : 2 * c + 2, :] = new_s
         total_t = total_t * scale_t + jnp.sum(e, axis=0, keepdims=True)
         weighted = weighted * scale_t + jnp.sum(e * (t - s), axis=0, keepdims=True)
-        total_s = total_s * scale_s + jnp.sum(jnp.exp(s - new_s), axis=0, keepdims=True)
+        total_s = total_s * scale_s + jnp.sum(f, axis=0, keepdims=True)
         return new_t, total_t, weighted, new_s, total_s
 
     lowest = jnp.full((1, q), -jnp.inf, F32)
@@ -250,11 +253,12 @@
         out_shape=(
             jax.ShapeDtypeStruct((slab, q), F32),
             jax.ShapeDtypeStruct((slab, q), F32),
+            jax.ShapeDtypeStruct((2 * slab // chunk, q), F32),
             jax.ShapeDtypeStruct((8, q), F32),
             jax.ShapeDtypeStruct((q, shape.sw), BF16),
         ),
         in_specs=[VMEM] * (5 + n),
-        out_specs=(VMEM,) * 4,
+        out_specs=(VMEM,) * 5,
         scratch_shapes=[pltpu.VMEM((q, 2 * shape.wide), BF16)],
         compiler_params=pltpu.CompilerParams(vmem_limit_bytes=8 * slab * q + 2 * slab * shape.total + 10 * MIB),
         cost_estimate=pl.CostEstimate(
@@ -274,7 +278,7 @@
     return top_t, total_t, weighted, top_s, total_s
 
 
-def grad_kernel(n, own, chunk, sw, order, t_in, s_in, mine, other, q_student, *rest):
+def grad_kernel(n, own, chunk, sw, order, t_in, s_in, tops, mine, other, q_student, *rest):
     shards, (divergence, q_grad), outs = rest[:n], rest[n : n + 2], rest[n + 2 : -1]
     e_grad = rest[-1]
     top_t, total_t, weighted, top_s, total_s = combine(mine[...], other[...])
@@ -284,9 +288,9 @@
 
     def step(c, total):
         at = slice(c * chunk, (c + 1) * chunk)
-        prob_t = jnp.exp(t_in[at, :] - top_t) * over_t
-        prob_s = jnp.exp(s_in[at, :] - top_s) * over_s
-        weights = (prob_s - prob_t).astype(BF16)
+        scale_t = jnp.exp(tops[2 * c : 2 * c + 1, :] - top_t) * over_t
+        scale_s = jnp.exp(tops[2 * c + 1 : 2 * c + 2, :] - top_s) * over_s
+        weights = (s_in[at, :] * scale_s - t_in[at, :] * scale_t).astype(BF16)
         grad = jnp.dot(weights, q_student[...], preferred_element_type=F32).astype(BF16)
         for k in range(per):
             e_grad[order[c * per + k]] = grad[k * own : (k + 1) * own, :]
@@ -307,7 +311,7 @@
         out[...] = e_grad[d * count : (d + 1) * count]
 
 
-def gradients(order, near, t, s, mine, other, q_student, shards):
+def gradients(order, near, t, s, tops, mine, other, q_student, shards):
     n, own = len(shards), shards[0].shape[0]
     q, sw = q_student.shape
     slab = n * own
@@ -320,7 +324,7 @@
             jax.ShapeDtypeStruct((q, sw), F32),
         )
         + (jax.ShapeDtypeStruct((n // near, own, sw), BF16),) * near,
-        in_specs=[SMEM] + [VMEM] * (5 + n),
+        in_specs=[SMEM] + [VMEM] * (6 + n),
         out_specs=(VMEM,) * (2 + near),
         scratch_shapes=[pltpu.VMEM((n, own, sw), BF16)],
         compiler_params=pltpu.CompilerParams(vmem_limit_bytes=8 * slab * q + 2 * slab * shape_total + 10 * MIB),
@@ -328,7 +332,7 @@
             flops=4 * q * slab * sw, bytes_accessed=8 * slab * q, transcendentals=2 * slab * q
         ),
         name="gradients",
-    )(order, t, s, mine, other, q_student, *shards)
+    )(order, t, s, tops, mine, other, q_student, *shards)
 
 
 def add_kernel(count, *refs):
@@ -424,14 +428,14 @@
             mine = mine + partner(mine, groups, far)
             far *= 2
         other = partner(mine, groups, far)
-        t, s, stats, q_student = scores(mine, other, relation, relation_b, cols, shards, shape)
+        expo_t, expo_s, tops, stats, q_student = scores(mine, other, relation, relation_b, cols, shards, shape)
         far = 1
         while far < groups // 2:
             found = combine(stats, partner(stats, groups, far))
             stats = jnp.concatenate(list(found) + [jnp.zeros_like(found[0])] * 3, axis=0)
             far *= 2
         divergence, q_grad, *blocks = gradients(
-            order, near, t, s, stats, partner(stats, groups, far), q_student, shards
+            order, near, expo_t, expo_s, tops, stats, partner(stats, groups, far), q_student, shards
         )
         far = 1
         while far < groups:

time: 82.6 us -> 82.2 us (level)
  no operation moved by 1% of the time
where the time goes in v6:
time: 82.2 us; the launch traced here: 82 us
  waiting for transfers between devices  33.5 us (41%)
  starting transfers between devices  24.6 us (30%)
  Pallas kernels  21.1 us (26%)
  other arithmetic  1.38 us (2%)
    ppermute x15, waiting for transfers between devices, move(): return lax.ppermute(x, 'query', sorted(pairs))  21.8 us
    ppermute x15, starting transfers between devices, move(): return lax.ppermute(x, 'query', sorted(pairs))  15.1 us
    pallas_call x1, Pallas kernels, relation_rows(): pl.pallas_call(functools.partial(relation_kernel, shape, rel, block, cut)...  6.93 us
    ppermute x3, starting transfers between devices, reduce_blocks(): total = total + lax.ppermute(sums[e], 'query', pairs).astype(F32)  5.57 us
    pallas_call x1, Pallas kernels, scores(): pl.pallas_call(functools.partial(score_kernel, shape, own, n, chunk), out...  5.26 us
    ppermute x3, waiting for transfers between devices, reduce_blocks(): lax.ppermute(blocks[d], 'query', [(i, i ^ d) for i in range(n)])  5.23 us
    pallas_call x2, Pallas kernels, anchor_rows(): pl.pallas_call(functools.partial(anchor_kernel, count, own, acc is not No...  4.6 us
    ppermute x4, waiting for transfers between devices, partner(): return lax.ppermute(x, 'entity', [(i, i ^ far) for i in range(size)])  3.88 us
  transfers between devices with their start and end apart: 25, of which 14 were waited for; matrix products, arithmetic and copies ran while one was open for 2% of the time, Pallas kernels for 14%

profile of v6, /device:TPU:0, one launch (start us, length us, event | category | flops | bytes accessed | tf_op | source)
XLA Modules:
  0.0 82.0 jit_solution(2434502788996650864)
XLA Ops:
  0.6 2.0 %pack_rows.1 = (bf16[128,1152]{1,0:T(8,128)(2,1)}, s32[512,8]{1,0:T(8,128)}) custom-call(bf16[1000,128]{1,0:T(8,128)(2,1)} %bitcast.14, bf16[128,128]{1,0:T(8,128)(2,1)} %student.2, s32[1,512]{1,0:T(1,128)} %bitcast.15, s32[1,512]{1,0:T(1,128)} %bitcast.16, s32[1,512]{1,0:T(1,128)} %bitcast.17), custom_call_target="tpu_custom_call" | custom-call | tf_op jit(solution)/shard_map/pack_rows/pallas_call | solution.py:97
  2.7 2.9 %collective-permute-start.2 = (bf16[128,1152]{1,0:T(8,128)(2,1)}, bf16[128,1152]{1,0:T(8,128)(2,1)S(1)}, u32[]{:S(2)}, u32[]{:S(2)}) collective-permute-start(bf16[128,1152]{1,0:T(8,128)(2,1)} %get-tuple-element.42.rest_0_), channel_id=1, source_target_pairs={{0,2},{2,0},{4,6},{6,4},{8,10},{10,8},{12,14},{14,12},{16,18},{18,... | collective-permute-start | bytes 884744 | tf_op jit(solution)/shard_map/ppermute | solution.py:56
  5.6 1.6 %collective-permute-start.1 = (bf16[128,1152]{1,0:T(8,128)(2,1)}, bf16[128,1152]{1,0:T(8,128)(2,1)S(1)}, u32[]{:S(2)}, u32[]{:S(2)}) collective-permute-start(bf16[128,1152]{1,0:T(8,128)(2,1)} %get-tuple-element.42.rest_0_), channel_id=1, source_target_pairs={{0,8},{2,10},{4,0},{6,2},{8,16},{10,18},{12,4},{14,6},{16,24},{18,... | collective-permute-start | bytes 884744 | tf_op jit(solution)/shard_map/ppermute | solution.py:56
  7.7 6.9 %relation_rows.1.relation = bf16[512,1152]{1,0:T(8,128)(2,1)} custom-call(s32[1]{0:T(128)} %bitcast.7.base, s32[512,8]{1,0:T(8,128)} %get-tuple-element.40.cols, bf16[1000,4131]{1,0:T(8,128)(2,1)} %bitcast.13, bf16[4131,128]{1,0:T(8,128)(2,1)} %student.3), custom_call_target="tpu_custom_call" | custom-call | flops 2359296000 | bytes 4608000 | tf_op jit(solution)/shard_map/relation_rows/pallas_call | solution.py:133
  14.6 1.0 %collective-permute-done.rest_1_ = bf16[128,1152]{1,0:T(8,128)(2,1)S(1)} collective-permute-done((bf16[128,1152]{1,0:T(8,128)(2,1)}, bf16[128,1152]{1,0:T(8,128)(2,1)S(1)}, u32[]{:S(2)}, u32[]{:S(2)}) %collective-permute-start) | collective-permute-done | bytes 294944 | tf_op jit(solution)/shard_map/ppermute | solution.py:56
  15.6 1.6 %collective-permute-start.4 = (bf16[128,1152]{1,0:T(8,128)(2,1)S(1)}, bf16[128,1152]{1,0:T(8,128)(2,1)S(1)}, u32[]{:S(2)}, u32[]{:S(2)}) collective-permute-start(bf16[128,1152]{1,0:T(8,128)(2,1)S(1)} %collective-permute-done.1.rest_2_), channel_id=1, source_target_pairs={{0,8},{2,10},{4,0},{6,2},{8,16},{10,18},{12,4},{14,6},{16,24},{18,... | collective-permute-start | bytes 884744 | tf_op jit(solution)/shard_map/ppermute | solution.py:56
  18.2 4.7 %collective-permute-done.4.rest_5_ = bf16[128,1152]{1,0:T(8,128)(2,1)S(1)} collective-permute-done((bf16[128,1152]{1,0:T(8,128)(2,1)S(1)}, bf16[128,1152]{1,0:T(8,128)(2,1)S(1)}, u32[]{:S(2)}, u32[]{:S(2)}) %collective-permute-start.4) | collective-permute-done | bytes 294944 | tf_op jit(solution)/shard_map/ppermute | solution.py:56
  22.9 1.6 %collective-permute-start.7 = (bf16[128,1152]{1,0:T(8,128)(2,1)S(1)}, bf16[128,1152]{1,0:T(8,128)(2,1)S(1)}, u32[]{:S(2)}, u32[]{:S(2)}) collective-permute-start(bf16[128,1152]{1,0:T(8,128)(2,1)S(1)} %collective-permute-done.4.rest_5_), channel_id=1, source_target_pairs={{0,8},{2,10},{4,0},{6,2},{8,16},{10,18},{12,4},{14,6},{16,24},{18,... | collective-permute-start | bytes 884744 | tf_op jit(solution)/shard_map/ppermute | solution.py:56
  24.4 1.5 %collective-permute-start.8 = (bf16[128,1152]{1,0:T(8,128)(2,1)S(1)}, bf16[128,1152]{1,0:T(8,128)(2,1)S(1)}, u32[]{:S(2)}, u32[]{:S(2)}) collective-permute-start(bf16[128,1152]{1,0:T(8,128)(2,1)S(1)} %collective-permute-done.3.rest_4_), channel_id=1, source_target_pairs={{0,2},{2,0},{4,6},{6,4},{8,10},{10,8},{12,14},{14,12},{16,18},{18,... | collective-permute-start | bytes 884744 | tf_op jit(solution)/shard_map/ppermute | solution.py:56
  26.4 4.3 %collective-permute-done.7.rest_8_ = bf16[128,1152]{1,0:T(8,128)(2,1)S(1)} collective-permute-done((bf16[128,1152]{1,0:T(8,128)(2,1)S(1)}, bf16[128,1152]{1,0:T(8,128)(2,1)S(1)}, u32[]{:S(2)}, u32[]{:S(2)}) %collective-permute-start.7) | collective-permute-done | bytes 294944 | tf_op jit(solution)/shard_map/ppermute | solution.py:56
  30.6 1.6 %collective-permute-start.11 = (bf16[128,1152]{1,0:T(8,128)(2,1)S(1)}, bf16[128,1152]{1,0:T(8,128)(2,1)S(1)}, u32[]{:S(2)}, u32[]{:S(2)}) collective-permute-start(bf16[128,1152]{1,0:T(8,128)(2,1)S(1)} %collective-permute-done.2.rest_3_), channel_id=1, source_target_pairs={{0,8},{2,10},{4,0},{6,2},{8,16},{10,18},{12,4},{14,6},{16,24},{18,... | collective-permute-start | bytes 884744 | tf_op jit(solution)/shard_map/ppermute | solution.py:56
  32.2 1.5 %collective-permute-done.6.rest_7_ = bf16[128,1152]{1,0:T(8,128)(2,1)S(1)} collective-permute-done((bf16[128,1152]{1,0:T(8,128)(2,1)S(1)}, bf16[128,1152]{1,0:T(8,128)(2,1)S(1)}, u32[]{:S(2)}, u32[]{:S(2)}) %collective-permute-start.6) | collective-permute-done | bytes 294944 | tf_op jit(solution)/shard_map/ppermute | solution.py:56
  34.2 0.7 constant_dynamic-slice_fusion
  34.9 8.5 %collective-permute-done.9.rest_12_ = bf16[128,1152]{1,0:T(8,128)(2,1)S(1)} collective-permute-done((bf16[128,1152]{1,0:T(8,128)(2,1)S(1)}, bf16[128,1152]{1,0:T(8,128)(2,1)S(1)}, u32[]{:S(2)}, u32[]{:S(2)}) %collective-permute-start.9) | collective-permute-done | bytes 294944 | tf_op jit(solution)/shard_map/ppermute | solution.py:56
  43.8 1.6 %collective-permute-start.13 = (bf16[128,1152]{1,0:T(8,128)(2,1)S(1)}, bf16[128,1152]{1,0:T(8,128)(2,1)S(1)}, u32[]{:S(2)}, u32[]{:S(2)}) collective-permute-start(bf16[128,1152]{1,0:T(8,128)(2,1)S(1)} %collective-permute-done.11.rest_11_), channel_id=1, source_target_pairs={{0,8},{2,10},{4,0},{6,2},{8,16},{10,18},{12,4},{14,6},{16,24},{18,... | collective-permute-start | bytes 884744 | tf_op jit(solution)/shard_map/ppermute | solution.py:56
  45.5 3.2 %anchor_rows.2.rest_0_ = bf16[512,1152]{1,0:T(8,128)(2,1)S(1)} custom-call(s32[16]{0:T(128)S(1)} %bitcast.12, s32[512,8]{1,0:T(8,128)S(1)} %copy-done.1, bf16[128,1152]{1,0:T(8,128)(2,1)S(1)} %copy-done.2, bf16[128,1152]{1,0:T(8,128)(2,1)S(1)} %collective-permute-done.rest_1_, bf16[128,1152]{1,0:T(8,128)(2,1)S(1)} %collective-permute-done.1.rest_2_, ...), custom_call_target="tpu_custom_call" | custom-call | flops 1962934272 | bytes 6193152 | tf_op jit(solution)/shard_map/anchor_rows/pallas_call | solution.py:178
  48.7 1.9 %collective-permute-done.13.rest_2_.rest_14_ = bf16[128,1152]{1,0:T(8,128)(2,1)S(1)} collective-permute-done((bf16[128,1152]{1,0:T(8,128)(2,1)S(1)}, bf16[128,1152]{1,0:T(8,128)(2,1)S(1)}, u32[]{:S(2)}, u32[]{:S(2)}) %collective-permute-start.13) | collective-permute-done | bytes 294944 | tf_op jit(solution)/shard_map/ppermute | solution.py:56
  50.6 1.4 %anchor_rows.3.mine = bf16[512,1152]{1,0:T(8,128)(2,1)S(1)} custom-call(s32[3]{0:T(128)S(1)} %slice_bitcast_fusion.bases, s32[512,8]{1,0:T(8,128)S(1)} %copy-done.1, bf16[512,1152]{1,0:T(8,128)(2,1)S(1)} %anchor_rows.2.rest_0_, bf16[128,1152]{1,0:T(8,128)(2,1)S(1)} %collective-permute-done.12.rest_1_.rest_13_, ...), custom_call_target="tpu_custom_call" | custom-call | flops 452984832 | bytes 3244032 | tf_op jit(solution)/shard_map/anchor_rows/pallas_call | solution.py:178
  52.0 2.8 %collective-permute-done.15.other = bf16[512,1152]{1,0:T(8,128)(2,1)S(1)} collective-permute-done((bf16[512,1152]{1,0:T(8,128)(2,1)S(1)}, bf16[512,1152]{1,0:T(8,128)(2,1)S(1)}, u32[]{:S(2)}, u32[]{:S(2)}) %collective-permute-start.15) | collective-permute-done | bytes 1179680 | tf_op jit(solution)/shard_map/ppermute | solution.py:69
  54.9 5.3 %scores.1 = (f32[2048,512]{1,0:T(8,128)S(1)}, f32[2048,512]{1,0:T(8,128)S(1)}, f32[8,512]{1,0:T(8,128)S(1)}, f32[8,512]{1,0:T(8,128)S(1)}, bf16[512,128]{1,0:T(8,128)(2,1)S(1)}) custom-call(bf16[512,1152]{1,0:T(8,128)(2,1)S(1)} %anchor_rows.3.mine, bf16[512,1152]{1,0:T(8,128)(2,1)S(1)} %collective-permute-done.15.other, bf16[512,1152]{1,0:T(8,128)(2,1)S(1)} %copy-done, ...), custom_call_target="tpu_custom_call" | custom-call | flops 2415919104 | bytes 13107200 | tf_op jit(solution)/shard_map/scores/pallas_call | solution.py:251
  60.3 1.0 %collective-permute-done.17.other = f32[8,512]{1,0:T(8,128)S(1)} collective-permute-done((f32[8,512]{1,0:T(8,128)S(1)}, f32[8,512]{1,0:T(8,128)S(1)}, u32[]{:S(2)}, u32[]{:S(2)}) %collective-permute-start.17) | collective-permute-done | bytes 16416 | tf_op jit(solution)/shard_map/ppermute | solution.py:69
  61.4 2.2 %gradients.1 = (f32[1,512]{1,0:T(1,128)}, f32[512,128]{1,0:T(8,128)S(1)}, bf16[4,128,128]{2,1,0:T(8,128)(2,1)S(1)}, bf16[4,128,128]{2,1,0:T(8,128)(2,1)S(1)}, bf...) custom-call(s32[16]{0:T(128)S(1)} %get-tuple-element.78.order, f32[2048,512]{1,0:T(8,128)S(1)} %get-tuple-element.60.t_in, ...), custom_call_target="tpu_custom_call" | custom-call | flops 536870912 | bytes 8388608 | tf_op jit(solution)/shard_map/gradients/pallas_call | solution.py:320
  63.7 2.1 %collective-permute-start.20 = (bf16[4,128,128]{2,1,0:T(8,128)(2,1)S(1)}, bf16[4,128,128]{2,1,0:T(8,128)(2,1)S(1)}, u32[]{:S(2)}, u32[]{:S(2)}) collective-permute-start(bf16[4,128,128]{2,1,0:T(8,128)(2,1)S(1)} %get-tuple-element.69), channel_id=1, source_target_pairs={{0,6},{2,4},{4,2},{6,0},{8,14},{10,12},{12,10},{14,8},{16,22},{18,... | collective-permute-start | bytes 393224 | tf_op jit(solution)/shard_map/ppermute | solution.py:364
  65.9 1.3 %collective-permute-start.19 = (bf16[4,128,128]{2,1,0:T(8,128)(2,1)S(1)}, bf16[4,128,128]{2,1,0:T(8,128)(2,1)S(1)}, u32[]{:S(2)}, u32[]{:S(2)}) collective-permute-start(bf16[4,128,128]{2,1,0:T(8,128)(2,1)S(1)} %get-tuple-element.68), channel_id=1, source_target_pairs={{0,4},{2,6},{4,0},{6,2},{8,12},{10,14},{12,8},{14,10},{16,20},{18,... | collective-permute-start | bytes 393224 | tf_op jit(solution)/shard_map/ppermute | solution.py:364
  67.2 0.7 add.30
  68.0 3.0 %collective-permute-done.20.refs_3_ = bf16[4,128,128]{2,1,0:T(8,128)(2,1)S(1)} collective-permute-done((bf16[4,128,128]{2,1,0:T(8,128)(2,1)S(1)}, bf16[4,128,128]{2,1,0:T(8,128)(2,1)S(1)}, u32[]{:S(2)}, u32[]{:S(2)}) %collective-permute-start.20) | collective-permute-done | bytes 131104 | tf_op jit(solution)/shard_map/ppermute | solution.py:364
  71.0 1.6 %collective-permute-done.18.refs_1_ = bf16[4,128,128]{2,1,0:T(8,128)(2,1)S(1)} collective-permute-done((bf16[4,128,128]{2,1,0:T(8,128)(2,1)S(1)}, bf16[4,128,128]{2,1,0:T(8,128)(2,1)S(1)}, u32[]{:S(2)}, u32[]{:S(2)}) %collective-permute-start.18) | collective-permute-done | bytes 131104 | tf_op jit(solution)/shard_map/ppermute | solution.py:364
  73.3 1.6 %collective-permute-start.22 = (bf16[128,128]{1,0:T(8,128)(2,1)S(1)}, bf16[128,128]{1,0:T(8,128)(2,1)S(1)}, u32[]{:S(2)}, u32[]{:S(2)}) collective-permute-start(bf16[128,128]{1,0:T(8,128)(2,1)S(1)} %get-tuple-element.73), channel_id=1, source_target_pairs={{0,8},{2,10},{4,12},{6,14},{8,16},{10,18},{12,20},{14,22},{16,24},... | collective-permute-start | bytes 98312 | tf_op jit(solution)/shard_map/ppermute | solution.py:370
  74.9 2.5 %collective-permute-start.23 = (bf16[128,128]{1,0:T(8,128)(2,1)S(1)}, bf16[128,128]{1,0:T(8,128)(2,1)S(1)}, u32[]{:S(2)}, u32[]{:S(2)}) collective-permute-start(bf16[128,128]{1,0:T(8,128)(2,1)S(1)} %get-tuple-element.74), channel_id=1, source_target_pairs={{0,16},{2,18},{4,20},{6,22},{8,24},{10,26},{12,28},{14,30},{16,0},... | collective-permute-start | bytes 98312 | tf_op jit(solution)/shard_map/ppermute | solution.py:370
  77.4 1.4 %collective-permute-start.24 = (bf16[128,128]{1,0:T(8,128)(2,1)S(1)}, bf16[128,128]{1,0:T(8,128)(2,1)S(1)}, u32[]{:S(2)}, u32[]{:S(2)}) collective-permute-start(bf16[128,128]{1,0:T(8,128)(2,1)S(1)} %get-tuple-element.75), channel_id=1, source_target_pairs={{0,24},{2,26},{4,28},{6,30},{8,0},{10,2},{12,4},{14,6},{16,8},{18,... | collective-permute-start | bytes 98312 | tf_op jit(solution)/shard_map/ppermute | solution.py:370
  79.0 1.2 %collective-permute-done.23 = bf16[128,128]{1,0:T(8,128)(2,1)S(1)} collective-permute-done((bf16[128,128]{1,0:T(8,128)(2,1)S(1)}, bf16[128,128]{1,0:T(8,128)(2,1)S(1)}, u32[]{:S(2)}, u32[]{:S(2)}) %collective-permute-start.23) | collective-permute-done | bytes 32800 | tf_op jit(solution)/shard_map/ppermute | solution.py:370
  80.2 1.1 %collective-permute-done.24 = bf16[128,128]{1,0:T(8,128)(2,1)S(1)} collective-permute-done((bf16[128,128]{1,0:T(8,128)(2,1)S(1)}, bf16[128,128]{1,0:T(8,128)(2,1)S(1)}, u32[]{:S(2)}, u32[]{:S(2)}) %collective-permute-start.24) | collective-permute-done | bytes 32800 | tf_op jit(solution)/shard_map/ppermute | solution.py:370
  (36 shorter events, 4.9 us)
Async XLA Ops:
  2.7 11.9 %collective-permute-start.2 = (bf16[128,1152]{1,0:T(8,128)(2,1)}, bf16[128,1152]{1,0:T(8,128)(2,1)S(1)}, u32[]{:S(2)}, u32[]{:S(2)}) collective-permute-start(bf16[128,1152]{1,0:T(8,128)(2,1)} %get-tuple-element.42.rest_0_), channel_id=1, source_target_pairs={{0,2},{2,0},{4,6},{6,4},{8,10},{10,8},{12,14},{14,12},{16,18},{18,... | collective-permute-start | bytes 884744 | tf_op jit(solution)/shard_map/ppermute | solution.py:56
  5.6 9.0 %collective-permute-start.1 = (bf16[128,1152]{1,0:T(8,128)(2,1)}, bf16[128,1152]{1,0:T(8,128)(2,1)S(1)}, u32[]{:S(2)}, u32[]{:S(2)}) collective-permute-start(bf16[128,1152]{1,0:T(8,128)(2,1)} %get-tuple-element.42.rest_0_), channel_id=1, source_target_pairs={{0,8},{2,10},{4,0},{6,2},{8,16},{10,18},{12,4},{14,6},{16,24},{18,... | collective-permute-start | bytes 884744 | tf_op jit(solution)/shard_map/ppermute | solution.py:56
  7.2 8.4 %collective-permute-start = (bf16[128,1152]{1,0:T(8,128)(2,1)}, bf16[128,1152]{1,0:T(8,128)(2,1)S(1)}, u32[]{:S(2)}, u32[]{:S(2)}) collective-permute-start(bf16[128,1152]{1,0:T(8,128)(2,1)} %get-tuple-element.42.rest_0_), channel_id=1, source_target_pairs={{0,4},{2,6},{4,12},{6,14},{8,0},{10,2},{12,20},{14,22},{16,8},{18,... | collective-permute-start | bytes 884744 | tf_op jit(solution)/shard_map/ppermute | solution.py:56
  7.7 37.8 %copy-start.1 = (s32[512,8]{1,0:T(8,128)S(1)}, s32[512,8]{1,0:T(8,128)}, u32[]{:S(2)}) copy-start(s32[512,8]{1,0:T(8,128)} %get-tuple-element.40.cols) | copy-start | bytes 49156
  7.7 37.8 %copy-start.2 = (bf16[128,1152]{1,0:T(8,128)(2,1)S(1)}, bf16[128,1152]{1,0:T(8,128)(2,1)}, u32[]{:S(2)}) copy-start(bf16[128,1152]{1,0:T(8,128)(2,1)} %get-tuple-element.42.rest_0_) | copy-start | bytes 884740
  15.6 7.3 %collective-permute-start.4 = (bf16[128,1152]{1,0:T(8,128)(2,1)S(1)}, bf16[128,1152]{1,0:T(8,128)(2,1)S(1)}, u32[]{:S(2)}, u32[]{:S(2)}) collective-permute-start(bf16[128,1152]{1,0:T(8,128)(2,1)S(1)} %collective-permute-done.1.rest_2_), channel_id=1, source_target_pairs={{0,8},{2,10},{4,0},{6,2},{8,16},{10,18},{12,4},{14,6},{16,24},{18,... | collective-permute-start | bytes 884744 | tf_op jit(solution)/shard_map/ppermute | solution.py:56
  17.2 7.3 %collective-permute-start.5 = (bf16[128,1152]{1,0:T(8,128)(2,1)S(1)}, bf16[128,1152]{1,0:T(8,128)(2,1)S(1)}, u32[]{:S(2)}, u32[]{:S(2)}) collective-permute-start(bf16[128,1152]{1,0:T(8,128)(2,1)S(1)} %collective-permute-done.rest_1_), channel_id=1, source_target_pairs={{0,2},{2,0},{4,6},{6,4},{8,10},{10,8},{12,14},{14,12},{16,18},{18,... | collective-permute-start | bytes 884744 | tf_op jit(solution)/shard_map/ppermute | solution.py:56
  17.7 6.7 %collective-permute-start.3 = (bf16[128,1152]{1,0:T(8,128)(2,1)S(1)}, bf16[128,1152]{1,0:T(8,128)(2,1)S(1)}, u32[]{:S(2)}, u32[]{:S(2)}) collective-permute-start(bf16[128,1152]{1,0:T(8,128)(2,1)S(1)} %collective-permute-done.rest_1_), channel_id=1, source_target_pairs={{0,4},{2,6},{4,12},{6,14},{8,0},{10,2},{12,20},{14,22},{16,8},{18,... | collective-permute-start | bytes 884744 | tf_op jit(solution)/shard_map/ppermute | solution.py:56
  22.9 7.8 %collective-permute-start.7 = (bf16[128,1152]{1,0:T(8,128)(2,1)S(1)}, bf16[128,1152]{1,0:T(8,128)(2,1)S(1)}, u32[]{:S(2)}, u32[]{:S(2)}) collective-permute-start(bf16[128,1152]{1,0:T(8,128)(2,1)S(1)} %collective-permute-done.4.rest_5_), channel_id=1, source_target_pairs={{0,8},{2,10},{4,0},{6,2},{8,16},{10,18},{12,4},{14,6},{16,24},{18,... | collective-permute-start | bytes 884744 | tf_op jit(solution)/shard_map/ppermute | solution.py:56
  24.4 7.8 %collective-permute-start.8 = (bf16[128,1152]{1,0:T(8,128)(2,1)S(1)}, bf16[128,1152]{1,0:T(8,128)(2,1)S(1)}, u32[]{:S(2)}, u32[]{:S(2)}) collective-permute-start(bf16[128,1152]{1,0:T(8,128)(2,1)S(1)} %collective-permute-done.3.rest_4_), channel_id=1, source_target_pairs={{0,2},{2,0},{4,6},{6,4},{8,10},{10,8},{12,14},{14,12},{16,18},{18,... | collective-permute-start | bytes 884744 | tf_op jit(solution)/shard_map/ppermute | solution.py:56
  25.9 7.8 %collective-permute-start.6 = (bf16[128,1152]{1,0:T(8,128)(2,1)S(1)}, bf16[128,1152]{1,0:T(8,128)(2,1)S(1)}, u32[]{:S(2)}, u32[]{:S(2)}) collective-permute-start(bf16[128,1152]{1,0:T(8,128)(2,1)S(1)} %collective-permute-done.3.rest_4_), channel_id=1, source_target_pairs={{0,4},{2,6},{4,12},{6,14},{8,0},{10,2},{12,20},{14,22},{16,8},{18,... | collective-permute-start | bytes 884744 | tf_op jit(solution)/shard_map/ppermute | solution.py:56
  30.6 13.2 %collective-permute-start.11 = (bf16[128,1152]{1,0:T(8,128)(2,1)S(1)}, bf16[128,1152]{1,0:T(8,128)(2,1)S(1)}, u32[]{:S(2)}, u32[]{:S(2)}) collective-permute-start(bf16[128,1152]{1,0:T(8,128)(2,1)S(1)} %collective-permute-done.2.rest_3_), channel_id=1, source_target_pairs={{0,8},{2,10},{4,0},{6,2},{8,16},{10,18},{12,4},{14,6},{16,24},{18,... | collective-permute-start | bytes 884744 | tf_op jit(solution)/shard_map/ppermute | solution.py:56
  33.7 9.6 %collective-permute-start.9 = (bf16[128,1152]{1,0:T(8,128)(2,1)S(1)}, bf16[128,1152]{1,0:T(8,128)(2,1)S(1)}, u32[]{:S(2)}, u32[]{:S(2)}) collective-permute-start(bf16[128,1152]{1,0:T(8,128)(2,1)S(1)} %collective-permute-done.6.rest_7_), channel_id=1, source_target_pairs={{0,2},{2,0},{4,6},{6,4},{8,10},{10,8},{12,14},{14,12},{16,18},{18,... | collective-permute-start | bytes 884744 | tf_op jit(solution)/shard_map/ppermute | solution.py:56
  33.7 9.7 %collective-permute-start.10 = (bf16[128,1152]{1,0:T(8,128)(2,1)S(1)}, bf16[128,1152]{1,0:T(8,128)(2,1)S(1)}, u32[]{:S(2)}, u32[]{:S(2)}) collective-permute-start(bf16[128,1152]{1,0:T(8,128)(2,1)S(1)} %collective-permute-done.6.rest_7_), channel_id=1, source_target_pairs={{0,4},{2,6},{4,12},{6,14},{8,0},{10,2},{12,20},{14,22},{16,8},{18,... | collective-permute-start | bytes 884744 | tf_op jit(solution)/shard_map/ppermute | solution.py:56
  43.4 7.2 %collective-permute-start.14 = (bf16[128,1152]{1,0:T(8,128)(2,1)S(1)}, bf16[128,1152]{1,0:T(8,128)(2,1)S(1)}, u32[]{:S(2)}, u32[]{:S(2)}) collective-permute-start(bf16[128,1152]{1,0:T(8,128)(2,1)S(1)} %collective-permute-done.7.rest_8_), channel_id=1, source_target_pairs={{0,2},{2,0},{4,6},{6,4},{8,10},{10,8},{12,14},{14,12},{16,18},{18,... | collective-permute-start | bytes 884744 | tf_op jit(solution)/shard_map/ppermute | solution.py:56
  43.4 7.2 %collective-permute-start.12 = (bf16[128,1152]{1,0:T(8,128)(2,1)S(1)}, bf16[128,1152]{1,0:T(8,128)(2,1)S(1)}, u32[]{:S(2)}, u32[]{:S(2)}) collective-permute-start(bf16[128,1152]{1,0:T(8,128)(2,1)S(1)} %collective-permute-done.9.rest_12_), channel_id=1, source_target_pairs={{0,4},{2,6},{4,12},{6,14},{8,0},{10,2},{12,20},{14,22},{16,8},{18,... | collective-permute-start | bytes 884744 | tf_op jit(solution)/shard_map/ppermute | solution.py:56
  43.8 6.7 %collective-permute-start.13 = (bf16[128,1152]{1,0:T(8,128)(2,1)S(1)}, bf16[128,1152]{1,0:T(8,128)(2,1)S(1)}, u32[]{:S(2)}, u32[]{:S(2)}) collective-permute-start(bf16[128,1152]{1,0:T(8,128)(2,1)S(1)} %collective-permute-done.11.rest_11_), channel_id=1, source_target_pairs={{0,8},{2,10},{4,0},{6,2},{8,16},{10,18},{12,4},{14,6},{16,24},{18,... | collective-permute-start | bytes 884744 | tf_op jit(solution)/shard_map/ppermute | solution.py:56
  45.5 6.6 %collective-permute-start.16 = (bf16[512,1152]{1,0:T(8,128)(2,1)}, bf16[512,1152]{1,0:T(8,128)(2,1)S(1)}, u32[]{:S(2)}, u32[]{:S(2)}) collective-permute-start(bf16[512,1152]{1,0:T(8,128)(2,1)} %relation_rows.1.relation), channel_id=1, source_target_pairs={{0,1},{1,0},{2,3},{3,2},{4,5},{5,4},{6,7},{7,6},{8,9},{9,8},{10,11... | collective-permute-start | bytes 3538952 | tf_op jit(solution)/shard_map/ppermute | solution.py:69
  48.7 6.2 %copy-start = (bf16[512,1152]{1,0:T(8,128)(2,1)S(1)}, bf16[512,1152]{1,0:T(8,128)(2,1)}, u32[]{:S(2)}) copy-start(bf16[512,1152]{1,0:T(8,128)(2,1)} %relation_rows.1.relation) | copy-start | bytes 3538948
  52.0 2.9 %collective-permute-start.15 = (bf16[512,1152]{1,0:T(8,128)(2,1)S(1)}, bf16[512,1152]{1,0:T(8,128)(2,1)S(1)}, u32[]{:S(2)}, u32[]{:S(2)}) collective-permute-start(bf16[512,1152]{1,0:T(8,128)(2,1)S(1)} %anchor_rows.3.mine), channel_id=1, source_target_pairs={{0,1},{1,0},{2,3},{3,2},{4,5},{5,4},{6,7},{7,6},{8,9},{9,8},{10,11... | collective-permute-start | bytes 3538952 | tf_op jit(solution)/shard_map/ppermute | solution.py:69
  60.1 1.2 %collective-permute-start.17 = (f32[8,512]{1,0:T(8,128)S(1)}, f32[8,512]{1,0:T(8,128)S(1)}, u32[]{:S(2)}, u32[]{:S(2)}) collective-permute-start(f32[8,512]{1,0:T(8,128)S(1)} %get-tuple-element.63.mine), channel_id=1, source_target_pairs={{0,1},{1,0},{2,3},{3,2},{4,5},{5,4},{6,7},{7,6},{8,9},{9,8},{10,11... | collective-permute-start | bytes 49160 | tf_op jit(solution)/shard_map/ppermute | solution.py:69
  63.6 3.7 %collective-permute-start.21 = (f32[512,128]{1,0:T(8,128)S(1)}, f32[512,128]{1,0:T(8,128)S(1)}, u32[]{:S(2)}, u32[]{:S(2)}) collective-permute-start(f32[512,128]{1,0:T(8,128)S(1)} %get-tuple-element.70), channel_id=1, source_target_pairs={{0,1},{1,0},{2,3},{3,2},{4,5},{5,4},{6,7},{7,6},{8,9},{9,8},{10,11... | collective-permute-start | bytes 786440 | tf_op jit(solution)/shard_map/ppermute | solution.py:69
  63.7 7.2 %collective-permute-start.20 = (bf16[4,128,128]{2,1,0:T(8,128)(2,1)S(1)}, bf16[4,128,128]{2,1,0:T(8,128)(2,1)S(1)}, u32[]{:S(2)}, u32[]{:S(2)}) collective-permute-start(bf16[4,128,128]{2,1,0:T(8,128)(2,1)S(1)} %get-tuple-element.69), channel_id=1, source_target_pairs={{0,6},{2,4},{4,2},{6,0},{8,14},{10,12},{12,10},{14,8},{16,22},{18,... | collective-permute-start | bytes 393224 | tf_op jit(solution)/shard_map/ppermute | solution.py:364
  65.9 6.7 %collective-permute-start.18 = (bf16[4,128,128]{2,1,0:T(8,128)(2,1)S(1)}, bf16[4,128,128]{2,1,0:T(8,128)(2,1)S(1)}, u32[]{:S(2)}, u32[]{:S(2)}) collective-permute-start(bf16[4,128,128]{2,1,0:T(8,128)(2,1)S(1)} %get-tuple-element.67), channel_id=1, source_target_pairs={{0,2},{2,0},{4,6},{6,4},{8,10},{10,8},{12,14},{14,12},{16,18},{18,... | collective-permute-start | bytes 393224 | tf_op jit(solution)/shard_map/ppermute | solution.py:364
  65.9 7.3 %collective-permute-start.19 = (bf16[4,128,128]{2,1,0:T(8,128)(2,1)S(1)}, bf16[4,128,128]{2,1,0:T(8,128)(2,1)S(1)}, u32[]{:S(2)}, u32[]{:S(2)}) collective-permute-start(bf16[4,128,128]{2,1,0:T(8,128)(2,1)S(1)} %get-tuple-element.68), channel_id=1, source_target_pairs={{0,4},{2,6},{4,0},{6,2},{8,12},{10,14},{12,8},{14,10},{16,20},{18,... | collective-permute-start | bytes 393224 | tf_op jit(solution)/shard_map/ppermute | solution.py:364
  73.3 5.8 %collective-permute-start.22 = (bf16[128,128]{1,0:T(8,128)(2,1)S(1)}, bf16[128,128]{1,0:T(8,128)(2,1)S(1)}, u32[]{:S(2)}, u32[]{:S(2)}) collective-permute-start(bf16[128,128]{1,0:T(8,128)(2,1)S(1)} %get-tuple-element.73), channel_id=1, source_target_pairs={{0,8},{2,10},{4,12},{6,14},{8,16},{10,18},{12,20},{14,22},{16,24},... | collective-permute-start | bytes 98312 | tf_op jit(solution)/shard_map/ppermute | solution.py:370
  74.9 5.3 %collective-permute-start.23 = (bf16[128,128]{1,0:T(8,128)(2,1)S(1)}, bf16[128,128]{1,0:T(8,128)(2,1)S(1)}, u32[]{:S(2)}, u32[]{:S(2)}) collective-permute-start(bf16[128,128]{1,0:T(8,128)(2,1)S(1)} %get-tuple-element.74), channel_id=1, source_target_pairs={{0,16},{2,18},{4,20},{6,22},{8,24},{10,26},{12,28},{14,30},{16,0},... | collective-permute-start | bytes 98312 | tf_op jit(solution)/shard_map/ppermute | solution.py:370
  77.4 3.9 %collective-permute-start.24 = (bf16[128,128]{1,0:T(8,128)(2,1)S(1)}, bf16[128,128]{1,0:T(8,128)(2,1)S(1)}, u32[]{:S(2)}, u32[]{:S(2)}) collective-permute-start(bf16[128,128]{1,0:T(8,128)(2,1)S(1)} %get-tuple-element.75), channel_id=1, source_target_pairs={{0,24},{2,26},{4,28},{6,30},{8,0},{10,2},{12,4},{14,6},{16,8},{18,... | collective-permute-start | bytes 98312 | tf_op jit(solution)/shard_map/ppermute | solution.py:370
